TPU v7x, 32 devices: a whole 2x2x4 slice. The times are simulated.
32 devices in a mesh: wide: 8 (over y, x, core), narrow: 4 (over z).
Axes of the slice: x: 2, y: 2, z: 4, core: 2. Of those that a mesh axis runs over, the one named last changes fastest.
Arguments:
- residual: bfloat16 [2048, 4608], P('wide'), may hold values from -6 to 6
- pre_gain: bfloat16 [4608], replicated, may hold values from 0.5 to 1.5
- query_weight: bfloat16 [4608, 4096], P('wide', 'narrow'), may hold values from -0.09375 to 0.09375
- key_weight: bfloat16 [4608, 2048], P('wide', 'narrow'), may hold values from -0.09375 to 0.09375
- value_weight: bfloat16 [4608, 2048], P('wide', 'narrow'), may hold values from -0.09375 to 0.09375
- output_weight: bfloat16 [4096, 4608], P('narrow', 'wide'), may hold values from -1 to 1
- adapter_down: bfloat16 [4608, 768], P('wide', 'narrow'), may hold values from -0.09375 to 0.09375
- adapter_up_query: bfloat16 [256, 4096], P(None, 'narrow'), may hold values from -1.5 to 1.5
- adapter_up_key: bfloat16 [256, 2048], P(None, 'narrow'), may hold values from -1.5 to 1.5
- adapter_up_value: bfloat16 [256, 2048], P(None, 'narrow'), may hold values from -1.5 to 1.5
- adapter_down_out: bfloat16 [4096, 256], P('narrow'), may hold values from -0.09375 to 0.09375
- adapter_up_out: bfloat16 [256, 4608], P(None, 'narrow'), may hold values from -1.5 to 1.5
- post_gain: bfloat16 [4608], P('narrow'), may hold values from 0.5 to 1.5
- sink_logits: float32 [32], P('narrow'), may hold values from -1 to 130
- prompt_lengths: int32 [4], replicated, may hold values from 1 to 1024, 2048 in all
- prompt_adapters: int32 [4], replicated, may hold values from 0 to 15
Outputs:
- layer_out: bfloat16 [2048, 4608], P('wide', 'narrow')
All inputs are finite; a program needn't handle non-finite values.
Results may differ from a plain program's by a relative error of at most 0.022.
Values may be sent and summed in bfloat16 or wider, within the bound.
No kernel may reach another device: no remote copies, remote signals or barrier semaphores. Data moves between devices by JAX's collectives and lax.ppermute only.
A program may use at most 128 MiB of HBM per device.

v0:
```python
import jax
import jax.numpy as jnp
from jax import lax
from jax.sharding import PartitionSpec as P

HEAD_DIM = 128
ADAPTERS = 16


epsilon = 1e-06
adapter_scale = 0.5
rotary_base = 10000.0
score_scale = 1.0 / 12.0


def token_layout(prompt_lengths, count, first):
    ends = jnp.cumsum(prompt_lengths, dtype=jnp.int32)
    starts = ends - prompt_lengths
    places = first + jnp.arange(count, dtype=jnp.int32)
    member = jnp.logical_and(
        places[:, None] >= starts[None, :], places[:, None] < ends[None, :]
    ).astype(jnp.int32)
    labels = jnp.arange(prompt_lengths.shape[0], dtype=jnp.int32)
    prompt = jnp.sum(member * labels[None, :], axis=1)
    position = places - jnp.sum(member * starts[None, :], axis=1)
    return (member, prompt, position)


def rotate(values, position):
    half = values.shape[-1] // 2
    exponent = jnp.arange(half, dtype=jnp.float32) * (2.0 / values.shape[-1])
    frequency = jnp.power(jnp.float32(rotary_base), -exponent)
    angle = position.astype(jnp.float32)[:, None] * frequency[None, :]
    cosine = jnp.cos(angle)[:, None, :]
    sine = jnp.sin(angle)[:, None, :]
    first_half = values[..., :half]
    second_half = values[..., half:]
    return jnp.concatenate(
        [first_half * cosine - second_half * sine, second_half * cosine + first_half * sine],
        axis=-1,
    )


def select_codes(codes, adapter, projections, adapters):
    count = codes.shape[0]
    width = codes.shape[1] // (adapters * projections)
    shaped = codes.reshape(count, adapters, projections, width)
    onehot = (adapter[:, None] == jnp.arange(adapters, dtype=jnp.int32)[None, :]).astype(
        codes.dtype
    )
    kept = shaped * onehot[:, :, None, None]
    return [kept[:, :, slot, :].reshape(count, adapters * width) for slot in range(projections)]


def add_adapter(partial_out, adapter_cols, offset, own_width):
    current = lax.dynamic_slice_in_dim(partial_out, offset, own_width, 1)
    return lax.dynamic_update_slice_in_dim(partial_out, current + adapter_cols, offset, 1)


def per_device(
    residual,
    pre_gain,
    query_weight,
    key_weight,
    value_weight,
    output_weight,
    adapter_down,
    adapter_up_query,
    adapter_up_key,
    adapter_up_value,
    adapter_down_out,
    adapter_up_out,
    post_gain,
    sink_logits,
    prompt_lengths,
    prompt_adapters,
):
    tok_rows = residual.shape[0]
    first = lax.axis_index("wide") * tok_rows
    member, prompt, position = token_layout(prompt_lengths, tok_rows, first)
    adapter = jnp.sum(member * prompt_adapters[None, :], axis=1)
    stream = residual.astype(jnp.float32)
    scale_rows = lax.rsqrt(jnp.mean(stream * stream, axis=1, keepdims=True) + epsilon)
    normed = (stream * scale_rows * pre_gain.astype(jnp.float32)[None, :]).astype(jnp.bfloat16)
    query_cols = query_weight.shape[1]
    key_cols = key_weight.shape[1]
    pieces = (
        lax.all_gather(query_weight, "wide", axis=0, tiled=True),
        lax.all_gather(key_weight, "wide", axis=0, tiled=True),
        lax.all_gather(value_weight, "wide", axis=0, tiled=True),
        lax.all_gather(adapter_down, "wide", axis=0, tiled=True),
    )
    query_part, key_part, value_part, code_part = tuple(
        (jnp.dot(normed, piece, preferred_element_type=jnp.float32) for piece in pieces)
    )
    codes = lax.all_gather(code_part.astype(jnp.bfloat16), "narrow", axis=1, tiled=True)
    chosen = select_codes(codes, adapter, 3, ADAPTERS)
    query = query_part + adapter_scale * jnp.dot(
        chosen[0], adapter_up_query, preferred_element_type=jnp.float32
    )
    key = key_part + adapter_scale * jnp.dot(
        chosen[1], adapter_up_key, preferred_element_type=jnp.float32
    )
    value = value_part + adapter_scale * jnp.dot(
        chosen[2], adapter_up_value, preferred_element_type=jnp.float32
    )
    local_heads = query_cols // HEAD_DIM
    local_kv = key_cols // HEAD_DIM
    group = local_heads // local_kv
    queries = (
        rotate(query.reshape(tok_rows, local_heads, HEAD_DIM), position)
        .astype(jnp.bfloat16)
        .reshape(tok_rows, local_kv, group, HEAD_DIM)
    )
    keys = rotate(key.reshape(tok_rows, local_kv, HEAD_DIM), position).astype(jnp.bfloat16)
    values = value.astype(jnp.bfloat16).reshape(tok_rows, local_kv, HEAD_DIM)
    sinks = sink_logits.reshape(local_kv, group)
    own_places = first + jnp.arange(tok_rows, dtype=jnp.int32)
    start_top = jnp.broadcast_to(sinks[None, :, :], (tok_rows, local_kv, group))
    start_total = jnp.ones((tok_rows, local_kv, group), jnp.float32)
    start_sum = jnp.zeros((tok_rows, local_kv, group, HEAD_DIM), jnp.float32)
    top = start_top
    total = start_total
    summed_values = start_sum
    piece_keys = lax.all_gather(keys, "wide", axis=0, tiled=True)
    piece_values = lax.all_gather(values, "wide", axis=0, tiled=True)
    count = piece_keys.shape[0]
    unused, key_prompt, unused_position = token_layout(prompt_lengths, count, jnp.int32(0))
    key_places = jnp.arange(count, dtype=jnp.int32)
    allowed = jnp.logical_and(
        prompt[:, None] == key_prompt[None, :], own_places[:, None] >= key_places[None, :]
    )[:, None, None, :]
    scores = (
        jnp.einsum("qgjd,kgd->qgjk", queries, piece_keys, preferred_element_type=jnp.float32)
        * score_scale
    )
    scores = jnp.where(allowed, scores, -1e30)
    fresh = jnp.maximum(top, jnp.max(scores, axis=-1))
    factor = jnp.exp(top - fresh)
    weights = jnp.where(allowed, jnp.exp(scores - fresh[..., None]), 0.0)
    total = total * factor + jnp.sum(weights, axis=-1)
    update = jnp.einsum(
        "qgjk,kgd->qgjd",
        weights.astype(jnp.bfloat16),
        piece_values,
        preferred_element_type=jnp.float32,
    )
    top, total, summed_values = (fresh, total, summed_values * factor[..., None] + update)
    attended = (
        (summed_values / total[..., None])
        .reshape(tok_rows, local_heads * HEAD_DIM)
        .astype(jnp.bfloat16)
    )
    code_terms = jnp.dot(attended, adapter_down_out, preferred_element_type=jnp.float32)
    codes_out = lax.psum(code_terms.astype(jnp.bfloat16), "narrow")
    chosen_out = select_codes(codes_out, adapter, 1, ADAPTERS)[0]
    adapter_cols = adapter_scale * jnp.dot(
        chosen_out, adapter_up_out, preferred_element_type=jnp.float32
    )
    own_width = adapter_up_out.shape[1]
    offset = lax.axis_index("narrow") * own_width
    partial_out = jnp.dot(
        attended,
        lax.all_gather(output_weight, "wide", axis=1, tiled=True),
        preferred_element_type=jnp.float32,
    )
    partial_out = add_adapter(partial_out, adapter_cols, offset, own_width)
    whole = lax.psum(partial_out.astype(jnp.bfloat16), "narrow").astype(jnp.float32)
    mean_square = jnp.mean(whole * whole, axis=1)
    projected = lax.dynamic_slice_in_dim(whole, offset, own_width, 1)
    factor_rows = lax.rsqrt(mean_square + epsilon)
    own_stream = lax.dynamic_slice_in_dim(stream, offset, own_width, 1)
    mixed = own_stream + projected * factor_rows[:, None] * post_gain.astype(jnp.float32)[None, :]
    return mixed.astype(jnp.bfloat16)


def solution(mesh):
    return jax.shard_map(
        per_device,
        mesh=mesh,
        in_specs=(
            P("wide", None),
            P(),
            P("wide", "narrow"),
            P("wide", "narrow"),
            P("wide", "narrow"),
            P("narrow", "wide"),
            P("wide", "narrow"),
            P(None, "narrow"),
            P(None, "narrow"),
            P(None, "narrow"),
            P("narrow", None),
            P(None, "narrow"),
            P("narrow"),
            P("narrow"),
            P(),
            P(),
        ),
        out_specs=P("wide", "narrow"),
        check_vma=False,
    )
```

profile of v0, /device:TPU:0, one launch (start us, length us, event | category | flops | bytes accessed | tf_op | source)
XLA Modules:
  0.0 454.4 jit_solution(10406578895520055039)
XLA Ops:
  12.3 2.4 multiply_reduce_fusion.1
  14.7 1.3 multiply_cosine_fusion
  16.0 23.3 %all-gather.21.cloned.1.call-done = bf16[8,576,192]{1,2,0:T(8,128)(2,1)} async-done(((bf16[1,576,192]{1,2,0:T(8,128)(2,1)}), bf16[8,576,192]{1,2,0:T(8,128)(2,1)}) %all-gather.21.cloned.1.call-update) | async-done | bytes 1769488 | tf_op jit(solution)/shard_map/all_gather | solution.py:91
  39.3 3.9 copy.39
  43.3 4.1 reshape.203
  47.4 2.6 convolution_convert_fusion.1
  50.1 14.7 %all_gather.26 = bf16[256,768]{0,1:T(8,128)(2,1)S(1)} all-gather(bf16[256,192]{0,1:T(8,128)(2,1)S(1)} %convolution_convert_fusion.1), channel_id=1, replica_groups=mesh['wide'=8,'narrow'=4] {'narrow'}, dimensions={1}, use_global_device_ids=true | all-gather | bytes 491520 | tf_op jit(solution)/shard_map/all_gather | solution.py:96
  65.5 14.6 %all-gather.9.cloned.1.call-done = bf16[4608,512]{1,0:T(8,128)(2,1)} async-done(((bf16[576,512]{1,0:T(8,128)(2,1)}), bf16[4608,512]{1,0:T(8,128)(2,1)}) %all-gather.9.cloned.1.call-update) | async-done | bytes 4718608 | tf_op jit(solution)/shard_map/all_gather | solution.py:89
  80.2 3.7 fusion.45
  85.0 1.2 reshape.199
  86.5 1.1 subtract_convert_fusion.1
  88.6 32.4 %all-gather.15.cloned.1.call-done = bf16[4608,512]{1,0:T(8,128)(2,1)} async-done(((bf16[576,512]{1,0:T(8,128)(2,1)}), bf16[4608,512]{1,0:T(8,128)(2,1)}) %all-gather.15.cloned.1.call-update) | async-done | bytes 4718608 | tf_op jit(solution)/shard_map/all_gather | solution.py:90
  121.0 3.7 fusion.43
  124.8 1.2 fusion.26
  129.3 52.3 %all-gather.13.cloned.1.call-done = bf16[4608,1024]{1,0:T(8,128)(2,1)} async-done(((bf16[576,1024]{1,0:T(8,128)(2,1)}), bf16[4608,1024]{1,0:T(8,128)(2,1)}) %all-gather.13.cloned.1.call-update) | async-done | bytes 9437200 | tf_op jit(solution)/shard_map/all_gather | solution.py:88
  181.6 5.3 %fusion.44 = f32[256,1024]{1,0:T(8,128)S(1)} fusion(bf16[4608,1024]{1,0:T(8,128)(2,1)} %all-gather.13.cloned.1.call-done, f32[4608]{0:T(1024)S(1)} %convert_element_type.59, f32[256]{0:T(256)S(1)} %add_rsqrt_fusion.1, bf16[256,4608]{1,0:T(8,128)(2,1)S(1)} %copy-done.2), kind=kOutput, calls=%fused_computation.69 | convolution fusion | flops 2420637696 | bytes 12864512 | tf_op jit(solution)/shard_map/dot_general | solution.py:94
  190.2 21.1 %all-gather.11.cloned.1.call-done = bf16[2048,4,128]{2,0,1:T(8,128)(2,1)} async-done(((bf16[256,4,128]{2,0,1:T(8,128)(2,1)}), bf16[2048,4,128]{2,0,1:T(8,128)(2,1)}) %all-gather.11.cloned.1.call-update) | async-done | bytes 2097168 | tf_op jit(solution)/shard_map/all_gather | solution.py:125
  211.3 5.0 %fusion = (f32[256,4,2]{0,2,1:T(2,128)S(1)}, f32[4,2048,256,2]{2,1,3,0:T(8,128)S(1)}) fusion(pred[256,2048]{0,1:T(8,128)(4,1)S(1)} %fusion.11, bf16[256,4,2,64]{3,0,2,1:T(8,128)(2,1)} %bitcast.77, bf16[256,4,2,64]{3,0,2,1:T(8,128)(2,1)} %bitcast.78, bf16[2048,4,128]{2,0,1:T(8,128)(2,1)} %all-gather.11.cloned.1.call-done), kind=kOutput, calls=%fused_computation.2 | convolution fusion | flops 1087371264 | bytes 19931136 | tf_op jit(solution)/shard_map/qgjd,kgd->qgjk/dot_general | solution.py:134
  216.4 4.0 fusion.1
  220.4 1.7 copy-done.1
  222.2 19.1 %all-gather.17.cloned.1.call-done = bf16[2048,4,128]{0,2,1:T(8,128)(2,1)} async-done(((bf16[256,4,128]{0,2,1:T(8,128)(2,1)}), bf16[2048,4,128]{0,2,1:T(8,128)(2,1)}) %all-gather.17.cloned.1.call-update) | async-done | bytes 2097168 | tf_op jit(solution)/shard_map/all_gather | solution.py:126
  241.3 10.8 %divide_convert_fusion = bf16[256,4,2,128]{0,3,2,1:T(8,128)(2,1)S(1)} fusion(f32[4,2048,256,2]{2,1,3,0:T(8,128)} %copy-done.1, f32[256,4,2]{0,2,1:T(2,128)S(1)} %broadcast_maximum_fusion, pred[256,2048]{0,1:T(8,128)(4,1)S(1)} %fusion.11, bf16[2048,4,128]{0,2,1:T(8,128)(2,1)} %all-gather.17.cloned.1.call-done, f32[256,4,2]{0,2,1:T(2,128)S(1)} %get-tuple-element.18, ...), kind=kOutput, calls=%fused_computation.31 | convolution fusion | flops 1095499776 | bytes 19947520 | tf_op jit(solution)/shard_map/qgjk,kgd->qgjd/dot_general | solution.py:142
  254.2 47.8 %all-gather.19.cloned.1.call-done = bf16[1024,4608]{0,1:T(8,128)(2,1)} async-done(((bf16[1024,576]{0,1:T(8,128)(2,1)}), bf16[1024,4608]{0,1:T(8,128)(2,1)}) %all-gather.19.cloned.1.call-update) | async-done | bytes 9437200 | tf_op jit(solution)/shard_map/all_gather | solution.py:164
  302.0 8.7 %fusion.48 = f32[256,4608]{1,0:T(8,128)} fusion(bf16[256,1024]{0,1:T(8,128)(2,1)} %bitcast.88, bf16[1024,4608]{0,1:T(8,128)(2,1)} %all-gather.19.cloned.1.call-done), kind=kOutput, calls=%fused_computation.73 | convolution fusion | flops 2415919104 | bytes 14680064 | tf_op jit(solution)/shard_map/dot_general | solution.py:162
  310.7 28.2 %all-reduce.3.cloned.1.call-done = bf16[256,256]{1,0:T(8,128)(2,1)} async-done(((bf16[256,256]{1,0:T(8,128)(2,1)}), bf16[256,256]{1,0:T(8,128)(2,1)}) %all-reduce.3.cloned.1.call-update) | async-done | bytes 131088 | tf_op jit(solution)/shard_map/psum | solution.py:155
  338.8 2.8 fusion.7
  341.6 4.0 convert_element_type.69
  345.7 2.7 convert_element_type.58
  348.4 92.7 %all-reduce.5.cloned.1.call-done = bf16[256,4608]{1,0:T(8,128)(2,1)} async-done(((bf16[256,4608]{1,0:T(8,128)(2,1)}), bf16[256,4608]{1,0:T(8,128)(2,1)}) %all-reduce.5.cloned.1.call-update) | async-done | bytes 2359312 | tf_op jit(solution)/shard_map/psum | solution.py:168
  441.1 2.2 multiply_reduce_fusion
  443.3 2.2 convert_element_type.70
  445.5 2.3 add_convert_fusion
  (75 shorter events, 17.6 us)
Async XLA Ops:
  6.5 332.3 %copy-start = (bf16[256,1152]{1,0:T(8,128)(2,1)S(1)}, bf16[256,1152]{1,0:T(8,128)(2,1)}, u32[]{:S(2)}) copy-start(bf16[256,1152]{1,0:T(8,128)(2,1)} %param.27) | copy-start | bytes 1769476
  6.5 32.8 %all-gather.21.cloned.1.call-start = ((), (), s32[]{:S(2)}) async-start(), calls=%async_computation.8 | async-start | bytes 2211840 | tf_op jit(solution)/shard_map/all_gather | solution.py:91
  7.3 72.9 %all-gather.9.cloned.1.call-start = ((), (), s32[]{:S(2)}) async-start(), calls=%async_computation | async-start | bytes 5308416 | tf_op jit(solution)/shard_map/all_gather | solution.py:89
  8.0 113.0 %all-gather.15.cloned.1.call-start = ((), (), s32[]{:S(2)}) async-start(), calls=%async_computation.3 | async-start | bytes 5308416 | tf_op jit(solution)/shard_map/all_gather | solution.py:90
  8.7 172.9 %all-gather.13.cloned.1.call-start = ((), (), s32[]{:S(2)}) async-start(), calls=%async_computation.2 | async-start | bytes 10616832 | tf_op jit(solution)/shard_map/all_gather | solution.py:88
  9.3 202.0 %all-gather.11.cloned.1.call-start = ((), (), s32[]{:S(2)}) async-start(), calls=%async_computation.1 | async-start | bytes 2359296 | tf_op jit(solution)/shard_map/all_gather | solution.py:125
  12.3 35.1 %copy-start.2 = (bf16[256,4608]{1,0:T(8,128)(2,1)S(1)}, bf16[256,4608]{1,0:T(8,128)(2,1)}, u32[]{:S(2)}) copy-start(bf16[256,4608]{1,0:T(8,128)(2,1)} %param.16) | copy-start | bytes 7077892
  65.5 18.4 %copy-start.9 = (bf16[256,512]{1,0:T(8,128)(2,1)S(1)}, bf16[256,512]{1,0:T(8,128)(2,1)}, u32[]{:S(2)}) copy-start(bf16[256,512]{1,0:T(8,128)(2,1)} %param.24) | copy-start | bytes 786436
  88.5 36.2 %copy-start.5 = (bf16[256,16,1,16]{0,3,2,1:T(8,128)(2,1)S(1)}, bf16[256,16,1,16]{0,3,2,1:T(8,128)(2,1)}, u32[]{:S(2)}) copy-start(bf16[256,16,1,16]{0,3,2,1:T(8,128)(2,1)} %get-tuple-element.14) | copy-start | bytes 393220
  88.5 39.3 %copy-start.11 = (f32[8]{0:T(128)S(1)}, f32[8]{0:T(128)}, u32[]{:S(2)}) copy-start(f32[8]{0:T(128)} %param.29) | copy-start | bytes 100
  88.5 152.7 %all-gather.17.cloned.1.call-start = ((), (), s32[]{:S(2)}) async-start(), calls=%async_computation.4 | async-start | bytes 2359296 | tf_op jit(solution)/shard_map/all_gather | solution.py:126
  126.8 175.2 %all-gather.19.cloned.1.call-start = ((), (), s32[]{:S(2)}) async-start(), calls=%async_computation.5 | async-start | bytes 10616832 | tf_op jit(solution)/shard_map/all_gather | solution.py:164
  127.6 211.3 %all-reduce.3.cloned.1.call-start = ((), (), s32[]{:S(2)}) async-start(), calls=%async_computation.6 | async-start | bytes 262144 | tf_op jit(solution)/shard_map/psum | solution.py:155
  181.6 5.3 %copy-start.6 = (bf16[256,1024]{1,0:T(8,128)(2,1)S(1)}, bf16[256,1024]{1,0:T(8,128)(2,1)}, u32[]{:S(2)}) copy-start(bf16[256,1024]{1,0:T(8,128)(2,1)} %param.23) | copy-start | bytes 1572868
  181.6 5.3 %copy-start.8 = (bf16[256,16,1,16]{0,3,2,1:T(8,128)(2,1)S(1)}, bf16[256,16,1,16]{0,3,2,1:T(8,128)(2,1)}, u32[]{:S(2)}) copy-start(bf16[256,16,1,16]{0,3,2,1:T(8,128)(2,1)} %get-tuple-element.15) | copy-start | bytes 393220
  186.9 0.9 copy-start.3
  186.9 1.0 copy-start.4
  216.3 5.8 %copy-start.1 = (f32[4,2048,256,2]{2,1,3,0:T(8,128)}, f32[4,2048,256,2]{2,1,3,0:T(8,128)S(1)}, u32[]{:S(2)}) copy-start(f32[4,2048,256,2]{2,1,3,0:T(8,128)S(1)} %get-tuple-element.22) | copy-start | bytes 50331652
  241.3 11.7 %copy-start.12 = (bf16[1024,256]{1,0:T(8,128)(2,1)S(1)}, bf16[1024,256]{1,0:T(8,128)(2,1)}, u32[]{:S(2)}) copy-start(bf16[1024,256]{1,0:T(8,128)(2,1)} %param.26) | copy-start | bytes 1572868
  252.1 0.8 copy-start.13
  254.0 84.9 %copy-start.7 = (bf16[256,256]{1,0:T(8,128)(2,1)S(1)}, bf16[256,256]{1,0:T(8,128)(2,1)}, u32[]{:S(2)}) copy-start(bf16[256,256]{1,0:T(8,128)(2,1)} %copy.46) | copy-start | bytes 393220
  254.0 187.1 %all-reduce.5.cloned.1.call-start = ((), (), s32[]{:S(2)}) async-start(), calls=%async_computation.7 | async-start | bytes 4718592 | tf_op jit(solution)/shard_map/psum | solution.py:168
  345.6 2.7 copy-start.10
Sparse Core Ops, SparseCore 0:
  9.2 30.0 all-gather.20
  41.2 38.9 all-gather.8
  82.0 38.9 all-gather.14
  122.7 58.8 all-gather.12
  183.4 27.8 all-gather.10
  213.0 28.1 all-gather.16
  243.1 58.8 all-gather.18
  304.3 34.4 all-reduce.2
  345.8 95.2 all-reduce.4
where the time goes:
time: 455 us; the launch traced here: 454 us
  waiting for transfers between devices  335 us (74%)
  matrix products  46.3 us (10%)
  other arithmetic  27.4 us (6%)
  local copies, waits for them, and re-layouts  17 us (4%)
  blocking collectives  14.7 us (3%)
  between operations  13.5 us (3%)
    psum x1, waiting for transfers between devices, per_device(): lax.psum(partial_out.astype(jnp.bfloat16), 'narrow').astype(jnp.float32)  92.7 us
    all_gather x1, waiting for transfers between devices, per_device(): lax.all_gather(query_weight, 'wide', axis=0, tiled=True)  52.3 us
    all_gather x1, waiting for transfers between devices, per_device(): lax.all_gather(output_weight, 'wide', axis=1, tiled=True)  47.8 us
    all_gather x1, waiting for transfers between devices, per_device(): lax.all_gather(value_weight, 'wide', axis=0, tiled=True)  32.4 us
    psum x1, waiting for transfers between devices, per_device(): codes_out = lax.psum(code_terms.astype(jnp.bfloat16), 'narrow')  28.2 us
    all_gather x1, waiting for transfers between devices, per_device(): lax.all_gather(adapter_down, 'wide', axis=0, tiled=True)  23.3 us
    all_gather x1, waiting for transfers between devices, per_device(): piece_keys = lax.all_gather(keys, 'wide', axis=0, tiled=True)  21.1 us
    all_gather x1, waiting for transfers between devices, per_device(): piece_values = lax.all_gather(values, 'wide', axis=0, tiled=True)  19.1 us
  transfers between devices with their start and end apart: 9, of which 9 were waited for; matrix products, arithmetic and copies ran while one was open for 16% of the time, Pallas kernels for 0%

commit v1 on v0

--- a/solution.py
+++ b/solution.py
@@ -1,16 +1,28 @@
+import functools
+
 import jax
 import jax.numpy as jnp
 from jax import lax
+from jax.experimental import pallas as pl
+from jax.experimental.pallas import tpu as pltpu
 from jax.sharding import PartitionSpec as P
 
 HEAD_DIM = 128
 ADAPTERS = 16
-
+RANK = 16
 
 epsilon = 1e-06
 adapter_scale = 0.5
 rotary_base = 10000.0
 score_scale = 1.0 / 12.0
+
+CHIPS = 4
+CHUNKS = 4
+F32 = jnp.float32
+BF16 = jnp.bfloat16
+SMEM = pl.BlockSpec(memory_space=pltpu.SMEM)
+VMEM = pl.BlockSpec(memory_space=pltpu.VMEM)
+ANY = pl.BlockSpec(memory_space=pl.ANY)
 
 
 def token_layout(prompt_lengths, count, first):
@@ -26,6 +38,575 @@
     return (member, prompt, position)
 
 
+def params(flops, bytes_accessed, transcendentals=0):
+    return dict(
+        compiler_params=pltpu.CompilerParams(vmem_limit_bytes=48 * 1024 * 1024),
+        cost_estimate=pl.CostEstimate(
+            flops=flops, bytes_accessed=bytes_accessed, transcendentals=transcendentals
+        ),
+    )
+
+
+def prompt_of(places, lengths_ref, prompts):
+    end = jnp.int32(0)
+    prompt = jnp.zeros_like(places)
+    start = jnp.zeros_like(places)
+    for p in range(prompts - 1):
+        end = end + lengths_ref[p]
+        past = places >= end
+        prompt = jnp.where(past, p + 1, prompt)
+        start = jnp.where(past, end, start)
+    return prompt, start
+
+
+def order(chip, core):
+    return (chip ^ (1 + core), chip ^ 3, chip ^ (2 - core), chip)
+
+
+def near(chip, core):
+    return (chip, chip ^ (1 + core), chip ^ (2 - core), chip ^ 3)
+
+
+def split_kernel(info_ref, x_ref, *refs):
+    outs, sems = refs[:4], refs[4]
+    chip = lax.shift_right_logical(info_ref[0], 1)
+    depth = outs[0].shape[1]
+    copies = []
+    for delta in (1, 2, 3, 0):
+        at = pl.multiple_of((chip ^ delta) * depth, 128)
+        copies.append(
+            pltpu.make_async_copy(x_ref.at[:, pl.ds(at, depth)], outs[delta], sems.at[delta])
+        )
+        copies[-1].start()
+    for copy in copies:
+        copy.wait()
+
+
+def split(info, x):
+    shape = jax.ShapeDtypeStruct((x.shape[0], x.shape[1] // CHIPS), x.dtype)
+    return pl.pallas_call(
+        split_kernel,
+        out_shape=(shape,) * 4,
+        in_specs=[SMEM, ANY],
+        out_specs=(ANY,) * 4,
+        scratch_shapes=[pltpu.SemaphoreType.DMA((4,))],
+        name="split",
+        **params(0, x.size * 4),
+    )(info, x)
+
+
+def columns_kernel(info_ref, q_ref, k_ref, v_ref, gain_ref, mine_ref, theirs_ref):
+    chip = lax.shift_right_logical(info_ref[0], 1)
+    own = info_ref[0] & 1
+    d = HEAD_DIM
+    gain = gain_ref[...]
+    for core, out in ((1 - own, theirs_ref), (own, mine_ref)):
+        for place, to in enumerate(order(chip, core)):
+            q = q_ref[:, pl.ds(pl.multiple_of((2 * to + core) * d, d), d)]
+            at = pl.ds(pl.multiple_of(to * d, d), d)
+            kv = jnp.where(core == 0, k_ref[:, at], v_ref[:, at])
+            out[:, 2 * place * d : (2 * place + 1) * d] = (q.astype(F32) * gain).astype(BF16)
+            out[:, (2 * place + 1) * d : (2 * place + 2) * d] = (kv.astype(F32) * gain).astype(BF16)
+
+
+def columns(info, q, k, v, gain):
+    shape = jax.ShapeDtypeStruct(q.shape, BF16)
+    return pl.pallas_call(
+        columns_kernel,
+        out_shape=(shape, shape),
+        in_specs=[SMEM] + [VMEM] * 4,
+        out_specs=(VMEM, VMEM),
+        name="columns",
+        **params(q.size * 4, q.size * 8),
+    )(info, q, k, v, gain)
+
+
+def adapters_kernel(prompts, info_ref, chosen_ref, down_ref, gain_ref, upq_ref, upk_ref, upv_ref, ado_ref, upo_ref, pack_ref, up_ref, out_ref):
+    me, z = info_ref[0], info_ref[1]
+    chip = lax.shift_right_logical(me, 1)
+    core = me & 1
+    d = HEAD_DIM
+    n_codes = prompts * RANK
+    local = down_ref.shape[1] // (3 * RANK)
+    rows = down_ref.shape[0]
+
+    shape = (3 * n_codes, down_ref.shape[1])
+    row = lax.broadcasted_iota(jnp.int32, shape, 0)
+    col = lax.broadcasted_iota(jnp.int32, shape, 1)
+    prompt = (row % n_codes) // RANK
+    adapter = jnp.zeros(shape, jnp.int32)
+    for p in range(prompts):
+        adapter = jnp.where(prompt == p, chosen_ref[p], adapter)
+    wanted = (adapter - z * local) * (3 * RANK) + (row // n_codes) * RANK + row % RANK
+    inside = jnp.logical_and(adapter >= z * local, adapter < (z + 1) * local)
+    pick = jnp.where(jnp.logical_and(inside, col == wanted), 1.0, 0.0).astype(BF16)
+    down = lax.dot_general(pick, down_ref[...], (((1,), (1,)), ((), ())), preferred_element_type=F32)
+    pack_ref[: 3 * n_codes, :] = (down * gain_ref[...]).astype(BF16)
+
+    def rows_of(p):
+        return pl.ds(pl.multiple_of(chosen_ref[p] * RANK, RANK), RANK)
+
+    for p in range(prompts):
+        both = upo_ref[rows_of(p), :].astype(F32) * adapter_scale
+        part = jnp.where(core == 0, both[:, :rows], both[:, rows:])
+        at = 3 * n_codes + p * RANK
+        pack_ref[at : at + RANK, :] = jnp.where(z == chip, part, 0.0).astype(BF16)
+
+    up_ref[...] = jnp.zeros_like(up_ref)
+    for p in range(prompts):
+        for place, to in enumerate(order(chip, core)):
+            q = upq_ref[rows_of(p), pl.ds(pl.multiple_of((2 * to + core) * d, d), d)].astype(F32)
+            at = pl.ds(pl.multiple_of(to * d, d), d)
+            k = upk_ref[rows_of(p), at].astype(F32)
+            v = upv_ref[rows_of(p), at].astype(F32)
+            kv = jnp.where(core == 0, k, v)
+            up_ref[p * RANK : (p + 1) * RANK, 2 * place * d : (2 * place + 1) * d] = (q * adapter_scale).astype(BF16)
+            up_ref[n_codes + p * RANK : n_codes + (p + 1) * RANK, (2 * place + 1) * d : (2 * place + 2) * d] = (
+                kv * adapter_scale
+            ).astype(BF16)
+
+    shape = (n_codes, ado_ref.shape[1])
+    row = lax.broadcasted_iota(jnp.int32, shape, 0)
+    col = lax.broadcasted_iota(jnp.int32, shape, 1)
+    adapter = jnp.zeros(shape, jnp.int32)
+    for p in range(prompts):
+        adapter = jnp.where(row // RANK == p, chosen_ref[p], adapter)
+    pick = jnp.where(col == adapter * RANK + row % RANK, 1.0, 0.0).astype(BF16)
+    for place, source in enumerate(near(chip, core)):
+        block = ado_ref[pl.ds(pl.multiple_of((2 * source + core) * d, d), d), :]
+        part = lax.dot_general(pick, block, (((1,), (1,)), ((), ())), preferred_element_type=F32)
+        out_ref[:, place * d : (place + 1) * d] = part.astype(BF16)
+
+
+def adapters(info, chosen, down, gain, upq, upk, upv, ado, upo):
+    prompts = chosen.shape[0]
+    n_codes = prompts * RANK
+    return pl.pallas_call(
+        functools.partial(adapters_kernel, prompts),
+        out_shape=(
+            jax.ShapeDtypeStruct((4 * n_codes, down.shape[0]), BF16),
+            jax.ShapeDtypeStruct((2 * n_codes, upq.shape[1]), BF16),
+            jax.ShapeDtypeStruct((n_codes, CHIPS * HEAD_DIM), BF16),
+        ),
+        in_specs=[SMEM, SMEM] + [VMEM] * 7,
+        out_specs=(VMEM,) * 3,
+        name="adapters",
+        **params(down.size * 400, down.size * 10),
+    )(info, chosen, down, gain, upq, upk, upv, ado, upo)
+
+
+def parity_kernel(info_ref, w_ref, mine_ref, theirs_ref, sems):
+    chip = lax.shift_right_logical(info_ref[0], 1)
+    own = info_ref[0] & 1
+    d = HEAD_DIM
+    copies = []
+    for core, out in ((1 - own, theirs_ref), (own, mine_ref)):
+        for place, source in enumerate(near(chip, core)):
+            at = pl.multiple_of((2 * source + core) * d, d)
+            copies.append(
+                pltpu.make_async_copy(
+                    w_ref.at[pl.ds(at, d), :], out.at[pl.ds(place * d, d), :], sems.at[len(copies)]
+                )
+            )
+            copies[-1].start()
+    for copy in copies:
+        copy.wait()
+
+
+def parity(info, w):
+    shape = jax.ShapeDtypeStruct((w.shape[0] // 2, w.shape[1]), w.dtype)
+    return pl.pallas_call(
+        parity_kernel,
+        out_shape=(shape, shape),
+        in_specs=[SMEM, ANY],
+        out_specs=(ANY, ANY),
+        scratch_shapes=[pltpu.SemaphoreType.DMA((8,))],
+        name="parity",
+        **params(0, w.size * 4),
+    )(info, w)
+
+
+def join_kernel(info_ref, mine_ref, other_ref, out_ref):
+    core = info_ref[0] & 1
+    mine, other = mine_ref[...].astype(F32), other_ref[...].astype(F32)
+    left = jnp.where(core == 0, mine, other)
+    right = jnp.where(core == 0, other, mine)
+    out_ref[...] = jnp.concatenate([left, right], axis=1).astype(out_ref.dtype)
+
+
+def join(info, mine, other):
+    rows, cols = mine.shape
+    return pl.pallas_call(
+        join_kernel,
+        out_shape=jax.ShapeDtypeStruct((rows, 2 * cols), mine.dtype),
+        in_specs=[SMEM, VMEM, VMEM],
+        out_specs=VMEM,
+        name="join",
+        **params(rows * cols * 4, rows * cols * 8),
+    )(info, mine, other)
+
+
+def project_kernel(blocks, first, prompts, info_ref, lengths_ref, *refs):
+    x_refs = refs[:8]
+    mine_ref, got_ref, pack_ref, b_ref, send_ref, keep_ref, x_ref, w_ref, sems = refs[8:]
+    me = info_ref[0]
+    core = me & 1
+    tok = x_ref.shape[0] // blocks
+    half = send_ref.shape[1]
+    n_codes = prompts * RANK
+    depth = mine_ref.shape[0]
+    copies = [
+        pltpu.make_async_copy(mine_ref, w_ref.at[pl.ds(pl.multiple_of(core * depth, 16), depth), :], sems.at[0]),
+        pltpu.make_async_copy(got_ref, w_ref.at[pl.ds(pl.multiple_of((1 - core) * depth, 16), depth), :], sems.at[1]),
+    ]
+    for copy in copies:
+        copy.start()
+    for i in range(blocks):
+        rel = me ^ (first + i)
+        for k in range(8):
+
+            @pl.when(rel == k)
+            def _():
+                pltpu.make_async_copy(x_refs[k], x_ref.at[pl.ds(i * tok, tok), :], sems.at[2 + i]).start()
+
+    for i in range(blocks):
+        pltpu.make_async_copy(x_refs[0], x_ref.at[pl.ds(i * tok, tok), :], sems.at[2 + i]).wait()
+    x = x_ref[...]
+    down = jnp.concatenate(
+        [
+            pack_ref[:n_codes, :],
+            jnp.where(core == 0, pack_ref[n_codes : 2 * n_codes, :], pack_ref[2 * n_codes : 3 * n_codes, :]),
+        ],
+        axis=0,
+    )
+    codes = lax.dot_general(x, down, (((1,), (1,)), ((), ())), preferred_element_type=F32)
+    rows = blocks * tok
+    places = first * tok + lax.broadcasted_iota(jnp.int32, (rows, 1), 0)
+    prompt, _ = prompt_of(places, lengths_ref, prompts)
+    lane = lax.broadcasted_iota(jnp.int32, codes.shape, 1)
+    owner = (lane % n_codes) // RANK
+    codes = jnp.where(owner == prompt, codes, 0.0).astype(BF16)
+    for copy in copies:
+        copy.wait()
+    for part, out in ((0, send_ref), (1, keep_ref)):
+        cols = pl.ds(part * half, half)
+        product = jnp.dot(x, w_ref[:, cols], preferred_element_type=F32)
+        product = product + jnp.dot(codes, b_ref[:, cols], preferred_element_type=F32)
+        out[...] = product.astype(out.dtype)
+
+
+def project(info, lengths, pieces, mine, got, pack, up, chunk, blocks):
+    tok, depth = pieces[0].shape
+    cols = mine.shape[1]
+    half = cols // 2
+    rows = blocks * tok
+    return pl.pallas_call(
+        functools.partial(project_kernel, blocks, chunk * blocks, lengths.shape[0]),
+        out_shape=(
+            jax.ShapeDtypeStruct((rows, half), BF16),
+            jax.ShapeDtypeStruct((rows, half), F32),
+        ),
+        in_specs=[SMEM, SMEM] + [ANY] * 10 + [VMEM] * 2,
+        out_specs=(VMEM, VMEM),
+        scratch_shapes=[
+            pltpu.VMEM((rows, depth), BF16),
+            pltpu.VMEM((depth, cols), BF16),
+            pltpu.SemaphoreType.DMA((2 + blocks,)),
+        ],
+        name="project",
+        **params(2 * rows * depth * cols, rows * depth * 2 + depth * cols * 2 + rows * half * 6),
+    )(info, lengths, *pieces, mine, got, pack, up)
+
+
+def finish_kernel(keep_ref, first_ref, second_ref, cos_ref, sin_ref, kcos_ref, ksin_ref, q_ref, kv_ref):
+    d = q_ref.shape[1]
+    own = keep_ref.shape[1] // 2
+    total = keep_ref[:, own:] + first_ref[:, :own].astype(F32) + second_ref[...].astype(F32)
+    q, kv = total[:, :d], total[:, d:]
+    q_ref[...] = (q * cos_ref[...] + pltpu.roll(q, d // 2, 1) * sin_ref[...]).astype(BF16)
+    kv_ref[...] = (kv * kcos_ref[...] + pltpu.roll(kv, d // 2, 1) * ksin_ref[...]).astype(BF16)
+
+
+def finish(keep, first, second, tables, chunk):
+    rows = keep.shape[0]
+    shape = jax.ShapeDtypeStruct((rows, HEAD_DIM), BF16)
+    whole = lambda a: pl.BlockSpec(a.shape, lambda i: (0, 0))
+    table = pl.BlockSpec((rows, HEAD_DIM), lambda i: (chunk, 0))
+    out = pl.BlockSpec((rows, HEAD_DIM), lambda i: (0, 0))
+    return pl.pallas_call(
+        finish_kernel,
+        grid=(1,),
+        out_shape=(shape, shape),
+        in_specs=[whole(keep), whole(first), whole(second)] + [table] * 4,
+        out_specs=(out, out),
+        name="finish",
+        **params(rows * 1024, rows * 4096),
+    )(keep, first, second, *tables)
+
+
+def attend_kernel(first, count, prompts, step, info_ref, lengths_ref, sink_ref, q_ref, *refs):
+    mine_refs, other_refs = refs[:count], refs[count : 2 * count]
+    outs = refs[2 * count : 2 * count + 4]
+    k_ref, v_ref, out_ref = refs[2 * count + 4 :]
+    rows, d = q_ref.shape
+    here, z = info_ref[0], info_ref[1]
+    core = here & 1
+    for i in range(count):
+        mine, other = mine_refs[i][...], other_refs[i][...]
+        k_ref[i * rows : (i + 1) * rows, :] = jnp.where(core == 0, mine, other)
+        v_ref[i * rows : (i + 1) * rows, :] = jnp.where(core == 0, other, mine)
+    sink = sink_ref[here]
+    for block in range(rows // step):
+        base = first + block * step
+        q = q_ref[pl.ds(block * step, step), :]
+        places = base + lax.broadcasted_iota(jnp.int32, (step, 1), 0)
+        _, starts = prompt_of(places, lengths_ref, prompts)
+        end = jnp.int32(0)
+        low = jnp.int32(0)
+        for p in range(prompts - 1):
+            end = end + lengths_ref[p]
+            low = jnp.where(base >= end, end, low)
+
+        def body(i, carry):
+            top, total, summed = carry
+            at = pl.multiple_of(i * step, step)
+            k = k_ref[pl.ds(at, step), :]
+            v = v_ref[pl.ds(at, step), :]
+            scores = lax.dot_general(q, k, (((1,), (1,)), ((), ())), preferred_element_type=F32) * score_scale
+            keys = at + lax.broadcasted_iota(jnp.int32, (step, step), 1)
+            allowed = jnp.logical_and(keys >= starts, keys <= places)
+            scores = jnp.where(allowed, scores, -1e30)
+            fresh = jnp.maximum(top, jnp.max(scores, axis=1, keepdims=True))
+            factor = jnp.exp(top - fresh)
+            weights = jnp.exp(scores - fresh)
+            total = total * factor + jnp.sum(weights, axis=1, keepdims=True)
+            summed = summed * factor + jnp.dot(weights.astype(BF16), v, preferred_element_type=F32)
+            return fresh, total, summed
+
+        top = jnp.full((step, 1), sink, F32)
+        total = jnp.ones((step, 1), F32)
+        summed = jnp.zeros((step, d), F32)
+        top, total, summed = lax.fori_loop(
+            low // step, (first // step) + block + 1, body, (top, total, summed)
+        )
+        out_ref[...] = (summed / total).astype(BF16)
+        part = step // 4
+        for k in range(4):
+            at = pl.multiple_of(((z + k) & 3) * part, part)
+            outs[k][block * part : (block + 1) * part, :] = out_ref[pl.ds(at, part), :]
+
+
+def attend(info, lengths, sinks, q, mine, other, first, step):
+    rows, d = q.shape
+    count = len(mine)
+    return pl.pallas_call(
+        functools.partial(attend_kernel, first, count, lengths.shape[0], step),
+        out_shape=(jax.ShapeDtypeStruct((rows // 4, d), BF16),) * 4,
+        in_specs=[SMEM, SMEM, SMEM] + [VMEM] * (1 + 2 * count),
+        out_specs=(VMEM,) * 4,
+        scratch_shapes=[pltpu.VMEM((count * rows, d), BF16)] * 2 + [pltpu.VMEM((step, d), BF16)],
+        name="attend",
+        **params(rows * 768 * 4 * d, rows * d * 4 + count * rows * d * 4, rows * 768),
+    )(info, lengths, sinks, q, *mine, *other)
+
+
+def output_kernel(prompts, info_ref, lengths_ref, *refs):
+    blocks = refs[:4]
+    weights = refs[4:8]
+    downs = refs[8:12]
+    pack_ref, keep_ref, send_ref, acc_ref = refs[12:]
+    me, z = info_ref[0], info_ref[1]
+    core = jnp.bitwise_and(me, 1)
+    rows = acc_ref.shape[0]
+    d = HEAD_DIM
+    codes = None
+    for k in range(4):
+        a = jnp.concatenate([blocks[r][:, k * d : (k + 1) * d] for r in range(4)], axis=1)
+        product = jnp.dot(a, weights[k][...], preferred_element_type=F32)
+        terms = lax.dot_general(a, downs[k][...], (((1,), (1,)), ((), ())), preferred_element_type=F32)
+        if k == 0:
+            acc_ref[...] = product
+            codes = terms
+        else:
+            acc_ref[...] += product
+            codes = codes + terms
+    part = keep_ref.shape[1]
+    row = lax.broadcasted_iota(jnp.int32, (rows, 1), 0)
+    places = (row // part) * (4 * part) + z * part + row % part
+    prompt, _ = prompt_of(places, lengths_ref, prompts)
+    lane = lax.broadcasted_iota(jnp.int32, codes.shape, 1)
+    codes = jnp.where(lane // RANK == prompt, codes, 0.0).astype(BF16)
+    up = pack_ref[3 * prompts * RANK :, :]
+    acc_ref[...] += jnp.dot(codes, up, preferred_element_type=F32)
+    for i in range(CHIPS):
+        mine = pl.multiple_of(i * 2 * part + core * part, part)
+        theirs = pl.multiple_of(i * 2 * part + (1 - core) * part, part)
+        keep_ref[i] = acc_ref[pl.ds(mine, part), :]
+        send_ref[i] = acc_ref[pl.ds(theirs, part), :].astype(BF16)
+
+
+def output(info, lengths, blocks, weights, downs, up):
+    rows = blocks[0].shape[0]
+    cols = weights[0].shape[1]
+    part = rows // 8
+    return pl.pallas_call(
+        functools.partial(output_kernel, lengths.shape[0]),
+        out_shape=(
+            jax.ShapeDtypeStruct((CHIPS, part, cols), F32),
+            jax.ShapeDtypeStruct((CHIPS, part, cols), BF16),
+        ),
+        in_specs=[SMEM, SMEM] + [VMEM] * 13,
+        out_specs=(VMEM, VMEM),
+        scratch_shapes=[pltpu.VMEM((rows, cols), F32)],
+        name="output",
+        **params(2 * rows * 2048 * cols, 2048 * cols * 2 + rows * 2048 * 2 + rows * cols * 3),
+    )(info, lengths, *blocks, *weights, *downs, up)
+
+
+def close_kernel(info_ref, stream_ref, gain_ref, *refs):
+    pieces = refs[:4]
+    out_ref = refs[4]
+    z = info_ref[1]
+    part = pieces[0].shape[0]
+    gain = gain_ref[...].astype(F32)
+    for k in range(4):
+        at = pl.multiple_of(jnp.bitwise_and(z - k + 4, 3) * part, part)
+        rows = pl.ds(at, part)
+        out_ref[rows, :] = (stream_ref[rows, :].astype(F32) + pieces[k][...].astype(F32) * gain).astype(BF16)
+
+
+def close(info, stream, gain, pieces):
+    return pl.pallas_call(
+        close_kernel,
+        out_shape=jax.ShapeDtypeStruct(stream.shape, BF16),
+        in_specs=[SMEM] + [VMEM] * 6,
+        out_specs=VMEM,
+        name="close",
+        **params(stream.size * 3, stream.size * 6),
+    )(info, stream, gain[None, :], *pieces)
+
+
+def per_device_heads(
+    residual,
+    pre_gain,
+    query_weight,
+    key_weight,
+    value_weight,
+    output_weight,
+    adapter_down,
+    adapter_up_query,
+    adapter_up_key,
+    adapter_up_value,
+    adapter_down_out,
+    adapter_up_out,
+    post_gain,
+    sink_logits,
+    prompt_lengths,
+    prompt_adapters,
+):
+    tok, features = residual.shape
+    depth = features // CHIPS
+    own_rows = query_weight.shape[0]
+    prompts = prompt_lengths.shape[0]
+    d = HEAD_DIM
+    me = lax.axis_index("wide")
+    z = lax.axis_index("narrow")
+    core = me & 1
+    chip = me >> 1
+    info = jnp.stack([me, z]).astype(jnp.int32)
+    wide = 2 * CHIPS
+    tokens = tok * wide
+
+    flip = lambda bits: [(i, i ^ bits) for i in range(wide)]
+    across = flip(1)
+    first_leg = [(i, i ^ (2 if i % 2 == 0 else 4)) for i in range(wide)]
+    second_leg = [(i, i ^ (4 if i % 2 == 0 else 2)) for i in range(wide)]
+    shift = lambda k: [(i, (i + k) % 4) for i in range(4)]
+    zflip = lambda bits: [(i, i ^ bits) for i in range(4)]
+
+    pieces = split(info, residual)
+    pieces = [pieces[0]] + [lax.ppermute(pieces[delta], "wide", flip(2 * delta)) for delta in (1, 2, 3)]
+    x_refs = []
+    for piece in pieces:
+        x_refs += [piece, lax.ppermute(piece, "wide", across)]
+
+    own_gain = lax.dynamic_slice(pre_gain, (me * own_rows,), (own_rows,)).astype(F32)
+    pack, up, out_down = adapters(
+        info, prompt_adapters, adapter_down, own_gain[None, :], adapter_up_query, adapter_up_key,
+        adapter_up_value, adapter_down_out, adapter_up_out,
+    )
+    pack = pack + lax.ppermute(pack, "narrow", zflip(1))
+    pack = pack + lax.ppermute(pack, "narrow", zflip(2))
+    pack = join(info, pack, lax.ppermute(pack, "wide", across))
+
+    w_mine, w_theirs = columns(info, query_weight, key_weight, value_weight, own_gain[:, None])
+    w_got = lax.ppermute(w_theirs, "wide", across)
+
+    ow_mine, ow_theirs = parity(info, output_weight)
+    out_weights = [join(info, ow_mine, lax.ppermute(ow_theirs, "wide", across))]
+    for _ in range(3):
+        out_weights.append(lax.ppermute(out_weights[-1], "narrow", shift(1)))
+    out_downs = [out_down] + [lax.ppermute(out_down, "narrow", shift(k)) for k in (1, 2, 3)]
+
+    stream = residual.astype(F32)
+    factor = lax.rsqrt(jnp.mean(stream * stream, axis=1) + epsilon)
+    factors = jnp.where(
+        jnp.arange(wide, dtype=jnp.int32)[:, None] == me, factor[None, :], 0.0
+    )
+    for bits in (1, 2, 4):
+        factors = factors + lax.ppermute(factors, "wide", flip(bits))
+    factors = factors.reshape(tokens)[:, None]
+    _, _, position = token_layout(prompt_lengths, tokens, jnp.int32(0))
+    half = d // 2
+    exponent = jnp.arange(half, dtype=F32) * (2.0 / d)
+    frequency = jnp.power(jnp.float32(rotary_base), -exponent)
+    angle = position.astype(F32)[:, None] * frequency[None, :]
+    cosine, sine = jnp.cos(angle) * factors, jnp.sin(angle) * factors
+    q_cos = jnp.concatenate([cosine, cosine], axis=1)
+    q_sin = jnp.concatenate([-sine, sine], axis=1)
+    kv_cos = jnp.where(core == 0, q_cos, factors)
+    kv_sin = jnp.where(core == 0, q_sin, 0.0)
+
+    blocks = wide // CHUNKS
+    rows = blocks * tok
+    mine, other = [], []
+    near_blocks = [[] for _ in range(4)]
+    tables = (q_cos, q_sin, kv_cos, kv_sin)
+    for chunk in range(CHUNKS):
+        send, keep = project(info, prompt_lengths, x_refs, w_mine, w_got, pack, up, chunk, blocks)
+        one = lax.ppermute(send, "wide", first_leg)
+        own = keep.shape[1] // 2
+        onward = (keep[:, :own] + one[:, own:].astype(F32)).astype(BF16)
+        two = lax.ppermute(onward, "wide", second_leg)
+        q, kv = finish(keep, one, two, tables, chunk)
+        mine.append(kv)
+        other.append(lax.ppermute(kv, "wide", across))
+        sub = attend(info, prompt_lengths, sink_logits, q, mine, other, chunk * rows, tok)
+        got = [sub[0]] + [lax.ppermute(sub[k], "narrow", shift(k)) for k in (1, 2, 3)]
+        near0 = jnp.concatenate(got, axis=1)
+        near1 = lax.ppermute(near0, "wide", first_leg)
+        near23 = lax.ppermute(jnp.stack([near0, near1]), "wide", second_leg)
+        for r, block in enumerate((near0, near1, near23[0], near23[1])):
+            near_blocks[r].append(block)
+    gathered = [jnp.concatenate(b, axis=0) for b in near_blocks]
+
+    kept, sent = output(info, prompt_lengths, gathered, out_weights, out_downs, pack)
+    total = (kept + lax.ppermute(sent, "wide", across).astype(F32)).astype(BF16)
+    rows_of = lambda to: lax.dynamic_index_in_dim(total, to, 0, keepdims=False)
+    full = [rows_of(chip)] + [
+        lax.ppermute(rows_of(chip ^ delta), "wide", flip(2 * delta)) for delta in (1, 2, 3)
+    ]
+    full = jnp.stack(full)
+    wide_rows = full.astype(F32)
+    mean_square = jnp.sum(wide_rows * wide_rows, axis=(0, 2)) / features
+    scaled = (wide_rows * lax.rsqrt(mean_square + epsilon)[None, :, None]).astype(BF16)
+    finals = []
+    for k in range(4):
+        piece = lax.dynamic_index_in_dim(scaled, chip ^ ((z + k) & 3), 0, keepdims=False)
+        finals.append(piece if k == 0 else lax.ppermute(piece, "narrow", shift(k)))
+    own_width = post_gain.shape[0]
+    own_stream = lax.dynamic_slice_in_dim(residual, z * own_width, own_width, 1)
+    return close(info, own_stream, post_gain, finals)
 def rotate(values, position):
     half = values.shape[-1] // 2
     exponent = jnp.arange(half, dtype=jnp.float32) * (2.0 / values.shape[-1])
@@ -174,9 +755,13 @@
     return mixed.astype(jnp.bfloat16)
 
 
+def fits(mesh):
+    return mesh.shape["wide"] == 2 * CHIPS and mesh.shape["narrow"] == 4
+
+
 def solution(mesh):
     return jax.shard_map(
-        per_device,
+        per_device_heads if fits(mesh) else per_device,
         mesh=mesh,
         in_specs=(
             P("wide", None),

time: 455 us -> 262 us (0.58)
  waiting for transfers between devices: 335 us -> 113 us
  Pallas kernels: 0 us -> 57.6 us
  starting transfers between devices: 0.72 us -> 49.7 us
  matrix products: 46.3 us -> 0 us
  blocking collectives: 14.7 us -> 0 us
  between operations: 13.5 us -> 0.74 us
  other arithmetic: 27.4 us -> 16.9 us
  local copies, waits for them, and re-layouts: 17 us -> 23.3 us
    all_gather x7 -> x0, waiting for transfers between devices: 211 us -> none  [the longest x1 52.3 us: per_device(): lax.all_gather(query_weight, 'wide', axis=0, tiled=True)]
    psum x2 -> x0, waiting for transfers between devices: 121 us -> none  [the longest x1 92.7 us: per_device(): lax.psum(partial_out.astype(jnp.bfloat16), 'narrow').astype(jnp.float32)]
    ppermute x0 -> x60, waiting for transfers between devices: none -> 113 us  [the longest x12 33.3 us: per_device_heads(): lax.ppermute(sub[k], 'narrow', shift(k))]
    pallas_call x0 -> x20, Pallas kernels: none -> 57.6 us  [the longest x4 23.6 us: project(): pl.pallas_call(functools.partial(project_kernel, blocks, chunk * blocks,...]
    ppermute x0 -> x60, starting transfers between devices: none -> 49.7 us  [the longest x12 8.08 us: per_device_heads(): lax.ppermute(sub[k], 'narrow', shift(k))]
    dot_general x12 -> x0, matrix products: 46.3 us -> none  [the longest x4 15.4 us: per_device(): jnp.dot(normed, piece, preferred_element_type=jnp.float32)]
    all_gather x1 -> x0, blocking collectives: 14.7 us -> none  [per_device(): lax.all_gather(code_part.astype(jnp.bfloat16), 'narrow', axis=1, tiled=True)]
    unnamed x30 -> x87, local copies, waits for them, and re-layouts: 7.27 us -> 18.6 us
  transfers between devices with their start and end apart: 9 -> 60, of which waited for: 9 -> 31; matrix products, arithmetic and copies ran while one was open for 16% -> 8% of each run, Pallas kernels for 0% -> 19%
where the time goes in v1:
time: 262 us; the launch traced here: 261 us
  waiting for transfers between devices  113 us (43%)
  Pallas kernels  57.6 us (22%)
  starting transfers between devices  49.7 us (19%)
  local copies, waits for them, and re-layouts  23.3 us (9%)
  other arithmetic  16.9 us (6%)
    ppermute x12, waiting for transfers between devices, per_device_heads(): lax.ppermute(sub[k], 'narrow', shift(k))  33.3 us
    pallas_call x4, Pallas kernels, project(): pl.pallas_call(functools.partial(project_kernel, blocks, chunk * blocks,...  23.6 us
    unnamed x87, local copies, waits for them, and re-layouts  18.6 us
    ppermute x3, waiting for transfers between devices, per_device_heads(): factors = factors + lax.ppermute(factors, 'wide', flip(bits))  17.8 us
    ppermute x3, waiting for transfers between devices, per_device_heads(): lax.ppermute(out_down, 'narrow', shift(k))  13.3 us
    ppermute x4, waiting for transfers between devices, per_device_heads(): near1 = lax.ppermute(near0, 'wide', first_leg)  12 us
    pallas_call x4, Pallas kernels, attend(): pl.pallas_call(functools.partial(attend_kernel, first, count, lengths.sha...  11.6 us
    ppermute x4, waiting for transfers between devices, per_device_heads(): near23 = lax.ppermute(jnp.stack([near0, near1]), 'wide', second_leg)  8.61 us
  transfers between devices with their start and end apart: 60, of which 31 were waited for; matrix products, arithmetic and copies ran while one was open for 8% of the time, Pallas kernels for 19%

profile of v1, /device:TPU:0, one launch (start us, length us, event | category | flops | bytes accessed | tf_op | source)
XLA Modules:
  0.0 261.0 jit_solution(16163135929488404234)
XLA Ops:
  8.6 3.1 %collective-permute-start.8 = (bf16[256,576]{1,0:T(8,128)(2,1)S(1)}, bf16[256,576]{1,0:T(8,128)(2,1)S(1)}, u32[]{:S(2)}, u32[]{:S(2)}) collective-permute-start(bf16[256,576]{1,0:T(8,128)(2,1)S(1)} %get-tuple-element.56), channel_id=1, source_target_pairs={{0,1},{1,0},{2,3},{3,2},{4,5},{5,4},{6,7},{7,6},{8,9},{9,8},{10,11... | collective-permute-start | bytes 884744 | tf_op jit(solution)/shard_map/ppermute | solution.py:538
  19.4 2.8 %collective-permute-start.9 = (bf16[256,576]{1,0:T(8,128)(2,1)S(1)}, bf16[256,576]{1,0:T(8,128)(2,1)S(1)}, u32[]{:S(2)}, u32[]{:S(2)}) collective-permute-start(bf16[256,576]{1,0:T(8,128)(2,1)S(1)} %add.92), channel_id=1, source_target_pairs={{0,2},{1,3},{2,0},{3,1},{4,6},{5,7},{6,4},{7,5},{8,10},{9,11},{10,... | collective-permute-start | bytes 884744 | tf_op jit(solution)/shard_map/ppermute | solution.py:539
  27.3 15.8 %collective-permute-done.14 = f32[8,256]{1,0:T(8,128)S(1)} collective-permute-done((f32[8,256]{1,0:T(8,128)S(1)}, f32[8,256]{1,0:T(8,128)S(1)}, u32[]{:S(2)}, u32[]{:S(2)}) %collective-permute-start.14) | collective-permute-done | bytes 8224 | tf_op jit(solution)/shard_map/ppermute | solution.py:557
  49.2 2.4 copy.29.w_ref
  52.9 2.3 parity.1
  62.0 5.9 %project.4 = (bf16[512,512]{1,0:T(8,128)(2,1)}, f32[512,512]{1,0:T(8,128)}) custom-call(s32[2]{0:T(128)S(1)} %pad_add_fusion.info_ref, s32[4]{0:T(128)S(1)} %copy-done.25, bf16[256,1152]{1,0:T(8,128)(2,1)S(1)} %get-tuple-element.50.refs_0_, bf16[256,1152]{1,0:T(8,128)(2,1)} %collective-permute-done.refs_1_, ...), custom_call_target="tpu_custom_call" | custom-call | flops 1207959552 | bytes 5111808 | tf_op jit(solution)/shard_map/project/pallas_call | solution.py:303
  69.6 6.0 %project.5 = (bf16[512,512]{1,0:T(8,128)(2,1)}, f32[512,512]{1,0:T(8,128)}) custom-call(s32[2]{0:T(128)S(1)} %pad_add_fusion.info_ref, s32[4]{0:T(128)S(1)} %copy-done.25, bf16[256,1152]{1,0:T(8,128)(2,1)S(1)} %get-tuple-element.50.refs_0_, bf16[256,1152]{1,0:T(8,128)(2,1)} %collective-permute-done.refs_1_, ...), custom_call_target="tpu_custom_call" | custom-call | flops 1207959552 | bytes 5111808 | tf_op jit(solution)/shard_map/project/pallas_call | solution.py:303
  75.9 6.1 %fusion.4 = (f32[2048,64]{1,0:T(8,128)}, f32[2048,64]{1,0:T(8,128)}, f32[2048,64]{1,0:T(8,128)}) fusion(f32[2048]{0:T(1024)S(1)} %bitcast.64, f32[64]{0:T(128)S(1)} %copy-done.33, f32[2048]{0:T(1024)S(1)} %subtract_convert_fusion), kind=kLoop, calls=%fused_computation.23 | loop fusion | flops 524288 | bytes 1589504 | tf_op jit(solution)/shard_map/neg | solution.py:566
  87.9 5.9 %project.6 = (bf16[512,512]{1,0:T(8,128)(2,1)S(1)}, f32[512,512]{1,0:T(8,128)}) custom-call(s32[2]{0:T(128)S(1)} %pad_add_fusion.info_ref, s32[4]{0:T(128)S(1)} %copy-done.25, bf16[256,1152]{1,0:T(8,128)(2,1)S(1)} %get-tuple-element.50.refs_0_, bf16[256,1152]{1,0:T(8,128)(2,1)} %collective-permute-done.refs_1_, ...), custom_call_target="tpu_custom_call" | custom-call | flops 1207959552 | bytes 5111808 | tf_op jit(solution)/shard_map/project/pallas_call | solution.py:303
  95.7 5.9 %project.7 = (bf16[512,512]{1,0:T(8,128)(2,1)S(1)}, f32[512,512]{1,0:T(8,128)}) custom-call(s32[2]{0:T(128)S(1)} %pad_add_fusion.info_ref, s32[4]{0:T(128)S(1)} %copy-done.25, bf16[256,1152]{1,0:T(8,128)(2,1)S(1)} %get-tuple-element.50.refs_0_, bf16[256,1152]{1,0:T(8,128)(2,1)} %collective-permute-done.refs_1_, ...), custom_call_target="tpu_custom_call" | custom-call | flops 1207959552 | bytes 5111808 | tf_op jit(solution)/shard_map/project/pallas_call | solution.py:303
  108.0 8.4 %collective-permute-done.32.first_ref = bf16[512,512]{1,0:T(8,128)(2,1)S(1)} collective-permute-done((bf16[512,512]{1,0:T(8,128)(2,1)S(1)}, bf16[512,512]{1,0:T(8,128)(2,1)S(1)}, u32[]{:S(2)}, u32[]{:S(2)}) %collective-permute-start.32) | collective-permute-done | bytes 524320 | tf_op jit(solution)/shard_map/ppermute | solution.py:577
  118.0 3.7 %broadcast_select_fusion = (f32[2048,128]{1,0:T(8,128)}, f32[2048,128]{1,0:T(8,128)S(1)}, f32[2048,128]{1,0:T(8,128)S(1)}, f32[2048,128]{1,0:T(8,128)S(1)}) fusion(pred[]{:T(512)S(6)} %eq.17, f32[2048,64]{1,0:T(8,128)} %get-tuple-element.116, f32[2048,64]{1,0:T(8,128)S(1)} %copy-done.30, f32[2048,64]{1,0:T(8,128)} %get-tuple-element.117, f32[2048]{0:T(1024)S(1)} %bitcast.65), kind=kLoop, calls=%fused_computation.20 | loop fusion | flops 1048576 | bytes 5775361 | tf_op jit(solution)/shard_map/jit(_where)/select_n | solution.py:568
  123.3 2.5 collective-permute-start.50
  134.5 4.0 %attend.5 = (bf16[128,128]{1,0:T(8,128)(2,1)S(1)}, bf16[128,128]{1,0:T(8,128)(2,1)S(1)}, bf16[128,128]{1,0:T(8,128)(2,1)S(1)}, bf16[128,128]{1,0:T(8,128)(2,1)S(1)}) custom-call(s32[2]{0:T(128)S(1)} %pad_add_fusion.info_ref, s32[4]{0:T(128)S(1)} %copy-done.25, f32[8]{0:T(128)S(1)} %copy-done.26, bf16[512,128]{1,0:T(8,128)(2,1)S(1)} %get-tuple-element.68.q_ref, ...), custom_call_target="tpu_custom_call" | custom-call | flops 201326592 | bytes 786432 | tf_op jit(solution)/shard_map/attend/pallas_call | solution.py:402
  140.2 2.2 attend.6
  144.6 3.2 %attend.7 = (bf16[128,128]{1,0:T(8,128)(2,1)S(1)}, bf16[128,128]{1,0:T(8,128)(2,1)S(1)}, bf16[128,128]{1,0:T(8,128)(2,1)S(1)}, bf16[128,128]{1,0:T(8,128)(2,1)S(1)}) custom-call(s32[2]{0:T(128)S(1)} %pad_add_fusion.info_ref, s32[4]{0:T(128)S(1)} %copy-done.25, f32[8]{0:T(128)S(1)} %copy-done.26, bf16[512,128]{1,0:T(8,128)(2,1)S(1)} %get-tuple-element.84.q_ref, ...), custom_call_target="tpu_custom_call" | custom-call | flops 201326592 | bytes 1310720 | tf_op jit(solution)/shard_map/attend/pallas_call | solution.py:402
  147.8 11.6 %collective-permute-done.17 = bf16[128,128]{1,0:T(8,128)(2,1)S(1)} collective-permute-done((bf16[128,128]{1,0:T(8,128)(2,1)S(1)}, bf16[128,128]{1,0:T(8,128)(2,1)S(1)}, u32[]{:S(2)}, u32[]{:S(2)}) %collective-permute-start.17) | collective-permute-done | bytes 32800 | tf_op jit(solution)/shard_map/ppermute | solution.py:585
  171.1 3.0 %collective-permute-done.29 = bf16[128,128]{1,0:T(8,128)(2,1)S(1)} collective-permute-done((bf16[128,128]{1,0:T(8,128)(2,1)S(1)}, bf16[128,128]{1,0:T(8,128)(2,1)S(1)}, u32[]{:S(2)}, u32[]{:S(2)}) %collective-permute-start.29) | collective-permute-done | bytes 32800 | tf_op jit(solution)/shard_map/ppermute | solution.py:585
  178.3 3.2 %collective-permute-done.35 = bf16[128,128]{1,0:T(8,128)(2,1)S(1)} collective-permute-done((bf16[128,128]{1,0:T(8,128)(2,1)S(1)}, bf16[128,128]{1,0:T(8,128)(2,1)S(1)}, u32[]{:S(2)}, u32[]{:S(2)}) %collective-permute-start.35) | collective-permute-done | bytes 32800 | tf_op jit(solution)/shard_map/ppermute | solution.py:585
  183.0 2.4 collective-permute-done.37
  185.5 2.5 collective-permute-done.38
  188.0 3.8 %collective-permute-done.39 = bf16[128,512]{1,0:T(8,128)(2,1)S(1)} collective-permute-done((bf16[128,512]{1,0:T(8,128)(2,1)S(1)}, bf16[128,512]{1,0:T(8,128)(2,1)S(1)}, u32[]{:S(2)}, u32[]{:S(2)}) %collective-permute-start.39) | collective-permute-done | bytes 131104 | tf_op jit(solution)/shard_map/ppermute | solution.py:587
  191.9 2.8 %collective-permute-done.40 = bf16[128,512]{1,0:T(8,128)(2,1)S(1)} collective-permute-done((bf16[128,512]{1,0:T(8,128)(2,1)S(1)}, bf16[128,512]{1,0:T(8,128)(2,1)S(1)}, u32[]{:S(2)}, u32[]{:S(2)}) %collective-permute-start.40) | collective-permute-done | bytes 131104 | tf_op jit(solution)/shard_map/ppermute | solution.py:587
  195.2 3.0 %collective-permute-done.41 = bf16[128,512]{1,0:T(8,128)(2,1)S(1)} collective-permute-done((bf16[128,512]{1,0:T(8,128)(2,1)S(1)}, bf16[128,512]{1,0:T(8,128)(2,1)S(1)}, u32[]{:S(2)}, u32[]{:S(2)}) %collective-permute-start.41) | collective-permute-done | bytes 131104 | tf_op jit(solution)/shard_map/ppermute | solution.py:587
  202.1 2.6 collective-permute-done.43
  211.2 13.3 %collective-permute-done.52.refs_11_ = bf16[64,512]{1,0:T(8,128)(2,1)S(1)} collective-permute-done((bf16[64,512]{1,0:T(8,128)(2,1)S(1)}, bf16[64,512]{1,0:T(8,128)(2,1)S(1)}, u32[]{:S(2)}, u32[]{:S(2)}) %collective-permute-start.52) | collective-permute-done | bytes 65568 | tf_op jit(solution)/shard_map/ppermute | solution.py:549
  225.5 6.3 %output.1 = (f32[4,64,1152]{2,1,0:T(8,128)S(1)}, bf16[4,64,1152]{2,1,0:T(8,128)(2,1)S(1)}) custom-call(s32[2]{0:T(128)S(1)} %pad_add_fusion.info_ref, s32[4]{0:T(128)S(1)} %copy-done.25, bf16[512,512]{1,0:T(8,128)(2,1)S(1)} %pad_maximum_fusion.3.refs_0_, bf16[512,512]{1,0:T(8,128)(2,1)S(1)} %pad_maximum_fusion.4.refs_1_, ...), custom_call_target="tpu_custom_call" | custom-call | flops 2415919104 | bytes 8585216 | tf_op jit(solution)/shard_map/output/pallas_call | solution.py:452
  239.9 3.2 %collective-permute-done.54 = bf16[64,1152]{1,0:T(8,128)(2,1)S(1)} collective-permute-done((bf16[64,1152]{1,0:T(8,128)(2,1)S(1)}, bf16[64,1152]{1,0:T(8,128)(2,1)S(1)}, u32[]{:S(2)}, u32[]{:S(2)}) %collective-permute-start.54) | collective-permute-done | bytes 147488 | tf_op jit(solution)/shard_map/ppermute | solution.py:597
  243.1 3.5 %collective-permute-done.55 = bf16[64,1152]{1,0:T(8,128)(2,1)S(1)} collective-permute-done((bf16[64,1152]{1,0:T(8,128)(2,1)S(1)}, bf16[64,1152]{1,0:T(8,128)(2,1)S(1)}, u32[]{:S(2)}, u32[]{:S(2)}) %collective-permute-start.55) | collective-permute-done | bytes 147488 | tf_op jit(solution)/shard_map/ppermute | solution.py:597
  248.4 2.6 collective-permute-start.59
  251.1 4.8 %collective-permute-done.57.refs_1_ = bf16[64,1152]{1,0:T(8,128)(2,1)S(1)} collective-permute-done((bf16[64,1152]{1,0:T(8,128)(2,1)S(1)}, bf16[64,1152]{1,0:T(8,128)(2,1)S(1)}, u32[]{:S(2)}, u32[]{:S(2)}) %collective-permute-start.57) | collective-permute-done | bytes 147488 | tf_op jit(solution)/shard_map/ppermute | solution.py:606
  255.8 3.7 %collective-permute-done.58.refs_2_ = bf16[64,1152]{1,0:T(8,128)(2,1)S(1)} collective-permute-done((bf16[64,1152]{1,0:T(8,128)(2,1)S(1)}, bf16[64,1152]{1,0:T(8,128)(2,1)S(1)}, u32[]{:S(2)}, u32[]{:S(2)}) %collective-permute-start.58) | collective-permute-done | bytes 147488 | tf_op jit(solution)/shard_map/ppermute | solution.py:606
  (245 shorter events, 107.8 us)
Async XLA Ops:
  8.6 10.8 %collective-permute-start.8 = (bf16[256,576]{1,0:T(8,128)(2,1)S(1)}, bf16[256,576]{1,0:T(8,128)(2,1)S(1)}, u32[]{:S(2)}, u32[]{:S(2)}) collective-permute-start(bf16[256,576]{1,0:T(8,128)(2,1)S(1)} %get-tuple-element.56), channel_id=1, source_target_pairs={{0,1},{1,0},{2,3},{3,2},{4,5},{5,4},{6,7},{7,6},{8,9},{9,8},{10,11... | collective-permute-start | bytes 884744 | tf_op jit(solution)/shard_map/ppermute | solution.py:538
  12.3 10.0 %collective-permute-start.13 = (f32[8,256]{1,0:T(8,128)S(1)}, f32[8,256]{1,0:T(8,128)S(1)}, u32[]{:S(2)}, u32[]{:S(2)}) collective-permute-start(f32[8,256]{1,0:T(8,128)S(1)} %broadcast_select_fusion.2), channel_id=1, source_target_pairs={{0,4},{4,0},{8,12},{12,8},{16,20},{20,16},{24,28},{28,24},{1,5},{5... | collective-permute-start | bytes 24584 | tf_op jit(solution)/shard_map/ppermute | solution.py:557
  14.2 32.8 %collective-permute-start.1 = (bf16[256,1152]{1,0:T(8,128)(2,1)}, bf16[256,1152]{1,0:T(8,128)(2,1)}, u32[]{:S(2)}, u32[]{:S(2)}) collective-permute-start(bf16[256,1152]{1,0:T(8,128)(2,1)} %get-tuple-element.51), channel_id=1, source_target_pairs={{0,8},{4,12},{8,0},{12,4},{16,24},{20,28},{24,16},{28,20},{1,9},{5... | collective-permute-start | bytes 1769480 | tf_op jit(solution)/shard_map/ppermute | solution.py:528
  15.7 31.8 %collective-permute-start.3 = (bf16[256,1152]{1,0:T(8,128)(2,1)}, bf16[256,1152]{1,0:T(8,128)(2,1)}, u32[]{:S(2)}, u32[]{:S(2)}) collective-permute-start(bf16[256,1152]{1,0:T(8,128)(2,1)} %get-tuple-element.52), channel_id=1, source_target_pairs={{0,16},{4,20},{8,24},{12,28},{16,0},{20,4},{24,8},{28,12},{1,17},{... | collective-permute-start | bytes 1769480 | tf_op jit(solution)/shard_map/ppermute | solution.py:528
  17.3 30.4 %collective-permute-start.5 = (bf16[256,1152]{1,0:T(8,128)(2,1)}, bf16[256,1152]{1,0:T(8,128)(2,1)}, u32[]{:S(2)}, u32[]{:S(2)}) collective-permute-start(bf16[256,1152]{1,0:T(8,128)(2,1)} %get-tuple-element.53), channel_id=1, source_target_pairs={{0,24},{4,28},{8,16},{12,20},{16,8},{20,12},{24,0},{28,4},{1,25},{... | collective-permute-start | bytes 1769480 | tf_op jit(solution)/shard_map/ppermute | solution.py:528
  19.4 23.7 %collective-permute-start.9 = (bf16[256,576]{1,0:T(8,128)(2,1)S(1)}, bf16[256,576]{1,0:T(8,128)(2,1)S(1)}, u32[]{:S(2)}, u32[]{:S(2)}) collective-permute-start(bf16[256,576]{1,0:T(8,128)(2,1)S(1)} %add.92), channel_id=1, source_target_pairs={{0,2},{1,3},{2,0},{3,1},{4,6},{5,7},{6,4},{7,5},{8,10},{9,11},{10,... | collective-permute-start | bytes 884744 | tf_op jit(solution)/shard_map/ppermute | solution.py:539
  22.3 20.7 %collective-permute-start.14 = (f32[8,256]{1,0:T(8,128)S(1)}, f32[8,256]{1,0:T(8,128)S(1)}, u32[]{:S(2)}, u32[]{:S(2)}) collective-permute-start(f32[8,256]{1,0:T(8,128)S(1)} %fusion.6), channel_id=1, source_target_pairs={{0,8},{4,12},{8,0},{12,4},{16,24},{20,28},{24,16},{28,20},{1,9},{5... | collective-permute-start | bytes 24584 | tf_op jit(solution)/shard_map/ppermute | solution.py:557
  43.0 18.9 %collective-permute-start.7 = (bf16[576,1024]{1,0:T(8,128)(2,1)}, bf16[576,1024]{1,0:T(8,128)(2,1)}, u32[]{:S(2)}, u32[]{:S(2)}) collective-permute-start(bf16[576,1024]{1,0:T(8,128)(2,1)} %get-tuple-element.55), channel_id=1, source_target_pairs={{0,4},{4,0},{8,12},{12,8},{16,20},{20,16},{24,28},{28,24},{1,5},{5... | collective-permute-start | bytes 3538952 | tf_op jit(solution)/shard_map/ppermute | solution.py:543
  47.0 14.5 %collective-permute-start = (bf16[256,1152]{1,0:T(8,128)(2,1)S(1)}, bf16[256,1152]{1,0:T(8,128)(2,1)}, u32[]{:S(2)}, u32[]{:S(2)}) collective-permute-start(bf16[256,1152]{1,0:T(8,128)(2,1)S(1)} %get-tuple-element.50.refs_0_), channel_id=1, source_target_pairs={{0,4},{4,0},{8,12},{12,8},{16,20},{20,16},{24,28},{28,24},{1,5},{5... | collective-permute-start | bytes 1769480 | tf_op jit(solution)/shard_map/ppermute | solution.py:531
  47.5 14.4 %collective-permute-start.2 = (bf16[256,1152]{1,0:T(8,128)(2,1)}, bf16[256,1152]{1,0:T(8,128)(2,1)}, u32[]{:S(2)}, u32[]{:S(2)}) collective-permute-start(bf16[256,1152]{1,0:T(8,128)(2,1)} %collective-permute-done.1.refs_2_), channel_id=1, source_target_pairs={{0,4},{4,0},{8,12},{12,8},{16,20},{20,16},{24,28},{28,24},{1,5},{5... | collective-permute-start | bytes 1769480 | tf_op jit(solution)/shard_map/ppermute | solution.py:531
  47.6 14.3 %collective-permute-start.4 = (bf16[256,1152]{1,0:T(8,128)(2,1)}, bf16[256,1152]{1,0:T(8,128)(2,1)}, u32[]{:S(2)}, u32[]{:S(2)}) collective-permute-start(bf16[256,1152]{1,0:T(8,128)(2,1)} %collective-permute-done.3.refs_4_), channel_id=1, source_target_pairs={{0,4},{4,0},{8,12},{12,8},{16,20},{20,16},{24,28},{28,24},{1,5},{5... | collective-permute-start | bytes 1769480 | tf_op jit(solution)/shard_map/ppermute | solution.py:531
  48.5 13.4 %collective-permute-start.6 = (bf16[256,1152]{1,0:T(8,128)(2,1)}, bf16[256,1152]{1,0:T(8,128)(2,1)}, u32[]{:S(2)}, u32[]{:S(2)}) collective-permute-start(bf16[256,1152]{1,0:T(8,128)(2,1)} %collective-permute-done.5.refs_6_), channel_id=1, source_target_pairs={{0,4},{4,0},{8,12},{12,8},{16,20},{20,16},{24,28},{28,24},{1,5},{5... | collective-permute-start | bytes 1769480 | tf_op jit(solution)/shard_map/ppermute | solution.py:531
  61.5 20.5 %collective-permute-start.46 = (bf16[512,576]{0,1:T(8,128)(2,1)S(1)}, bf16[512,576]{0,1:T(8,128)(2,1)}, u32[]{:S(2)}, u32[]{:S(2)}) collective-permute-start(bf16[512,576]{0,1:T(8,128)(2,1)S(1)} %copy-done.31), channel_id=1, source_target_pairs={{0,4},{4,0},{8,12},{12,8},{16,20},{20,16},{24,28},{28,24},{1,5},{5... | collective-permute-start | bytes 1769480 | tf_op jit(solution)/shard_map/ppermute | solution.py:546
  67.9 34.0 %collective-permute-start.11 = (bf16[512,512]{1,0:T(8,128)(2,1)}, bf16[512,512]{1,0:T(8,128)(2,1)}, u32[]{:S(2)}, u32[]{:S(2)}) collective-permute-start(bf16[512,512]{1,0:T(8,128)(2,1)} %get-tuple-element.59), channel_id=1, source_target_pairs={{0,8},{4,20},{8,0},{12,28},{16,24},{20,4},{24,16},{28,12},{1,9},{5... | collective-permute-start | bytes 1572872 | tf_op jit(solution)/shard_map/ppermute | solution.py:577
  75.6 29.1 %collective-permute-start.20 = (bf16[512,512]{1,0:T(8,128)(2,1)}, bf16[512,512]{1,0:T(8,128)(2,1)}, u32[]{:S(2)}, u32[]{:S(2)}) collective-permute-start(bf16[512,512]{1,0:T(8,128)(2,1)} %get-tuple-element.67), channel_id=1, source_target_pairs={{0,8},{4,20},{8,0},{12,28},{16,24},{20,4},{24,16},{28,12},{1,9},{5... | collective-permute-start | bytes 1572872 | tf_op jit(solution)/shard_map/ppermute | solution.py:577
  87.2 40.0 %collective-permute-start.47 = (bf16[512,1152]{1,0:T(8,128)(2,1)S(1)}, bf16[512,1152]{1,0:T(8,128)(2,1)}, u32[]{:S(2)}, u32[]{:S(2)}) collective-permute-start(bf16[512,1152]{1,0:T(8,128)(2,1)S(1)} %join.3.refs_4_), channel_id=1, source_target_pairs={{0,1},{1,2},{2,3},{3,0},{4,5},{5,6},{6,7},{7,4},{8,9},{9,10},{10,1... | collective-permute-start | bytes 3538952 | tf_op jit(solution)/shard_map/ppermute | solution.py:548
  93.8 12.5 %collective-permute-start.26 = (bf16[512,512]{1,0:T(8,128)(2,1)S(1)}, bf16[512,512]{1,0:T(8,128)(2,1)S(1)}, u32[]{:S(2)}, u32[]{:S(2)}) collective-permute-start(bf16[512,512]{1,0:T(8,128)(2,1)S(1)} %get-tuple-element.75), channel_id=1, source_target_pairs={{0,8},{4,20},{8,0},{12,28},{16,24},{20,4},{24,16},{28,12},{1,9},{5... | collective-permute-start | bytes 1572872 | tf_op jit(solution)/shard_map/ppermute | solution.py:577
  101.6 14.8 %collective-permute-start.32 = (bf16[512,512]{1,0:T(8,128)(2,1)S(1)}, bf16[512,512]{1,0:T(8,128)(2,1)S(1)}, u32[]{:S(2)}, u32[]{:S(2)}) collective-permute-start(bf16[512,512]{1,0:T(8,128)(2,1)S(1)} %get-tuple-element.83), channel_id=1, source_target_pairs={{0,8},{4,20},{8,0},{12,28},{16,24},{20,4},{24,16},{28,12},{1,9},{5... | collective-permute-start | bytes 1572872 | tf_op jit(solution)/shard_map/ppermute | solution.py:577
  103.1 18.7 %collective-permute-start.12 = (bf16[512,256]{1,0:T(8,128)(2,1)S(1)}, bf16[512,256]{1,0:T(8,128)(2,1)S(1)}, u32[]{:S(2)}, u32[]{:S(2)}) collective-permute-start(bf16[512,256]{1,0:T(8,128)(2,1)S(1)} %add_convert_fusion.4), channel_id=1, source_target_pairs={{0,16},{4,12},{8,24},{12,4},{16,0},{20,28},{24,8},{28,20},{1,17},{... | collective-permute-start | bytes 786440 | tf_op jit(solution)/shard_map/ppermute | solution.py:580
  105.8 17.5 %collective-permute-start.21 = (bf16[512,256]{1,0:T(8,128)(2,1)S(1)}, bf16[512,256]{1,0:T(8,128)(2,1)S(1)}, u32[]{:S(2)}, u32[]{:S(2)}) collective-permute-start(bf16[512,256]{1,0:T(8,128)(2,1)S(1)} %add_convert_fusion.3), channel_id=1, source_target_pairs={{0,16},{4,12},{8,24},{12,4},{16,0},{20,28},{24,8},{28,20},{1,17},{... | collective-permute-start | bytes 786440 | tf_op jit(solution)/shard_map/ppermute | solution.py:580
  106.4 22.1 %collective-permute-start.27 = (bf16[512,256]{1,0:T(8,128)(2,1)S(1)}, bf16[512,256]{1,0:T(8,128)(2,1)S(1)}, u32[]{:S(2)}, u32[]{:S(2)}) collective-permute-start(bf16[512,256]{1,0:T(8,128)(2,1)S(1)} %add_convert_fusion.2), channel_id=1, source_target_pairs={{0,16},{4,12},{8,24},{12,4},{16,0},{20,28},{24,8},{28,20},{1,17},{... | collective-permute-start | bytes 786440 | tf_op jit(solution)/shard_map/ppermute | solution.py:580
  116.5 13.9 %collective-permute-start.33 = (bf16[512,256]{1,0:T(8,128)(2,1)S(1)}, bf16[512,256]{1,0:T(8,128)(2,1)S(1)}, u32[]{:S(2)}, u32[]{:S(2)}) collective-permute-start(bf16[512,256]{1,0:T(8,128)(2,1)S(1)} %add_convert_fusion.1), channel_id=1, source_target_pairs={{0,16},{4,12},{8,24},{12,4},{16,0},{20,28},{24,8},{28,20},{1,17},{... | collective-permute-start | bytes 786440 | tf_op jit(solution)/shard_map/ppermute | solution.py:580
  123.3 87.9 %collective-permute-start.50 = (bf16[64,512]{1,0:T(8,128)(2,1)S(1)}, bf16[64,512]{1,0:T(8,128)(2,1)S(1)}, u32[]{:S(2)}, u32[]{:S(2)}) collective-permute-start(bf16[64,512]{1,0:T(8,128)(2,1)S(1)} %copy-done.29), channel_id=1, source_target_pairs={{0,1},{1,2},{2,3},{3,0},{4,5},{5,6},{6,7},{7,4},{8,9},{9,10},{10,1... | collective-permute-start | bytes 196616 | tf_op jit(solution)/shard_map/ppermute | solution.py:549
  127.2 84.0 %collective-permute-start.51 = (bf16[64,512]{1,0:T(8,128)(2,1)S(1)}, bf16[64,512]{1,0:T(8,128)(2,1)S(1)}, u32[]{:S(2)}, u32[]{:S(2)}) collective-permute-start(bf16[64,512]{1,0:T(8,128)(2,1)S(1)} %copy-done.29), channel_id=1, source_target_pairs={{0,2},{1,3},{2,0},{3,1},{4,6},{5,7},{6,4},{7,5},{8,10},{9,11},{10,... | collective-permute-start | bytes 196616 | tf_op jit(solution)/shard_map/ppermute | solution.py:549
  128.5 73.1 %collective-permute-start.48 = (bf16[512,1152]{1,0:T(8,128)(2,1)}, bf16[512,1152]{1,0:T(8,128)(2,1)S(1)}, u32[]{:S(2)}, u32[]{:S(2)}) collective-permute-start(bf16[512,1152]{1,0:T(8,128)(2,1)} %collective-permute-done.47.refs_5_), channel_id=1, source_target_pairs={{0,1},{1,2},{2,3},{3,0},{4,5},{5,6},{6,7},{7,4},{8,9},{9,10},{10,1... | collective-permute-start | bytes 3538952 | tf_op jit(solution)/shard_map/ppermute | solution.py:548
  138.5 20.9 %collective-permute-start.17 = (bf16[128,128]{1,0:T(8,128)(2,1)S(1)}, bf16[128,128]{1,0:T(8,128)(2,1)S(1)}, u32[]{:S(2)}, u32[]{:S(2)}) collective-permute-start(bf16[128,128]{1,0:T(8,128)(2,1)S(1)} %get-tuple-element.63), channel_id=1, source_target_pairs={{0,1},{1,2},{2,3},{3,0},{4,5},{5,6},{6,7},{7,4},{8,9},{9,10},{10,1... | collective-permute-start | bytes 98312 | tf_op jit(solution)/shard_map/ppermute | solution.py:585
  142.4 18.8 %collective-permute-start.18 = (bf16[128,128]{1,0:T(8,128)(2,1)S(1)}, bf16[128,128]{1,0:T(8,128)(2,1)S(1)}, u32[]{:S(2)}, u32[]{:S(2)}) collective-permute-start(bf16[128,128]{1,0:T(8,128)(2,1)S(1)} %get-tuple-element.64), channel_id=1, source_target_pairs={{0,2},{1,3},{2,0},{3,1},{4,6},{5,7},{6,4},{7,5},{8,10},{9,11},{10,... | collective-permute-start | bytes 98312 | tf_op jit(solution)/shard_map/ppermute | solution.py:585
  201.6 22.9 %collective-permute-start.49 = (bf16[512,1152]{1,0:T(8,128)(2,1)S(1)}, bf16[512,1152]{1,0:T(8,128)(2,1)S(1)}, u32[]{:S(2)}, u32[]{:S(2)}) collective-permute-start(bf16[512,1152]{1,0:T(8,128)(2,1)S(1)} %collective-permute-done.48.refs_6_), channel_id=1, source_target_pairs={{0,1},{1,2},{2,3},{3,0},{4,5},{5,6},{6,7},{7,4},{8,9},{9,10},{10,1... | collective-permute-start | bytes 3538952 | tf_op jit(solution)/shard_map/ppermute | solution.py:548
  207.4 17.0 %collective-permute-start.52 = (bf16[64,512]{1,0:T(8,128)(2,1)S(1)}, bf16[64,512]{1,0:T(8,128)(2,1)S(1)}, u32[]{:S(2)}, u32[]{:S(2)}) collective-permute-start(bf16[64,512]{1,0:T(8,128)(2,1)S(1)} %copy-done.29), channel_id=1, source_target_pairs={{0,3},{1,0},{2,1},{3,2},{4,7},{5,4},{6,5},{7,6},{8,11},{9,8},{10,9... | collective-permute-start | bytes 196616 | tf_op jit(solution)/shard_map/ppermute | solution.py:549
  237.8 8.8 %collective-permute-start.55 = (bf16[64,1152]{1,0:T(8,128)(2,1)S(1)}, bf16[64,1152]{1,0:T(8,128)(2,1)S(1)}, u32[]{:S(2)}, u32[]{:S(2)}) collective-permute-start(bf16[64,1152]{1,0:T(8,128)(2,1)S(1)} %get-tuple-element.105), channel_id=1, source_target_pairs={{0,16},{4,20},{8,24},{12,28},{16,0},{20,4},{24,8},{28,12},{1,17},{... | collective-permute-start | bytes 442376 | tf_op jit(solution)/shard_map/ppermute | solution.py:597
  247.7 11.7 %collective-permute-start.58 = (bf16[64,1152]{1,0:T(8,128)(2,1)S(1)}, bf16[64,1152]{1,0:T(8,128)(2,1)S(1)}, u32[]{:S(2)}, u32[]{:S(2)}) collective-permute-start(bf16[64,1152]{1,0:T(8,128)(2,1)S(1)} %get-tuple-element.100), channel_id=1, source_target_pairs={{0,2},{1,3},{2,0},{3,1},{4,6},{5,7},{6,4},{7,5},{8,10},{9,11},{10,... | collective-permute-start | bytes 442376 | tf_op jit(solution)/shard_map/ppermute | solution.py:606
  248.4 11.1 %collective-permute-start.59 = (bf16[64,1152]{1,0:T(8,128)(2,1)S(1)}, bf16[64,1152]{1,0:T(8,128)(2,1)S(1)}, u32[]{:S(2)}, u32[]{:S(2)}) collective-permute-start(bf16[64,1152]{1,0:T(8,128)(2,1)S(1)} %get-tuple-element.99), channel_id=1, source_target_pairs={{0,3},{1,0},{2,1},{3,2},{4,7},{5,4},{6,5},{7,6},{8,11},{9,8},{10,9... | collective-permute-start | bytes 442376 | tf_op jit(solution)/shard_map/ppermute | solution.py:606
  (64 other events, 317.0 us)

commit v2 on v0

--- a/solution.py
+++ b/solution.py
@@ -1,16 +1,29 @@
+import functools
+
 import jax
 import jax.numpy as jnp
 from jax import lax
+from jax.experimental import pallas as pl
+from jax.experimental.pallas import tpu as pltpu
 from jax.sharding import PartitionSpec as P
 
 HEAD_DIM = 128
 ADAPTERS = 16
-
+RANK = 16
 
 epsilon = 1e-06
 adapter_scale = 0.5
 rotary_base = 10000.0
 score_scale = 1.0 / 12.0
+
+CHIPS = 4
+CHUNKS = 4
+F32 = jnp.float32
+BF16 = jnp.bfloat16
+SMEM = pl.BlockSpec(memory_space=pltpu.SMEM)
+VMEM = pl.BlockSpec(memory_space=pltpu.VMEM)
+ANY = pl.BlockSpec(memory_space=pl.ANY)
+HBM = pl.BlockSpec(memory_space=pltpu.HBM)
 
 
 def token_layout(prompt_lengths, count, first):
@@ -26,6 +39,706 @@
     return (member, prompt, position)
 
 
+def call(kernel, operands, specs, out_shape, after=(), scratch=(), name=None, flops=0, moved=0, transcendentals=0, grant=24, **more):
+    n = len(after)
+    return pl.pallas_call(
+        lambda *refs: kernel(*refs[n:]),
+        out_shape=out_shape,
+        in_specs=[ANY] * n + list(specs),
+        scratch_shapes=list(scratch),
+        name=name,
+        compiler_params=pltpu.CompilerParams(vmem_limit_bytes=grant * 1024 * 1024),
+        cost_estimate=pl.CostEstimate(flops=flops // 64, bytes_accessed=moved // 64, transcendentals=transcendentals // 64),
+        **more,
+    )(*after, *operands)
+
+
+def prompt_of(places, lengths_ref, prompts):
+    end = jnp.int32(0)
+    prompt = jnp.zeros_like(places)
+    start = jnp.zeros_like(places)
+    for p in range(prompts - 1):
+        end = end + lengths_ref[p]
+        past = places >= end
+        prompt = jnp.where(past, p + 1, prompt)
+        start = jnp.where(past, end, start)
+    return prompt, start
+
+
+def order(chip, core):
+    return (chip ^ (1 + core), chip ^ 3, chip ^ (2 - core), chip)
+
+
+NEXT = (1, 3, 0, 2)
+BEFORE = (2, 0, 3, 1)
+
+
+def plane(table, z):
+    return jnp.where(z == 0, table[0], jnp.where(z == 1, table[1], jnp.where(z == 2, table[2], table[3])))
+
+
+def near(chip, core):
+    return (chip, chip ^ (1 + core), chip ^ (2 - core), chip ^ 3)
+
+
+def norm_kernel(steps, x_hbm, gain_ref, *refs):
+    outs, (x_ref, y_ref, sems) = refs[:4], refs[4:]
+    chip = lax.shift_right_logical(lax.axis_index("wide"), 1)
+    depth = outs[0].shape[1]
+    step = x_ref.shape[0] // steps
+    copies = [
+        pltpu.make_async_copy(x_hbm.at[pl.ds(i * step, step), :], x_ref.at[pl.ds(i * step, step), :], sems.at[i])
+        for i in range(steps)
+    ]
+    for copy in copies:
+        copy.start()
+    gain = gain_ref[...].astype(F32)
+    for i in range(steps):
+        copies[i].wait()
+        rows = slice(i * step, (i + 1) * step)
+        x = x_ref[rows, :].astype(F32)
+        scale = lax.rsqrt(jnp.sum(x * x, axis=1, keepdims=True) / x.shape[1] + epsilon)
+        y_ref[...] = (x * scale * gain).astype(BF16)
+        for delta in range(4):
+            outs[delta][rows, :] = y_ref[:, pl.ds(pl.multiple_of((chip ^ delta) * depth, 128), depth)]
+
+
+def norm(x, gain, steps, after):
+    rows, cols = x.shape
+    shape = jax.ShapeDtypeStruct((rows, cols // CHIPS), x.dtype)
+    return call(
+        functools.partial(norm_kernel, steps), (x, gain[None, :]), [HBM, VMEM], (shape,) * 4, after,
+        scratch=[
+            pltpu.VMEM((rows, cols), BF16),
+            pltpu.VMEM((rows // steps, cols), BF16),
+            pltpu.SemaphoreType.DMA((steps,)),
+        ],
+        out_specs=(VMEM,) * 4, name="norm", grant=60, flops=x.size * 4, moved=x.size * 4,
+    )
+
+
+def arrange_kernel(q_ref, k_ref, v_ref, o_ref, mine_ref, theirs_ref, sems):
+    chip = lax.shift_right_logical(lax.axis_index("wide"), 1)
+    own = lax.axis_index("wide") & 1
+    d = HEAD_DIM
+    copies = []
+
+    def copy(ref, at, out, to, width):
+        source = ref.at[:, pl.ds(pl.multiple_of(at, d), width)]
+        copies.append(pltpu.make_async_copy(source, out.at[:, pl.ds(to, width)], sems.at[len(copies)]))
+        copies[-1].start()
+
+    for core, out in ((1 - own, theirs_ref), (own, mine_ref)):
+        for place, to in enumerate(order(chip, core)):
+            for ref, width, at in ((q_ref, 2 * d, 0), (k_ref, d, 2 * d), (v_ref, d, 3 * d)):
+                copy(ref, to * width, out, 4 * place * d + at, width)
+        for place, source in enumerate(near(chip, core)):
+            copy(o_ref, (2 * source + core) * d, out, (4 * CHIPS + place) * d, d)
+    for one in copies:
+        one.wait()
+
+
+def arrange(q, k, v, o, after):
+    shape = jax.ShapeDtypeStruct((q.shape[0], 5 * CHIPS * HEAD_DIM), BF16)
+    return call(
+        arrange_kernel, (q, k, v, o), [ANY] * 4, (shape, shape), after,
+        scratch=[pltpu.SemaphoreType.DMA((32,))], out_specs=(ANY, ANY), name="arrange", moved=q.size * 16,
+    )
+
+
+def choose(shape, row_prompt, chosen_ref, prompts):
+    adapter = jnp.zeros(shape, jnp.int32)
+    for p in range(prompts):
+        adapter = jnp.where(row_prompt == p, chosen_ref[p], adapter)
+    return adapter
+
+
+def pick_kernel(prompts, chosen_ref, down_hbm, upo_hbm, pack_ref, down_ref, upo_ref, sems):
+    me, z = lax.axis_index("wide"), lax.axis_index("narrow")
+    chip = lax.shift_right_logical(me, 1)
+    core = me & 1
+    n_codes = prompts * RANK
+    local = down_ref.shape[0] // (3 * RANK)
+    rows = down_ref.shape[1]
+    copies = [pltpu.make_async_copy(down_hbm, down_ref, sems.at[prompts])]
+    for p in range(prompts):
+        at = pl.ds(pl.multiple_of(chosen_ref[p] * RANK, RANK), RANK)
+        copies.append(pltpu.make_async_copy(upo_hbm.at[at, :], upo_ref.at[pl.ds(p * RANK, RANK), :], sems.at[p]))
+    for copy in copies:
+        copy.start()
+    shape = (3 * n_codes, down_ref.shape[0])
+    row = lax.broadcasted_iota(jnp.int32, shape, 0)
+    col = lax.broadcasted_iota(jnp.int32, shape, 1)
+    adapter = choose(shape, (row % n_codes) // RANK, chosen_ref, prompts)
+    wanted = (adapter - z * local) * (3 * RANK) + (row // n_codes) * RANK + row % RANK
+    inside = jnp.logical_and(adapter >= z * local, adapter < (z + 1) * local)
+    pick = jnp.where(jnp.logical_and(inside, col == wanted), 1.0, 0.0).astype(BF16)
+    for copy in copies:
+        copy.wait()
+    down = jnp.dot(pick, down_ref[...], preferred_element_type=F32)
+    pack_ref[: 3 * n_codes, :] = down.astype(BF16)
+    both = upo_ref[...].astype(F32) * adapter_scale
+    part = jnp.where(core == 0, both[:, :rows], both[:, rows:])
+    pack_ref[3 * n_codes :, :] = jnp.where(z == chip, part, 0.0).astype(BF16)
+
+
+def pick(chosen, down, upo, after):
+    prompts = chosen.shape[0]
+    n_codes = prompts * RANK
+    return call(
+        functools.partial(pick_kernel, prompts), (chosen, down, upo), [SMEM, HBM, HBM],
+        jax.ShapeDtypeStruct((4 * n_codes, down.shape[1]), BF16),
+        after,
+        scratch=[
+            pltpu.VMEM(down.shape, BF16),
+            pltpu.VMEM((n_codes, upo.shape[1]), BF16),
+            pltpu.SemaphoreType.DMA((prompts + 1,)),
+        ],
+        out_specs=VMEM, name="pick", grant=60, flops=down.size * 400, moved=down.size * 6,
+    )
+
+
+def merge_kernel(a_ref, b_ref, out_ref):
+    out_ref[...] = (a_ref[...].astype(F32) + b_ref[...].astype(F32)).astype(out_ref.dtype)
+
+
+def merge(a, b, after=()):
+    return call(
+        merge_kernel, (a, b), [VMEM, VMEM], jax.ShapeDtypeStruct(a.shape, BF16), after,
+        out_specs=VMEM, name="merge", flops=a.size, moved=a.size * 6,
+    )
+
+
+def ups_kernel(prompts, chosen_ref, upq_ref, upk_ref, upv_ref, ado_ref, up_ref, out_ref):
+    me = lax.axis_index("wide")
+    chip = lax.shift_right_logical(me, 1)
+    core = me & 1
+    d = HEAD_DIM
+    n_codes = prompts * RANK
+    up_ref[...] = jnp.zeros_like(up_ref)
+    for p in range(prompts):
+        rows = pl.ds(pl.multiple_of(chosen_ref[p] * RANK, RANK), RANK)
+        for place, to in enumerate(order(chip, core)):
+            for slot, (ref, width, at) in enumerate(((upq_ref, 2 * d, 0), (upk_ref, d, 2 * d), (upv_ref, d, 3 * d))):
+                part = ref[rows, pl.ds(pl.multiple_of(to * width, d), width)].astype(F32) * adapter_scale
+                first = slot * n_codes + p * RANK
+                left = 4 * place * d + at
+                up_ref[first : first + RANK, left : left + width] = part.astype(BF16)
+    shape = (n_codes, ado_ref.shape[1])
+    row = lax.broadcasted_iota(jnp.int32, shape, 0)
+    col = lax.broadcasted_iota(jnp.int32, shape, 1)
+    adapter = choose(shape, row // RANK, chosen_ref, prompts)
+    pick = jnp.where(col == adapter * RANK + row % RANK, 1.0, 0.0).astype(BF16)
+    for place, source in enumerate(near(chip, core)):
+        block = ado_ref[pl.ds(pl.multiple_of((2 * source + core) * d, d), d), :]
+        part = lax.dot_general(pick, block, (((1,), (1,)), ((), ())), preferred_element_type=F32)
+        out_ref[:, place * d : (place + 1) * d] = part.astype(BF16)
+
+
+def ups(chosen, upq, upk, upv, ado, after):
+    prompts = chosen.shape[0]
+    n_codes = prompts * RANK
+    return call(
+        functools.partial(ups_kernel, prompts), (chosen, upq, upk, upv, ado), [SMEM] + [VMEM] * 4,
+        (
+            jax.ShapeDtypeStruct((3 * n_codes, 2 * upq.shape[1]), BF16),
+            jax.ShapeDtypeStruct((n_codes, CHIPS * HEAD_DIM), BF16),
+        ),
+        after, out_specs=(VMEM,) * 2, name="ups", flops=upq.size * 100, moved=upq.size * 6,
+    )
+
+
+def stack_kernel(mine_ref, got_ref, down_ref, w_ref, ring_ref, sems):
+    core = lax.axis_index("wide") & 1
+    rows = mine_ref.shape[0]
+    cols = w_ref.shape[1]
+    width = ring_ref.shape[1]
+    copies = []
+    for i, (ref, at) in enumerate(((mine_ref, core), (got_ref, 1 - core))):
+        to = pl.ds(pl.multiple_of(at * rows, 16), rows)
+        copies.append(pltpu.make_async_copy(ref.at[:, pl.ds(cols, width)], ring_ref.at[to, :], sems.at[2 * i]))
+        copies.append(pltpu.make_async_copy(ref.at[:, pl.ds(0, cols)], w_ref.at[to, :], sems.at[2 * i + 1]))
+    copies.append(pltpu.make_async_copy(down_ref, ring_ref.at[pl.ds(2 * rows, down_ref.shape[0]), :], sems.at[4]))
+    for copy in copies:
+        copy.start()
+    for copy in copies:
+        copy.wait()
+
+
+def stack(mine, got, down, after):
+    rows, cols = mine.shape
+    width = down.shape[1]
+    return call(
+        stack_kernel, (mine, got, down), [ANY] * 3,
+        (
+            jax.ShapeDtypeStruct((2 * rows, cols - width), mine.dtype),
+            jax.ShapeDtypeStruct((2 * rows + down.shape[0], width), mine.dtype),
+        ),
+        after,
+        scratch=[pltpu.SemaphoreType.DMA((5,))], out_specs=(ANY, ANY), name="stack", moved=rows * cols * 8,
+    )
+
+
+def join_kernel(mine_ref, other_ref, out_ref):
+    core = lax.axis_index("wide") & 1
+    mine, other = mine_ref[...].astype(F32), other_ref[...].astype(F32)
+    left = jnp.where(core == 0, mine, other)
+    right = jnp.where(core == 0, other, mine)
+    out_ref[...] = jnp.concatenate([left, right], axis=1).astype(out_ref.dtype)
+
+
+def join(mine, other):
+    rows, cols = mine.shape
+    return call(
+        join_kernel, (mine, other), [VMEM, VMEM], jax.ShapeDtypeStruct((rows, 2 * cols), mine.dtype),
+        out_specs=VMEM, name="join", flops=rows * cols * 4, moved=rows * cols * 8,
+    )
+
+
+def project_kernel(chunk, prompts, lengths_ref, *refs):
+    x_refs = refs[:4]
+    w_ref, pack_ref, up_ref = refs[4:7]
+    send_ref, keep_ref, x_ref, sem = refs[-4:]
+    me = lax.axis_index("wide")
+    chip = lax.shift_right_logical(me, 1)
+    core = me & 1
+    rows = x_ref.shape[0]
+    half = send_ref.shape[1]
+    n_codes = prompts * RANK
+    for k in range(4):
+
+        @pl.when((chip ^ chunk) == k)
+        def _():
+            pltpu.make_async_copy(x_refs[k], x_ref, sem).start()
+
+    pltpu.make_async_copy(x_refs[0], x_ref, sem).wait()
+    x = x_ref[...]
+    codes = lax.dot_general(
+        x, pack_ref[: 3 * n_codes, :], (((1,), (1,)), ((), ())), preferred_element_type=F32
+    )
+    places = (2 * chunk + core) * rows + lax.broadcasted_iota(jnp.int32, (rows, 1), 0)
+    prompt, _ = prompt_of(places, lengths_ref, prompts)
+    lane = lax.broadcasted_iota(jnp.int32, codes.shape, 1)
+    owner = (lane % n_codes) // RANK
+    codes = jnp.where(owner == prompt, codes, 0.0).astype(BF16)
+    for part, out in ((0, send_ref), (1, keep_ref)):
+        cols = pl.ds(part * half, half)
+        product = jnp.dot(x, w_ref[:, cols], preferred_element_type=F32)
+        product = product + jnp.dot(codes, up_ref[:, cols], preferred_element_type=F32)
+        out[...] = product.astype(out.dtype)
+
+
+def project(lengths, pieces, w, pack, up, chunk, after, carry=()):
+    rows, depth = pieces[0].shape
+    half = w.shape[1] // 2
+    n = len(after) + 8
+    out = call(
+        functools.partial(project_kernel, chunk, lengths.shape[0]),
+        (lengths, *pieces, w, pack, up, *carry),
+        [SMEM] + [ANY] * 4 + [VMEM] * 3 + [ANY] * len(carry),
+        tuple(jax.ShapeDtypeStruct(c.shape, c.dtype) for c in carry)
+        + (jax.ShapeDtypeStruct((rows, half), BF16), jax.ShapeDtypeStruct((rows, half), F32)),
+        after,
+        scratch=[pltpu.VMEM((rows, depth), BF16), pltpu.SemaphoreType.DMA(())],
+        out_specs=(ANY,) * len(carry) + (VMEM, VMEM), name="project",
+        input_output_aliases={n + i: i for i in range(len(carry))},
+        flops=2 * rows * depth * w.shape[1], moved=rows * depth * 2 + w.size * 2 + rows * half * 6,
+    )
+    return out[-2], out[-1], out[:-2]
+
+
+def onward_kernel(keep_ref, first_ref, *refs):
+    out_ref = refs[-1]
+    own = out_ref.shape[1]
+    out_ref[...] = (keep_ref[:, :own] + first_ref[:, own:].astype(F32)).astype(BF16)
+
+
+def onward(keep, first, after, carry=()):
+    rows, cols = keep.shape
+    n = len(after) + 2
+    out = call(
+        onward_kernel, (keep, first, *carry), [VMEM, VMEM] + [ANY] * len(carry),
+        tuple(jax.ShapeDtypeStruct(c.shape, c.dtype) for c in carry)
+        + (jax.ShapeDtypeStruct((rows, cols // 2), BF16),),
+        after, out_specs=(ANY,) * len(carry) + (VMEM,), name="onward",
+        input_output_aliases={n + i: i for i in range(len(carry))},
+        flops=rows * cols, moved=rows * cols * 4,
+    )
+    return out[-1], out[:-1]
+
+
+def finish_kernel(chunk, keep_ref, first_ref, second_ref, cos_ref, sin_ref, own_ref, send_ref):
+    rows = own_ref.shape[0]
+    d = HEAD_DIM
+    own = keep_ref.shape[1] // 2
+    core = lax.axis_index("wide") & 1
+    at = pl.ds(pl.multiple_of((2 * chunk + core) * rows, rows), rows)
+    cosine, sine = cos_ref[at, :], sin_ref[at, :]
+
+    def turned(x):
+        return x * cosine + pltpu.roll(x, d // 2, 1) * sine
+
+    total = keep_ref[:, own:] + first_ref[:, :own].astype(F32) + second_ref[...].astype(F32)
+    q0, q1, k = (turned(total[:, i * d : (i + 1) * d]) for i in range(3))
+    own_ref[:, :d] = jnp.where(core == 0, q0, q1).astype(BF16)
+    send_ref[:, :d] = jnp.where(core == 0, q1, q0).astype(BF16)
+    both = jnp.concatenate([k, total[:, 3 * d :]], axis=1).astype(BF16)
+    own_ref[:, d:] = both
+    send_ref[:, d:] = both
+
+
+def finish(keep, first, second, tables, chunk, after):
+    rows = keep.shape[0]
+    shape = jax.ShapeDtypeStruct((rows, 3 * HEAD_DIM), BF16)
+    return call(
+        functools.partial(finish_kernel, chunk),
+        (keep, first, second, *tables), [VMEM] * 5, (shape, shape), after,
+        out_specs=(VMEM, VMEM), name="finish", flops=rows * 2048, moved=rows * 8192,
+    )
+
+
+def attend_kernel(chunk, prompts, n_before, n_carry, lengths_ref, sink_ref, *refs):
+    count = chunk + 1
+    mine_refs, other_refs = refs[:count], refs[count : 2 * count]
+    befores = refs[2 * count : 2 * count + n_before]
+    outs = refs[2 * count + n_before + 2 * n_carry :][:4]
+    q_ref, k_ref, v_ref, out_ref = refs[-4:]
+    step = mine_refs[0].shape[0]
+    d = HEAD_DIM
+    here, z = lax.axis_index("wide"), lax.axis_index("narrow")
+    core = here & 1
+    for i in range(count):
+        mine, other = mine_refs[i][...], other_refs[i][...]
+        for half, block in enumerate((jnp.where(core == 0, mine, other), jnp.where(core == 0, other, mine))):
+            at = pl.ds((2 * i + half) * step, step)
+            k_ref[at, :] = block[:, d : 2 * d]
+            v_ref[at, :] = block[:, 2 * d :]
+            if i == chunk:
+                q_ref[half] = block[:, :d]
+    sink = sink_ref[here]
+    to = (z, plane(NEXT, z), 3 - z, plane(BEFORE, z))
+    part = step // 4
+    shift = 0
+    for k in range(n_before):
+        shift = befores[k].shape[0]
+        outs[k][:shift, :] = befores[k][...]
+    for block in range(2):
+        base = (2 * chunk + block) * step
+        q = q_ref[block]
+        places = base + lax.broadcasted_iota(jnp.int32, (step, 1), 0)
+        _, starts = prompt_of(places, lengths_ref, prompts)
+        end = jnp.int32(0)
+        low = jnp.int32(0)
+        for p in range(prompts - 1):
+            end = end + lengths_ref[p]
+            low = jnp.where(base >= end, end, low)
+
+        def body(i, carry):
+            top, total, summed = carry
+            at = pl.multiple_of(i * step, step)
+            k = k_ref[pl.ds(at, step), :]
+            v = v_ref[pl.ds(at, step), :]
+            scores = lax.dot_general(q, k, (((1,), (1,)), ((), ())), preferred_element_type=F32) * score_scale
+            keys = at + lax.broadcasted_iota(jnp.int32, (step, step), 1)
+            allowed = jnp.logical_and(keys >= starts, keys <= places)
+            scores = jnp.where(allowed, scores, -1e30)
+            fresh = jnp.maximum(top, jnp.max(scores, axis=1, keepdims=True))
+            factor = jnp.exp(top - fresh)
+            weights = jnp.exp(scores - fresh)
+            total = total * factor + jnp.sum(weights, axis=1, keepdims=True)
+            summed = summed * factor + jnp.dot(weights.astype(BF16), v, preferred_element_type=F32)
+            return fresh, total, summed
+
+        top = jnp.full((step, 1), sink, F32)
+        total = jnp.ones((step, 1), F32)
+        summed = jnp.zeros((step, d), F32)
+        top, total, summed = lax.fori_loop(
+            low // step, 2 * chunk + block + 1, body, (top, total, summed)
+        )
+        out_ref[...] = (summed / total).astype(BF16)
+        for k in range(4):
+            at = pl.multiple_of(to[k] * part, part)
+            first = shift + block * part
+            outs[k][first : first + part, :] = out_ref[pl.ds(at, part), :]
+
+
+def attend(lengths, sinks, mine, other, chunk, after, before=(), carry=()):
+    step = mine[0].shape[0]
+    d = HEAD_DIM
+    count = chunk + 1
+    rows = step // 2 + (before[0].shape[0] if before else 0)
+    n = len(after) + 2 + 2 * count + len(before)
+    out = call(
+        functools.partial(attend_kernel, chunk, lengths.shape[0], len(before), len(carry)),
+        (lengths, sinks, *mine[:count], *other[:count], *before, *carry),
+        [SMEM, SMEM] + [VMEM] * (2 * count + len(before)) + [ANY] * len(carry),
+        tuple(jax.ShapeDtypeStruct(c.shape, c.dtype) for c in carry)
+        + (jax.ShapeDtypeStruct((rows, d), BF16),) * 4,
+        after,
+        scratch=[pltpu.VMEM((2, step, d), BF16)]
+        + [pltpu.VMEM((2 * count * step, d), BF16)] * 2
+        + [pltpu.VMEM((step, d), BF16)],
+        out_specs=(ANY,) * len(carry) + (VMEM,) * 4, name="attend",
+        input_output_aliases={n + i: i for i in range(len(carry))},
+        flops=2 * step * 768 * 4 * d, moved=step * d * 8 * count, transcendentals=2 * step * 768,
+    )
+    return out[len(carry) :], out[: len(carry)]
+
+
+def beside_kernel(*refs):
+    out_ref = refs[-1]
+    width = refs[0].shape[1]
+    for i, ref in enumerate(refs[:-1]):
+        out_ref[:, i * width : (i + 1) * width] = ref[...]
+
+
+def beside(parts, after):
+    rows, cols = parts[0].shape
+    return call(
+        beside_kernel, parts, [VMEM] * len(parts), jax.ShapeDtypeStruct((rows, cols * len(parts)), BF16), after,
+        out_specs=VMEM, name="beside", moved=rows * cols * len(parts) * 4,
+    )
+
+
+def output_kernel(group, prompts, lengths_ref, *refs):
+    blocks = refs[:4]
+    weights = refs[4:7]
+    pack_ref, keep_ref, send_ref, acc_ref = refs[7:]
+    me, z = lax.axis_index("wide"), lax.axis_index("narrow")
+    core = me & 1
+    rows, cols = acc_ref.shape
+    d = HEAD_DIM
+    count, part = keep_ref.shape[1:3]
+    row = lax.broadcasted_iota(jnp.int32, (rows, 1), 0)
+    up = pack_ref[3 * prompts * RANK :, :]
+
+    def times(k, w_ref):
+        a = jnp.concatenate([blocks[r][:, k * d : (k + 1) * d] for r in range(4)], axis=1)
+        product = lax.dot_general(a, w_ref[:cols, :], (((1,), (1,)), ((), ())), preferred_element_type=F32)
+        codes = lax.dot_general(a, w_ref[cols:, :], (((1,), (1,)), ((), ())), preferred_element_type=F32)
+        return product, codes
+
+    def leave(slot, codes, plane):
+        places = (2 * count * group + row // part) * (4 * part) + plane * part + row % part
+        prompt, _ = prompt_of(places, lengths_ref, prompts)
+        lane = lax.broadcasted_iota(jnp.int32, codes.shape, 1)
+        codes = jnp.where(lane // RANK == prompt, codes, 0.0).astype(BF16)
+        acc_ref[...] += jnp.dot(codes, up, preferred_element_type=F32)
+        for i in range(count):
+            mine = pl.multiple_of(i * 2 * part + core * part, part)
+            theirs = pl.multiple_of(i * 2 * part + (1 - core) * part, part)
+            keep_ref[slot, i] = acc_ref[pl.ds(mine, part), :]
+            send_ref[slot, i] = acc_ref[pl.ds(theirs, part), :].astype(BF16)
+
+    product, codes = times(3, weights[0])
+    acc_ref[...] = product
+    leave(1, codes, plane(BEFORE, z))
+    product, codes = times(0, weights[0])
+    acc_ref[...] = product
+    for k in (1, 2):
+        product, terms = times(k, weights[k])
+        acc_ref[...] += product
+        codes = codes + terms
+    leave(0, codes, z)
+
+
+def output(lengths, blocks, weights, pack, group, part, after):
+    rows = blocks[0].shape[0]
+    cols = pack.shape[1]
+    shape = (2, rows // (2 * part), part, cols)
+    return call(
+        functools.partial(output_kernel, group, lengths.shape[0]),
+        (lengths, *blocks, *weights, pack),
+        [SMEM] + [VMEM] * 8,
+        (jax.ShapeDtypeStruct(shape, F32), jax.ShapeDtypeStruct(shape, BF16)),
+        after,
+        scratch=[pltpu.VMEM((rows, cols), F32)],
+        out_specs=(VMEM, VMEM), name="output",
+        flops=2 * rows * 2048 * cols, moved=2048 * cols * 2 + rows * 2048 * 2 + rows * cols * 3,
+    )
+
+
+def fold_kernel(keep_ref, got_ref, out_ref, send_ref):
+    out_ref[...] = keep_ref[0] + got_ref[0].astype(F32)
+    send_ref[...] = (keep_ref[1] + got_ref[1].astype(F32)).astype(BF16)
+
+
+def fold(keep, got):
+    shape = keep.shape[1:]
+    return call(
+        fold_kernel, (keep, got), [VMEM, VMEM],
+        (jax.ShapeDtypeStruct(shape, F32), jax.ShapeDtypeStruct(shape, BF16)),
+        out_specs=(VMEM, VMEM), name="fold", flops=keep.size, moved=keep.size * 8,
+    )
+
+
+def close_kernel(stream_ref, gain_ref, *refs):
+    pieces = refs[:4]
+    out_ref = refs[4]
+    z = lax.axis_index("narrow")
+    part = pieces[0].shape[0]
+    gain = gain_ref[...].astype(F32)
+    for k in range(4):
+        at = pl.multiple_of(jnp.bitwise_and(z - k + 4, 3) * part, part)
+        rows = pl.ds(at, part)
+        out_ref[rows, :] = (stream_ref[rows, :].astype(F32) + pieces[k][...].astype(F32) * gain).astype(BF16)
+
+
+def close(stream, gain, pieces):
+    return call(
+        close_kernel, (stream, gain[None, :], *pieces), [VMEM] * 6,
+        jax.ShapeDtypeStruct(stream.shape, BF16),
+        out_specs=VMEM, name="close", flops=stream.size * 3, moved=stream.size * 6,
+    )
+
+
+def per_device_heads(
+    residual,
+    pre_gain,
+    query_weight,
+    key_weight,
+    value_weight,
+    output_weight,
+    adapter_down,
+    adapter_up_query,
+    adapter_up_key,
+    adapter_up_value,
+    adapter_down_out,
+    adapter_up_out,
+    post_gain,
+    sink_logits,
+    prompt_lengths,
+    prompt_adapters,
+):
+    tok, features = residual.shape
+    depth = features // CHIPS
+    own_rows = query_weight.shape[0]
+    prompts = prompt_lengths.shape[0]
+    d = HEAD_DIM
+    me = lax.axis_index("wide")
+    z = lax.axis_index("narrow")
+    core = me & 1
+    chip = me >> 1
+    wide = 2 * CHIPS
+    tokens = tok * wide
+
+    flip = lambda bits: [(i, i ^ bits) for i in range(wide)]
+    across = flip(1)
+    first_leg = [(i, i ^ (2 if i % 2 == 0 else 4)) for i in range(wide)]
+    second_leg = [(i, i ^ (4 if i % 2 == 0 else 2)) for i in range(wide)]
+    shift = lambda k: [(i, (i + k) % 4) for i in range(4)]
+    to_next = [(i, NEXT[i]) for i in range(4)]
+    to_second = [(i, 3 - i) for i in range(4)]
+    to_before = [(i, BEFORE[i]) for i in range(4)]
+    zflip = lambda bits: [(i, i ^ bits) for i in range(4)]
+
+    _, _, position = token_layout(prompt_lengths, tokens, jnp.int32(0))
+    half = d // 2
+    exponent = jnp.arange(half, dtype=F32) * (2.0 / d)
+    frequency = jnp.power(jnp.float32(rotary_base), -exponent)
+    angle = position.astype(F32)[:, None] * frequency[None, :]
+    cosine, sine = jnp.cos(angle), jnp.sin(angle)
+    cosine = jnp.concatenate([cosine, cosine], axis=1)
+    sine = jnp.concatenate([-sine, sine], axis=1)
+
+    pack = pick(prompt_adapters, adapter_down.T, adapter_up_out, ())
+    cut = norm(residual, pre_gain, 4, (pack,))
+    pieces = [cut[0]] + [lax.ppermute(cut[delta], "wide", flip(2 * delta)) for delta in (1, 2, 3)]
+    pack = merge(pack, lax.ppermute(pack, "narrow", zflip(1)), cut)
+    w_mine, w_theirs = arrange(
+        query_weight, key_weight, value_weight, output_weight.T, (pack, pieces[1])
+    )
+    up, out_down = ups(
+        prompt_adapters, adapter_up_query, adapter_up_key, adapter_up_value, adapter_down_out, (w_mine,)
+    )
+    w, ring0 = stack(w_mine, lax.ppermute(w_theirs, "wide", across), out_down, (up,))
+    pack = merge(pack, lax.ppermute(pack, "narrow", zflip(2)), (w, cosine, sine))
+    pack = join(pack, lax.ppermute(pack, "wide", across))
+    ring1 = lax.ppermute(ring0, "narrow", to_next)
+
+    tables = (cosine, sine)
+    part = tok // 4
+    sends, keeps, ones, twos, mine, other = [], [], [], [], [], []
+
+    def product(chunk, after, carry=()):
+        send, keep, carried = project(prompt_lengths, pieces, w, pack, up, chunk, after, carry)
+        sends.append(send)
+        keeps.append(keep)
+        ones.append(lax.ppermute(send, "wide", first_leg))
+        return carried
+
+    def pass_on(chunk, after, carry=()):
+        out, carried = onward(keeps[chunk], ones[chunk], after, carry)
+        twos.append(lax.ppermute(out, "wide", second_leg))
+        return (out, *carried)
+
+    def rotate_chunk(chunk, after):
+        own, send = finish(keeps[chunk], ones[chunk], twos[chunk], tables, chunk, after)
+        mine.append(own)
+        other.append(lax.ppermute(send, "wide", across))
+        return own
+
+    def attend_chunk(chunk, after, before=(), carry=()):
+        return attend(prompt_lengths, sink_logits, mine, other, chunk, after, before, carry)
+
+    def gather_group(sub, after):
+        near0 = beside(
+            (
+                sub[0],
+                lax.ppermute(sub[1], "narrow", to_next),
+                lax.ppermute(sub[2], "narrow", to_second),
+                sub[3],
+            ),
+            after,
+        )
+        near1 = lax.ppermute(near0, "wide", first_leg)
+        near2 = lax.ppermute(near0, "wide", second_leg)
+        near3 = lax.ppermute(near1, "wide", second_leg)
+        return near0, near1, near2, near3
+
+    product(0, (cosine, sine))
+    product(1, (sends[0],))
+    (out0,) = pass_on(0, (sends[1],))
+    product(2, (out0,))
+    (out1,) = pass_on(1, (sends[2],))
+    q0 = rotate_chunk(0, (out1,))
+    product(3, (q0,))
+    out2, ring1 = pass_on(2, (sends[3],), (ring1,))
+    ring2 = lax.ppermute(ring1, "narrow", to_next)
+    q1 = rotate_chunk(1, (out2,))
+    sub0, _ = attend_chunk(0, (q1,))
+    (out3,) = pass_on(3, (sub0[0],))
+    q2 = rotate_chunk(2, (out3,))
+    sub1, _ = attend_chunk(1, (q2,), sub0)
+    q3 = rotate_chunk(3, (sub1[0],))
+    sub2, _ = attend_chunk(2, (q3,))
+    sub3, _ = attend_chunk(3, (sub2[0],), sub2)
+    out_weights = (ring0, ring1, ring2)
+    halves = []
+    before = sub3[0]
+    for group, sub in enumerate((sub1, sub3)):
+        keep, send = output(
+            prompt_lengths, gather_group(sub, (sub3[0],)), out_weights, pack, group, part, (before,)
+        )
+        main, extra = fold(keep, lax.ppermute(send, "wide", across))
+        halves.append(merge(main, lax.ppermute(extra, "narrow", to_before)))
+        before = keep
+    total = jnp.concatenate(halves)
+    rows_of = lambda to: lax.dynamic_index_in_dim(total, to, 0, keepdims=False)
+    full = [rows_of(chip)] + [
+        lax.ppermute(rows_of(chip ^ delta), "wide", flip(2 * delta)) for delta in (1, 2, 3)
+    ]
+    full = jnp.stack(full)
+    wide_rows = full.astype(F32)
+    mean_square = jnp.sum(wide_rows * wide_rows, axis=(0, 2)) / features
+    scaled = (wide_rows * lax.rsqrt(mean_square + epsilon)[None, :, None]).astype(BF16)
+    finals = []
+    for k in range(4):
+        piece = lax.dynamic_index_in_dim(scaled, chip ^ ((z + k) & 3), 0, keepdims=False)
+        finals.append(piece if k == 0 else lax.ppermute(piece, "narrow", shift(k)))
+    own_width = post_gain.shape[0]
+    own_stream = lax.dynamic_slice_in_dim(residual, z * own_width, own_width, 1)
+    return close(own_stream, post_gain, finals)
 def rotate(values, position):
     half = values.shape[-1] // 2
     exponent = jnp.arange(half, dtype=jnp.float32) * (2.0 / values.shape[-1])
@@ -174,9 +887,13 @@
     return mixed.astype(jnp.bfloat16)
 
 
+def fits(mesh):
+    return mesh.shape["wide"] == 2 * CHIPS and mesh.shape["narrow"] == 4
+
+
 def solution(mesh):
     return jax.shard_map(
-        per_device,
+        per_device_heads if fits(mesh) else per_device,
         mesh=mesh,
         in_specs=(
             P("wide", None),

time: 455 us -> 184 us (0.40)
  waiting for transfers between devices: 335 us -> 67.6 us
  starting transfers between devices: 0.72 us -> 55.4 us
  Pallas kernels: 0 us -> 47.9 us
  matrix products: 46.3 us -> 0 us
  other arithmetic: 27.4 us -> 5.33 us
  blocking collectives: 14.7 us -> 0 us
  between operations: 13.5 us -> 0.46 us
  local copies, waits for them, and re-layouts: 17 us -> 6.41 us
    all_gather x7 -> x0, waiting for transfers between devices: 211 us -> none  [the longest x1 52.3 us: per_device(): lax.all_gather(query_weight, 'wide', axis=0, tiled=True)]
    psum x2 -> x0, waiting for transfers between devices: 121 us -> none  [the longest x1 92.7 us: per_device(): lax.psum(partial_out.astype(jnp.bfloat16), 'narrow').astype(jnp.float32)]
    ppermute x0 -> x41, waiting for transfers between devices: none -> 67.6 us  [the longest x2 12.4 us: per_device_heads(): halves.append(merge(main, lax.ppermute(extra, 'narrow', to_before)))]
    ppermute x0 -> x41, starting transfers between devices: none -> 55.4 us  [the longest x2 6.98 us: gather_group(): lax.ppermute(sub[2], 'narrow', to_second)]
    pallas_call x0 -> x33, Pallas kernels: none -> 47.9 us  [call(): pl.pallas_call(lambda *refs: kernel(*refs[n:]), out_shape=out_shape, in_s...]
    dot_general x12 -> x0, matrix products: 46.3 us -> none  [the longest x4 15.4 us: per_device(): jnp.dot(normed, piece, preferred_element_type=jnp.float32)]
    all_gather x1 -> x0, blocking collectives: 14.7 us -> none  [per_device(): lax.all_gather(code_part.astype(jnp.bfloat16), 'narrow', axis=1, tiled=True)]
    convert_element_type x8 -> x2, other arithmetic: 12 us -> 0.21 us  [the longest x1 0.2 us: per_device_heads(): (wide_rows * lax.rsqrt(mean_square + epsilon)[None, :, None]).astype(BF16)]
  transfers between devices with their start and end apart: 9 -> 41, of which waited for: 9 -> 22; matrix products, arithmetic and copies ran while one was open for 16% -> 3% of each run, Pallas kernels for 0% -> 21%
where the time goes in v2:
time: 184 us; the launch traced here: 183 us
  waiting for transfers between devices  67.6 us (37%)
  starting transfers between devices  55.4 us (30%)
  Pallas kernels  47.9 us (26%)
  local copies, waits for them, and re-layouts  6.41 us (3%)
  other arithmetic  5.33 us (3%)
    pallas_call x33, Pallas kernels, call(): pl.pallas_call(lambda *refs: kernel(*refs[n:]), out_shape=out_shape, in_s...  47.9 us
    ppermute x2, waiting for transfers between devices, per_device_heads(): halves.append(merge(main, lax.ppermute(extra, 'narrow', to_before)))  12.4 us
    ppermute x1, waiting for transfers between devices, per_device_heads(): pack = merge(pack, lax.ppermute(pack, 'narrow', zflip(1)), cut)  7.59 us
    ppermute x3, waiting for transfers between devices, per_device_heads(): lax.ppermute(cut[delta], 'wide', flip(2 * delta))  7.57 us
    ppermute x2, starting transfers between devices, gather_group(): lax.ppermute(sub[2], 'narrow', to_second)  6.98 us
    ppermute x1, waiting for transfers between devices, per_device_heads(): lax.ppermute(pack, 'narrow', zflip(2))  6.82 us
    ppermute x3, starting transfers between devices, per_device_heads(): lax.ppermute(cut[delta], 'wide', flip(2 * delta))  6.27 us
    ppermute x4, starting transfers between devices, product(): ones.append(lax.ppermute(send, 'wide', first_leg))  6.22 us
  transfers between devices with their start and end apart: 41, of which 22 were waited for; matrix products, arithmetic and copies ran while one was open for 3% of the time, Pallas kernels for 21%

profile of v2, /device:TPU:0, one launch (start us, length us, event | category | flops | bytes accessed | tf_op | source)
XLA Modules:
  0.0 183.1 jit_solution(1664694440800708749)
XLA Ops:
  1.3 2.6 %pick.1.refs_0_.refs_4_ = bf16[256,576]{1,0:T(8,128)(2,1)} custom-call(s32[4]{0:T(128)} %refs_1_.12, bf16[192,576]{1,0:T(8,128)(2,1)} %bitcast.30, bf16[256,1152]{1,0:T(8,128)(2,1)} %refs_2_.8), custom_call_target="tpu_custom_call" | custom-call | flops 691200 | bytes 10368 | tf_op jit(solution)/shard_map/pick/pallas_call | solution.py:44
  3.9 4.7 %norm.1 = (bf16[256,1152]{1,0:T(8,128)(2,1)}, bf16[256,1152]{1,0:T(8,128)(2,1)}, bf16[256,1152]{1,0:T(8,128)(2,1)}, bf16[256,1152]{1,0:T(8,128)(2,1)}) custom-call(bf16[256,576]{1,0:T(8,128)(2,1)} %pick.1.refs_0_.refs_4_, bf16[256,4608]{1,0:T(8,128)(2,1)} %refs_1_.11, bf16[1,4608]{1,0:T(2,128)(2,1)} %broadcast_in_dim.5.refs_2_), custom_call_target="tpu_custom_call" | custom-call | flops 73728 | bytes 73728 | tf_op jit(solution)/shard_map/norm/pallas_call | solution.py:44
  8.7 3.0 %collective-permute-start = (bf16[256,1152]{1,0:T(8,128)(2,1)}, bf16[256,1152]{1,0:T(8,128)(2,1)S(1)}, u32[]{:S(2)}, u32[]{:S(2)}) collective-permute-start(bf16[256,1152]{1,0:T(8,128)(2,1)} %get-tuple-element.58.refs_1_), channel_id=1, source_target_pairs={{0,8},{4,12},{8,0},{12,4},{16,24},{20,28},{24,16},{28,20},{1,9},{5... | collective-permute-start | bytes 1769480 | tf_op jit(solution)/shard_map/ppermute | solution.py:646
  13.2 7.6 %collective-permute-done.3.refs_5_ = bf16[256,576]{1,0:T(8,128)(2,1)S(1)} collective-permute-done((bf16[256,576]{1,0:T(8,128)(2,1)S(1)}, bf16[256,576]{1,0:T(8,128)(2,1)S(1)}, u32[]{:S(2)}, u32[]{:S(2)}) %collective-permute-start.3) | collective-permute-done | bytes 294944 | tf_op jit(solution)/shard_map/ppermute | solution.py:647
  31.9 2.7 %collective-permute-start.5 = (bf16[256,576]{1,0:T(8,128)(2,1)}, bf16[256,576]{1,0:T(8,128)(2,1)S(1)}, u32[]{:S(2)}, u32[]{:S(2)}) collective-permute-start(bf16[256,576]{1,0:T(8,128)(2,1)} %copy-done.3), channel_id=1, source_target_pairs={{0,2},{1,3},{2,0},{3,1},{4,6},{5,7},{6,4},{7,5},{8,10},{9,11},{10,... | collective-permute-start | bytes 884744 | tf_op jit(solution)/shard_map/ppermute | solution.py:655
  34.6 3.7 %fusion.2 = (f32[2048,64]{1,0:T(8,128)S(1)}, f32[2048,64]{1,0:T(8,128)S(1)}, f32[2048,64]{1,0:T(8,128)S(1)}) fusion(f32[64]{0:T(128)S(1)} %negate_power_fusion, f32[2048]{0:T(1024)S(1)} %subtract_convert_fusion), kind=kLoop, calls=%fused_computation.17 | loop fusion | flops 262144 | bytes 1581312 | tf_op jit(solution)/shard_map/neg | solution.py:642
  42.8 6.8 %collective-permute-done.5.refs_4_ = bf16[256,576]{1,0:T(8,128)(2,1)S(1)} collective-permute-done((bf16[256,576]{1,0:T(8,128)(2,1)}, bf16[256,576]{1,0:T(8,128)(2,1)S(1)}, u32[]{:S(2)}, u32[]{:S(2)}) %collective-permute-start.5) | collective-permute-done | bytes 294944 | tf_op jit(solution)/shard_map/ppermute | solution.py:655
  51.6 5.4 %collective-permute-done.1.refs_5_.refs_4_ = bf16[256,1152]{1,0:T(8,128)(2,1)} collective-permute-done((bf16[256,1152]{1,0:T(8,128)(2,1)}, bf16[256,1152]{1,0:T(8,128)(2,1)}, u32[]{:S(2)}, u32[]{:S(2)}) %collective-permute-start.1) | collective-permute-done | bytes 589856 | tf_op jit(solution)/shard_map/ppermute | solution.py:646
  57.0 2.8 %project.4 = (bf16[256,1024]{1,0:T(8,128)(2,1)S(1)}, f32[256,1024]{1,0:T(8,128)S(1)}) custom-call(f32[2048,128]{1,0:T(8,128)S(1)} %get-tuple-element.120.refs_1_.refs_0_.refs_4_, f32[2048,128]{1,0:T(8,128)S(1)} %get-tuple-element.121.refs_2_.refs_1_.refs_5_, s32[4]{0:T(128)S(1)} %copy-done.14, bf16[256,1152]{1,0:T(8,128)(2,1)S(1)} %copy-done.1, ...), custom_call_target="tpu_custom_call" | custom-call | flops 18874368 | bytes 107520 | tf_op jit(solution)/shard_map/project/pallas_call | solution.py:44
  61.6 2.8 %project.5 = (bf16[256,1024]{1,0:T(8,128)(2,1)S(1)}, f32[256,1024]{1,0:T(8,128)S(1)}) custom-call(bf16[256,1024]{1,0:T(8,128)(2,1)S(1)} %get-tuple-element.66.refs_0_, s32[4]{0:T(128)S(1)} %copy-done.14, bf16[256,1152]{1,0:T(8,128)(2,1)S(1)} %copy-done.1, bf16[256,1152]{1,0:T(8,128)(2,1)S(1)} %collective-permute-done.refs_1_.refs_4_.refs_3_, ...), custom_call_target="tpu_custom_call" | custom-call | flops 18874368 | bytes 107520 | tf_op jit(solution)/shard_map/project/pallas_call | solution.py:44
  64.8 4.3 %collective-permute-done.7.refs_2_ = bf16[256,1024]{1,0:T(8,128)(2,1)S(1)} collective-permute-done((bf16[256,1024]{1,0:T(8,128)(2,1)S(1)}, bf16[256,1024]{1,0:T(8,128)(2,1)S(1)}, u32[]{:S(2)}, u32[]{:S(2)}) %collective-permute-start.7) | collective-permute-done | bytes 524320 | tf_op jit(solution)/shard_map/ppermute | solution.py:667
  69.1 2.8 %collective-permute-start.9 = (bf16[256,512]{1,0:T(8,128)(2,1)S(1)}, bf16[256,512]{1,0:T(8,128)(2,1)S(1)}, u32[]{:S(2)}, u32[]{:S(2)}) collective-permute-start(bf16[256,512]{1,0:T(8,128)(2,1)S(1)} %onward.4.refs_0_), channel_id=1, source_target_pairs={{0,16},{4,12},{8,24},{12,4},{16,0},{20,28},{24,8},{28,20},{1,17},{... | collective-permute-start | bytes 786440 | tf_op jit(solution)/shard_map/ppermute | solution.py:672
  71.9 3.9 %project.6 = (bf16[256,1024]{1,0:T(8,128)(2,1)S(1)}, f32[256,1024]{1,0:T(8,128)S(1)}) custom-call(bf16[256,512]{1,0:T(8,128)(2,1)S(1)} %onward.4.refs_0_, s32[4]{0:T(128)S(1)} %copy-done.14, bf16[256,1152]{1,0:T(8,128)(2,1)S(1)} %copy-done.1, bf16[256,1152]{1,0:T(8,128)(2,1)S(1)} %collective-permute-done.refs_1_.refs_4_.refs_3_, ...), custom_call_target="tpu_custom_call" | custom-call | flops 18874368 | bytes 107520 | tf_op jit(solution)/shard_map/project/pallas_call | solution.py:44
  77.9 3.7 %project.7 = (bf16[256,1024]{1,0:T(8,128)(2,1)S(1)}, f32[256,1024]{1,0:T(8,128)S(1)}) custom-call(bf16[256,384]{1,0:T(8,128)(2,1)S(1)} %get-tuple-element.71.refs_0_.refs_3_, s32[4]{0:T(128)S(1)} %copy-done.14, bf16[256,1152]{1,0:T(8,128)(2,1)S(1)} %copy-done.1, bf16[256,1152]{1,0:T(8,128)(2,1)S(1)} %collective-permute-done.refs_1_.refs_4_.refs_3_, ...), custom_call_target="tpu_custom_call" | custom-call | flops 18874368 | bytes 107520 | tf_op jit(solution)/shard_map/project/pallas_call | solution.py:44
  81.7 2.5 %collective-permute-start.14 = (bf16[256,1024]{1,0:T(8,128)(2,1)S(1)}, bf16[256,1024]{1,0:T(8,128)(2,1)S(1)}, u32[]{:S(2)}, u32[]{:S(2)}) collective-permute-start(bf16[256,1024]{1,0:T(8,128)(2,1)S(1)} %get-tuple-element.72.refs_0_), channel_id=1, source_target_pairs={{0,8},{4,20},{8,0},{12,28},{16,24},{20,4},{24,16},{28,12},{1,9},{5... | collective-permute-start | bytes 1572872 | tf_op jit(solution)/shard_map/ppermute | solution.py:667
  87.9 4.5 %collective-permute-done.12.refs_3_ = bf16[256,512]{1,0:T(8,128)(2,1)S(1)} collective-permute-done((bf16[256,512]{1,0:T(8,128)(2,1)S(1)}, bf16[256,512]{1,0:T(8,128)(2,1)S(1)}, u32[]{:S(2)}, u32[]{:S(2)}) %collective-permute-start.12) | collective-permute-done | bytes 262176 | tf_op jit(solution)/shard_map/ppermute | solution.py:672
  99.0 2.7 %attend.5 = (bf16[256,128]{1,0:T(8,128)(2,1)S(1)}, bf16[256,128]{1,0:T(8,128)(2,1)S(1)}, bf16[256,128]{1,0:T(8,128)(2,1)S(1)}, bf16[256,128]{1,0:T(8,128)(2,1)S(1)}) custom-call(bf16[256,384]{1,0:T(8,128)(2,1)S(1)} %get-tuple-element.80.refs_0_.refs_5_, s32[4]{0:T(128)S(1)} %copy-done.14, f32[8]{0:T(128)S(1)} %copy-done.15, ...), custom_call_target="tpu_custom_call" | custom-call | flops 3145728 | bytes 8192 | tf_op jit(solution)/shard_map/attend/pallas_call | solution.py:44
  103.8 4.1 %collective-permute-start.21 = (bf16[256,128]{1,0:T(8,128)(2,1)S(1)}, bf16[256,128]{1,0:T(8,128)(2,1)S(1)}, u32[]{:S(2)}, u32[]{:S(2)}) collective-permute-start(bf16[256,128]{1,0:T(8,128)(2,1)S(1)} %get-tuple-element.95), channel_id=1, source_target_pairs={{0,3},{1,2},{2,1},{3,0},{4,7},{5,6},{6,5},{7,4},{8,11},{9,10},{10,... | collective-permute-start | bytes 196616 | tf_op jit(solution)/shard_map/ppermute | solution.py:689
  107.9 4.1 %attend.6 = (bf16[128,128]{1,0:T(8,128)(2,1)S(1)}, bf16[128,128]{1,0:T(8,128)(2,1)S(1)}, bf16[128,128]{1,0:T(8,128)(2,1)S(1)}, bf16[128,128]{1,0:T(8,128)(2,1)S(1)}) custom-call(bf16[256,384]{1,0:T(8,128)(2,1)S(1)} %get-tuple-element.86.refs_0_.refs_6_, s32[4]{0:T(128)S(1)} %copy-done.14, f32[8]{0:T(128)S(1)} %copy-done.15, ...), custom_call_target="tpu_custom_call" | custom-call | flops 3145728 | bytes 12288 | tf_op jit(solution)/shard_map/attend/pallas_call | solution.py:44
  112.0 4.2 %attend.7 = (bf16[256,128]{1,0:T(8,128)(2,1)S(1)}, bf16[256,128]{1,0:T(8,128)(2,1)S(1)}, bf16[256,128]{1,0:T(8,128)(2,1)S(1)}, bf16[256,128]{1,0:T(8,128)(2,1)S(1)}) custom-call(bf16[128,128]{1,0:T(8,128)(2,1)S(1)} %get-tuple-element.88.refs_0_.refs_11_, s32[4]{0:T(128)S(1)} %copy-done.14, f32[8]{0:T(128)S(1)} %copy-done.15, ...), custom_call_target="tpu_custom_call" | custom-call | flops 3145728 | bytes 16384 | tf_op jit(solution)/shard_map/attend/pallas_call | solution.py:44
  116.6 2.9 %collective-permute-start.29 = (bf16[256,128]{1,0:T(8,128)(2,1)S(1)}, bf16[256,128]{1,0:T(8,128)(2,1)S(1)}, u32[]{:S(2)}, u32[]{:S(2)}) collective-permute-start(bf16[256,128]{1,0:T(8,128)(2,1)S(1)} %get-tuple-element.103), channel_id=1, source_target_pairs={{0,3},{1,2},{2,1},{3,0},{4,7},{5,6},{6,5},{7,4},{8,11},{9,10},{10,... | collective-permute-start | bytes 196616 | tf_op jit(solution)/shard_map/ppermute | solution.py:689
  126.4 2.3 %collective-permute-start.24 = (bf16[256,512]{1,0:T(8,128)(2,1)S(1)}, bf16[256,512]{1,0:T(8,128)(2,1)S(1)}, u32[]{:S(2)}, u32[]{:S(2)}) collective-permute-start(bf16[256,512]{1,0:T(8,128)(2,1)S(1)} %collective-permute-done.22.refs_3_), channel_id=1, source_target_pairs={{0,16},{4,12},{8,24},{12,4},{16,0},{20,28},{24,8},{28,20},{1,17},{... | collective-permute-start | bytes 786440 | tf_op jit(solution)/shard_map/ppermute | solution.py:696
  128.8 3.9 %collective-permute-done.30.refs_3_ = bf16[256,512]{1,0:T(8,128)(2,1)S(1)} collective-permute-done((bf16[256,512]{1,0:T(8,128)(2,1)S(1)}, bf16[256,512]{1,0:T(8,128)(2,1)S(1)}, u32[]{:S(2)}, u32[]{:S(2)}) %collective-permute-start.30) | collective-permute-done | bytes 262176 | tf_op jit(solution)/shard_map/ppermute | solution.py:694
  134.4 3.2 %output.2 = (f32[2,2,64,1152]{3,2,1,0:T(8,128)S(1)}, bf16[2,2,64,1152]{3,2,1,0:T(8,128)(2,1)S(1)}) custom-call(bf16[256,128]{1,0:T(8,128)(2,1)S(1)} %get-tuple-element.93.refs_0_.refs_1_, s32[4]{0:T(128)S(1)} %copy-done.14, bf16[256,512]{1,0:T(8,128)(2,1)S(1)} %beside.2.refs_2_, bf16[256,512]{1,0:T(8,128)(2,1)S(1)} %collective-permute-done.22.refs_3_, ...), custom_call_target="tpu_custom_call" | custom-call | flops 18874368 | bytes 103936 | tf_op jit(solution)/shard_map/output/pallas_call | solution.py:44
  139.7 3.2 %output.3 = (f32[2,2,64,1152]{3,2,1,0:T(8,128)S(1)}, bf16[2,2,64,1152]{3,2,1,0:T(8,128)(2,1)S(1)}) custom-call(f32[2,2,64,1152]{3,2,1,0:T(8,128)S(1)} %get-tuple-element.98.refs_0_, s32[4]{0:T(128)S(1)} %copy-done.14, bf16[256,512]{1,0:T(8,128)(2,1)S(1)} %beside.3.refs_2_, bf16[256,512]{1,0:T(8,128)(2,1)S(1)} %collective-permute-done.30.refs_3_, ...), custom_call_target="tpu_custom_call" | custom-call | flops 18874368 | bytes 103936 | tf_op jit(solution)/shard_map/output/pallas_call | solution.py:44
  146.5 6.7 %collective-permute-done.27.refs_1_ = bf16[2,64,1152]{2,1,0:T(8,128)(2,1)S(1)} collective-permute-done((bf16[2,64,1152]{2,1,0:T(8,128)(2,1)S(1)}, bf16[2,64,1152]{2,1,0:T(8,128)(2,1)S(1)}, u32[]{:S(2)}, u32[]{:S(2)}) %collective-permute-start.27) | collective-permute-done | bytes 294944 | tf_op jit(solution)/shard_map/ppermute | solution.py:724
  153.2 5.7 %collective-permute-done.34.refs_1_ = bf16[2,64,1152]{2,1,0:T(8,128)(2,1)S(1)} collective-permute-done((bf16[2,64,1152]{2,1,0:T(8,128)(2,1)S(1)}, bf16[2,64,1152]{2,1,0:T(8,128)(2,1)S(1)}, u32[]{:S(2)}, u32[]{:S(2)}) %collective-permute-start.34) | collective-permute-done | bytes 294944 | tf_op jit(solution)/shard_map/ppermute | solution.py:724
  162.8 3.1 %collective-permute-done.35 = bf16[64,1152]{1,0:T(8,128)(2,1)S(1)} collective-permute-done((bf16[64,1152]{1,0:T(8,128)(2,1)S(1)}, bf16[64,1152]{1,0:T(8,128)(2,1)S(1)}, u32[]{:S(2)}, u32[]{:S(2)}) %collective-permute-start.35) | collective-permute-done | bytes 147488 | tf_op jit(solution)/shard_map/ppermute | solution.py:729
  165.9 2.7 %collective-permute-done.36 = bf16[64,1152]{1,0:T(8,128)(2,1)S(1)} collective-permute-done((bf16[64,1152]{1,0:T(8,128)(2,1)S(1)}, bf16[64,1152]{1,0:T(8,128)(2,1)S(1)}, u32[]{:S(2)}, u32[]{:S(2)}) %collective-permute-start.36) | collective-permute-done | bytes 147488 | tf_op jit(solution)/shard_map/ppermute | solution.py:729
  169.2 2.4 %collective-permute-start.38 = (bf16[64,1152]{1,0:T(8,128)(2,1)S(1)}, bf16[64,1152]{1,0:T(8,128)(2,1)S(1)}, u32[]{:S(2)}, u32[]{:S(2)}) collective-permute-start(bf16[64,1152]{1,0:T(8,128)(2,1)S(1)} %get-tuple-element.111), channel_id=1, source_target_pairs={{0,1},{1,2},{2,3},{3,0},{4,5},{5,6},{6,7},{7,4},{8,9},{9,10},{10,1... | collective-permute-start | bytes 442376 | tf_op jit(solution)/shard_map/ppermute | solution.py:738
  172.4 2.8 %collective-permute-start.40 = (bf16[64,1152]{1,0:T(8,128)(2,1)S(1)}, bf16[64,1152]{1,0:T(8,128)(2,1)S(1)}, u32[]{:S(2)}, u32[]{:S(2)}) collective-permute-start(bf16[64,1152]{1,0:T(8,128)(2,1)S(1)} %get-tuple-element.109), channel_id=1, source_target_pairs={{0,3},{1,0},{2,1},{3,2},{4,7},{5,4},{6,5},{7,6},{8,11},{9,8},{10,9... | collective-permute-start | bytes 442376 | tf_op jit(solution)/shard_map/ppermute | solution.py:738
  177.9 4.2 %collective-permute-done.39.refs_4_ = bf16[64,1152]{1,0:T(8,128)(2,1)S(1)} collective-permute-done((bf16[64,1152]{1,0:T(8,128)(2,1)S(1)}, bf16[64,1152]{1,0:T(8,128)(2,1)S(1)}, u32[]{:S(2)}, u32[]{:S(2)}) %collective-permute-start.39) | collective-permute-done | bytes 147488 | tf_op jit(solution)/shard_map/ppermute | solution.py:738
  (134 shorter events, 60.6 us)
Async XLA Ops:
  8.7 16.5 %collective-permute-start = (bf16[256,1152]{1,0:T(8,128)(2,1)}, bf16[256,1152]{1,0:T(8,128)(2,1)S(1)}, u32[]{:S(2)}, u32[]{:S(2)}) collective-permute-start(bf16[256,1152]{1,0:T(8,128)(2,1)} %get-tuple-element.58.refs_1_), channel_id=1, source_target_pairs={{0,8},{4,12},{8,0},{12,4},{16,24},{20,28},{24,16},{28,20},{1,9},{5... | collective-permute-start | bytes 1769480 | tf_op jit(solution)/shard_map/ppermute | solution.py:646
  11.7 9.2 %collective-permute-start.3 = (bf16[256,576]{1,0:T(8,128)(2,1)S(1)}, bf16[256,576]{1,0:T(8,128)(2,1)S(1)}, u32[]{:S(2)}, u32[]{:S(2)}) collective-permute-start(bf16[256,576]{1,0:T(8,128)(2,1)S(1)} %copy-done.2), channel_id=1, source_target_pairs={{0,1},{1,0},{2,3},{3,2},{4,5},{5,4},{6,7},{7,6},{8,9},{9,8},{10,11... | collective-permute-start | bytes 884744 | tf_op jit(solution)/shard_map/ppermute | solution.py:647
  28.2 12.2 %collective-permute-start.4 = (bf16[576,2560]{1,0:T(8,128)(2,1)}, bf16[576,2560]{1,0:T(8,128)(2,1)}, u32[]{:S(2)}, u32[]{:S(2)}) collective-permute-start(bf16[576,2560]{1,0:T(8,128)(2,1)} %get-tuple-element.63), channel_id=1, source_target_pairs={{0,4},{4,0},{8,12},{12,8},{16,20},{20,16},{24,28},{28,24},{1,5},{5... | collective-permute-start | bytes 8847368 | tf_op jit(solution)/shard_map/ppermute | solution.py:654
  28.3 28.7 %collective-permute-start.1 = (bf16[256,1152]{1,0:T(8,128)(2,1)}, bf16[256,1152]{1,0:T(8,128)(2,1)}, u32[]{:S(2)}, u32[]{:S(2)}) collective-permute-start(bf16[256,1152]{1,0:T(8,128)(2,1)} %get-tuple-element.59.refs_2_), channel_id=1, source_target_pairs={{0,16},{4,20},{8,24},{12,28},{16,0},{20,4},{24,8},{28,12},{1,17},{... | collective-permute-start | bytes 1769480 | tf_op jit(solution)/shard_map/ppermute | solution.py:646
  30.2 26.9 %collective-permute-start.2 = (bf16[256,1152]{1,0:T(8,128)(2,1)}, bf16[256,1152]{1,0:T(8,128)(2,1)}, u32[]{:S(2)}, u32[]{:S(2)}) collective-permute-start(bf16[256,1152]{1,0:T(8,128)(2,1)} %get-tuple-element.60.refs_3_), channel_id=1, source_target_pairs={{0,24},{4,28},{8,16},{12,20},{16,8},{20,12},{24,0},{28,4},{1,25},{... | collective-permute-start | bytes 1769480 | tf_op jit(solution)/shard_map/ppermute | solution.py:646
  31.9 17.7 %collective-permute-start.5 = (bf16[256,576]{1,0:T(8,128)(2,1)}, bf16[256,576]{1,0:T(8,128)(2,1)S(1)}, u32[]{:S(2)}, u32[]{:S(2)}) collective-permute-start(bf16[256,576]{1,0:T(8,128)(2,1)} %copy-done.3), channel_id=1, source_target_pairs={{0,2},{1,3},{2,0},{3,1},{4,6},{5,7},{6,4},{7,5},{8,10},{9,11},{10,... | collective-permute-start | bytes 884744 | tf_op jit(solution)/shard_map/ppermute | solution.py:655
  49.8 35.9 %collective-permute-start.11 = (bf16[1216,512]{1,0:T(8,128)(2,1)S(1)}, bf16[1216,512]{1,0:T(8,128)(2,1)S(1)}, u32[]{:S(2)}, u32[]{:S(2)}) collective-permute-start(bf16[1216,512]{1,0:T(8,128)(2,1)S(1)} %get-tuple-element.74.refs_6_), channel_id=1, source_target_pairs={{0,1},{1,3},{2,0},{3,2},{4,5},{5,7},{6,4},{7,6},{8,9},{9,11},{10,8... | collective-permute-start | bytes 3735560 | tf_op jit(solution)/shard_map/ppermute | solution.py:657
  59.8 9.2 %collective-permute-start.7 = (bf16[256,1024]{1,0:T(8,128)(2,1)S(1)}, bf16[256,1024]{1,0:T(8,128)(2,1)S(1)}, u32[]{:S(2)}, u32[]{:S(2)}) collective-permute-start(bf16[256,1024]{1,0:T(8,128)(2,1)S(1)} %get-tuple-element.66.refs_0_), channel_id=1, source_target_pairs={{0,8},{4,20},{8,0},{12,28},{16,24},{20,4},{24,16},{28,12},{1,9},{5... | collective-permute-start | bytes 1572872 | tf_op jit(solution)/shard_map/ppermute | solution.py:667
  64.4 13.1 %collective-permute-start.8 = (bf16[256,1024]{1,0:T(8,128)(2,1)S(1)}, bf16[256,1024]{1,0:T(8,128)(2,1)S(1)}, u32[]{:S(2)}, u32[]{:S(2)}) collective-permute-start(bf16[256,1024]{1,0:T(8,128)(2,1)S(1)} %get-tuple-element.67.refs_0_), channel_id=1, source_target_pairs={{0,8},{4,20},{8,0},{12,28},{16,24},{20,4},{24,16},{28,12},{1,9},{5... | collective-permute-start | bytes 1572872 | tf_op jit(solution)/shard_map/ppermute | solution.py:667
  69.1 8.6 %collective-permute-start.9 = (bf16[256,512]{1,0:T(8,128)(2,1)S(1)}, bf16[256,512]{1,0:T(8,128)(2,1)S(1)}, u32[]{:S(2)}, u32[]{:S(2)}) collective-permute-start(bf16[256,512]{1,0:T(8,128)(2,1)S(1)} %onward.4.refs_0_), channel_id=1, source_target_pairs={{0,16},{4,12},{8,24},{12,4},{16,0},{20,28},{24,8},{28,20},{1,17},{... | collective-permute-start | bytes 786440 | tf_op jit(solution)/shard_map/ppermute | solution.py:672
  75.8 9.9 %collective-permute-start.10 = (bf16[256,1024]{1,0:T(8,128)(2,1)S(1)}, bf16[256,1024]{1,0:T(8,128)(2,1)S(1)}, u32[]{:S(2)}, u32[]{:S(2)}) collective-permute-start(bf16[256,1024]{1,0:T(8,128)(2,1)S(1)} %get-tuple-element.69.refs_0_), channel_id=1, source_target_pairs={{0,8},{4,20},{8,0},{12,28},{16,24},{20,4},{24,16},{28,12},{1,9},{5... | collective-permute-start | bytes 1572872 | tf_op jit(solution)/shard_map/ppermute | solution.py:667
  81.7 14.7 %collective-permute-start.14 = (bf16[256,1024]{1,0:T(8,128)(2,1)S(1)}, bf16[256,1024]{1,0:T(8,128)(2,1)S(1)}, u32[]{:S(2)}, u32[]{:S(2)}) collective-permute-start(bf16[256,1024]{1,0:T(8,128)(2,1)S(1)} %get-tuple-element.72.refs_0_), channel_id=1, source_target_pairs={{0,8},{4,20},{8,0},{12,28},{16,24},{20,4},{24,16},{28,12},{1,9},{5... | collective-permute-start | bytes 1572872 | tf_op jit(solution)/shard_map/ppermute | solution.py:667
  84.2 8.2 %collective-permute-start.12 = (bf16[256,512]{1,0:T(8,128)(2,1)S(1)}, bf16[256,512]{1,0:T(8,128)(2,1)S(1)}, u32[]{:S(2)}, u32[]{:S(2)}) collective-permute-start(bf16[256,512]{1,0:T(8,128)(2,1)S(1)} %onward.5.refs_0_), channel_id=1, source_target_pairs={{0,16},{4,12},{8,24},{12,4},{16,0},{20,28},{24,8},{28,20},{1,17},{... | collective-permute-start | bytes 786440 | tf_op jit(solution)/shard_map/ppermute | solution.py:672
  85.8 48.6 %collective-permute-start.25 = (bf16[1216,512]{1,0:T(8,128)(2,1)S(1)}, bf16[1216,512]{1,0:T(8,128)(2,1)S(1)}, u32[]{:S(2)}, u32[]{:S(2)}) collective-permute-start(bf16[1216,512]{1,0:T(8,128)(2,1)S(1)} %get-tuple-element.97.refs_7_), channel_id=1, source_target_pairs={{0,1},{1,3},{2,0},{3,2},{4,5},{5,7},{6,4},{7,6},{8,9},{9,11},{10,8... | collective-permute-start | bytes 3735560 | tf_op jit(solution)/shard_map/ppermute | solution.py:707
  87.4 10.2 %collective-permute-start.15 = (bf16[256,512]{1,0:T(8,128)(2,1)S(1)}, bf16[256,512]{1,0:T(8,128)(2,1)S(1)}, u32[]{:S(2)}, u32[]{:S(2)}) collective-permute-start(bf16[256,512]{1,0:T(8,128)(2,1)S(1)} %get-tuple-element.75.refs_0_), channel_id=1, source_target_pairs={{0,16},{4,12},{8,24},{12,4},{16,0},{20,28},{24,8},{28,20},{1,17},{... | collective-permute-start | bytes 786440 | tf_op jit(solution)/shard_map/ppermute | solution.py:672
  97.8 10.1 %collective-permute-start.18 = (bf16[256,384]{1,0:T(8,128)(2,1)S(1)}, bf16[256,384]{1,0:T(8,128)(2,1)S(1)}, u32[]{:S(2)}, u32[]{:S(2)}) collective-permute-start(bf16[256,384]{1,0:T(8,128)(2,1)S(1)} %get-tuple-element.87), channel_id=1, source_target_pairs={{0,4},{4,0},{8,12},{12,8},{16,20},{20,16},{24,28},{28,24},{1,5},{5... | collective-permute-start | bytes 589832 | tf_op jit(solution)/shard_map/ppermute | solution.py:678
  103.1 8.9 %collective-permute-start.19 = (bf16[256,384]{1,0:T(8,128)(2,1)S(1)}, bf16[256,384]{1,0:T(8,128)(2,1)S(1)}, u32[]{:S(2)}, u32[]{:S(2)}) collective-permute-start(bf16[256,384]{1,0:T(8,128)(2,1)S(1)} %get-tuple-element.89), channel_id=1, source_target_pairs={{0,4},{4,0},{8,12},{12,8},{16,20},{20,16},{24,28},{28,24},{1,5},{5... | collective-permute-start | bytes 589832 | tf_op jit(solution)/shard_map/ppermute | solution.py:678
  103.2 16.3 %collective-permute-start.20 = (bf16[256,128]{1,0:T(8,128)(2,1)S(1)}, bf16[256,128]{1,0:T(8,128)(2,1)S(1)}, u32[]{:S(2)}, u32[]{:S(2)}) collective-permute-start(bf16[256,128]{1,0:T(8,128)(2,1)S(1)} %get-tuple-element.94), channel_id=1, source_target_pairs={{0,1},{1,3},{2,0},{3,2},{4,5},{5,7},{6,4},{7,6},{8,9},{9,11},{10,8... | collective-permute-start | bytes 196616 | tf_op jit(solution)/shard_map/ppermute | solution.py:688
  103.8 15.7 %collective-permute-start.21 = (bf16[256,128]{1,0:T(8,128)(2,1)S(1)}, bf16[256,128]{1,0:T(8,128)(2,1)S(1)}, u32[]{:S(2)}, u32[]{:S(2)}) collective-permute-start(bf16[256,128]{1,0:T(8,128)(2,1)S(1)} %get-tuple-element.95), channel_id=1, source_target_pairs={{0,3},{1,2},{2,1},{3,0},{4,7},{5,6},{6,5},{7,4},{8,11},{9,10},{10,... | collective-permute-start | bytes 196616 | tf_op jit(solution)/shard_map/ppermute | solution.py:689
  116.2 7.2 %collective-permute-start.28 = (bf16[256,128]{1,0:T(8,128)(2,1)S(1)}, bf16[256,128]{1,0:T(8,128)(2,1)S(1)}, u32[]{:S(2)}, u32[]{:S(2)}) collective-permute-start(bf16[256,128]{1,0:T(8,128)(2,1)S(1)} %get-tuple-element.102), channel_id=1, source_target_pairs={{0,1},{1,3},{2,0},{3,2},{4,5},{5,7},{6,4},{7,6},{8,9},{9,11},{10,8... | collective-permute-start | bytes 196616 | tf_op jit(solution)/shard_map/ppermute | solution.py:688
  119.5 6.9 %collective-permute-start.22 = (bf16[256,512]{1,0:T(8,128)(2,1)S(1)}, bf16[256,512]{1,0:T(8,128)(2,1)S(1)}, u32[]{:S(2)}, u32[]{:S(2)}) collective-permute-start(bf16[256,512]{1,0:T(8,128)(2,1)S(1)} %beside.2.refs_2_), channel_id=1, source_target_pairs={{0,8},{4,20},{8,0},{12,28},{16,24},{20,4},{24,16},{28,12},{1,9},{5... | collective-permute-start | bytes 786440 | tf_op jit(solution)/shard_map/ppermute | solution.py:694
  123.4 9.3 %collective-permute-start.30 = (bf16[256,512]{1,0:T(8,128)(2,1)S(1)}, bf16[256,512]{1,0:T(8,128)(2,1)S(1)}, u32[]{:S(2)}, u32[]{:S(2)}) collective-permute-start(bf16[256,512]{1,0:T(8,128)(2,1)S(1)} %beside.3.refs_2_), channel_id=1, source_target_pairs={{0,8},{4,20},{8,0},{12,28},{16,24},{20,4},{24,16},{28,12},{1,9},{5... | collective-permute-start | bytes 786440 | tf_op jit(solution)/shard_map/ppermute | solution.py:694
  124.9 9.4 %collective-permute-start.23 = (bf16[256,512]{1,0:T(8,128)(2,1)S(1)}, bf16[256,512]{1,0:T(8,128)(2,1)S(1)}, u32[]{:S(2)}, u32[]{:S(2)}) collective-permute-start(bf16[256,512]{1,0:T(8,128)(2,1)S(1)} %beside.2.refs_2_), channel_id=1, source_target_pairs={{0,16},{4,12},{8,24},{12,4},{16,0},{20,28},{24,8},{28,20},{1,17},{... | collective-permute-start | bytes 786440 | tf_op jit(solution)/shard_map/ppermute | solution.py:695
  126.4 8.0 %collective-permute-start.24 = (bf16[256,512]{1,0:T(8,128)(2,1)S(1)}, bf16[256,512]{1,0:T(8,128)(2,1)S(1)}, u32[]{:S(2)}, u32[]{:S(2)}) collective-permute-start(bf16[256,512]{1,0:T(8,128)(2,1)S(1)} %collective-permute-done.22.refs_3_), channel_id=1, source_target_pairs={{0,16},{4,12},{8,24},{12,4},{16,0},{20,28},{24,8},{28,20},{1,17},{... | collective-permute-start | bytes 786440 | tf_op jit(solution)/shard_map/ppermute | solution.py:696
  128.7 9.1 %collective-permute-start.31 = (bf16[256,512]{1,0:T(8,128)(2,1)S(1)}, bf16[256,512]{1,0:T(8,128)(2,1)S(1)}, u32[]{:S(2)}, u32[]{:S(2)}) collective-permute-start(bf16[256,512]{1,0:T(8,128)(2,1)S(1)} %beside.3.refs_2_), channel_id=1, source_target_pairs={{0,16},{4,12},{8,24},{12,4},{16,0},{20,28},{24,8},{28,20},{1,17},{... | collective-permute-start | bytes 786440 | tf_op jit(solution)/shard_map/ppermute | solution.py:695
  132.7 7.1 %collective-permute-start.32 = (bf16[256,512]{1,0:T(8,128)(2,1)S(1)}, bf16[256,512]{1,0:T(8,128)(2,1)S(1)}, u32[]{:S(2)}, u32[]{:S(2)}) collective-permute-start(bf16[256,512]{1,0:T(8,128)(2,1)S(1)} %collective-permute-done.30.refs_3_), channel_id=1, source_target_pairs={{0,16},{4,12},{8,24},{12,4},{16,0},{20,28},{24,8},{28,20},{1,17},{... | collective-permute-start | bytes 786440 | tf_op jit(solution)/shard_map/ppermute | solution.py:696
  143.2 9.9 %collective-permute-start.27 = (bf16[2,64,1152]{2,1,0:T(8,128)(2,1)S(1)}, bf16[2,64,1152]{2,1,0:T(8,128)(2,1)S(1)}, u32[]{:S(2)}, u32[]{:S(2)}) collective-permute-start(bf16[2,64,1152]{2,1,0:T(8,128)(2,1)S(1)} %get-tuple-element.101), channel_id=1, source_target_pairs={{0,2},{1,0},{2,3},{3,1},{4,6},{5,4},{6,7},{7,5},{8,10},{9,8},{10,1... | collective-permute-start | bytes 884744 | tf_op jit(solution)/shard_map/ppermute | solution.py:724
  145.1 13.8 %collective-permute-start.34 = (bf16[2,64,1152]{2,1,0:T(8,128)(2,1)S(1)}, bf16[2,64,1152]{2,1,0:T(8,128)(2,1)S(1)}, u32[]{:S(2)}, u32[]{:S(2)}) collective-permute-start(bf16[2,64,1152]{2,1,0:T(8,128)(2,1)S(1)} %get-tuple-element.108), channel_id=1, source_target_pairs={{0,2},{1,0},{2,3},{3,1},{4,6},{5,4},{6,7},{7,5},{8,10},{9,8},{10,1... | collective-permute-start | bytes 884744 | tf_op jit(solution)/shard_map/ppermute | solution.py:724
  160.4 8.3 %collective-permute-start.36 = (bf16[64,1152]{1,0:T(8,128)(2,1)S(1)}, bf16[64,1152]{1,0:T(8,128)(2,1)S(1)}, u32[]{:S(2)}, u32[]{:S(2)}) collective-permute-start(bf16[64,1152]{1,0:T(8,128)(2,1)S(1)} %get-tuple-element.115), channel_id=1, source_target_pairs={{0,16},{4,20},{8,24},{12,28},{16,0},{20,4},{24,8},{28,12},{1,17},{... | collective-permute-start | bytes 442376 | tf_op jit(solution)/shard_map/ppermute | solution.py:729
  169.2 8.7 %collective-permute-start.38 = (bf16[64,1152]{1,0:T(8,128)(2,1)S(1)}, bf16[64,1152]{1,0:T(8,128)(2,1)S(1)}, u32[]{:S(2)}, u32[]{:S(2)}) collective-permute-start(bf16[64,1152]{1,0:T(8,128)(2,1)S(1)} %get-tuple-element.111), channel_id=1, source_target_pairs={{0,1},{1,2},{2,3},{3,0},{4,5},{5,6},{6,7},{7,4},{8,9},{9,10},{10,1... | collective-permute-start | bytes 442376 | tf_op jit(solution)/shard_map/ppermute | solution.py:738
  171.5 10.6 %collective-permute-start.39 = (bf16[64,1152]{1,0:T(8,128)(2,1)S(1)}, bf16[64,1152]{1,0:T(8,128)(2,1)S(1)}, u32[]{:S(2)}, u32[]{:S(2)}) collective-permute-start(bf16[64,1152]{1,0:T(8,128)(2,1)S(1)} %get-tuple-element.110), channel_id=1, source_target_pairs={{0,2},{1,3},{2,0},{3,1},{4,6},{5,7},{6,4},{7,5},{8,10},{9,11},{10,... | collective-permute-start | bytes 442376 | tf_op jit(solution)/shard_map/ppermute | solution.py:738
  172.4 9.7 %collective-permute-start.40 = (bf16[64,1152]{1,0:T(8,128)(2,1)S(1)}, bf16[64,1152]{1,0:T(8,128)(2,1)S(1)}, u32[]{:S(2)}, u32[]{:S(2)}) collective-permute-start(bf16[64,1152]{1,0:T(8,128)(2,1)S(1)} %get-tuple-element.109), channel_id=1, source_target_pairs={{0,3},{1,0},{2,1},{3,2},{4,7},{5,4},{6,5},{7,6},{8,11},{9,8},{10,9... | collective-permute-start | bytes 442376 | tf_op jit(solution)/shard_map/ppermute | solution.py:738
  (27 other events, 108.3 us)

commit v3 on v2

--- a/solution.py
+++ b/solution.py
@@ -82,45 +82,57 @@
 
 
 def norm_kernel(steps, x_hbm, gain_ref, *refs):
-    outs, (x_ref, y_ref, sems) = refs[:4], refs[4:]
-    chip = lax.shift_right_logical(lax.axis_index("wide"), 1)
-    depth = outs[0].shape[1]
-    step = x_ref.shape[0] // steps
+    (first_ref, second_ref, own_ref), (x_ref, y_ref, sems) = refs[:3], refs[3:]
+    me = lax.axis_index("wide")
+    chip, core = lax.shift_right_logical(me, 1), me & 1
+    depth = own_ref.shape[1]
+    rows = x_ref.shape[0]
+    step = rows // steps
     copies = [
         pltpu.make_async_copy(x_hbm.at[pl.ds(i * step, step), :], x_ref.at[pl.ds(i * step, step), :], sems.at[i])
         for i in range(steps)
     ]
     for copy in copies:
         copy.start()
-    gain = gain_ref[...].astype(F32)
+    gain = gain_ref[...].astype(F32).reshape(1, -1)
     for i in range(steps):
         copies[i].wait()
-        rows = slice(i * step, (i + 1) * step)
-        x = x_ref[rows, :].astype(F32)
+        at = i * step
+        x = x_ref[at : at + step, :].astype(F32)
         scale = lax.rsqrt(jnp.sum(x * x, axis=1, keepdims=True) / x.shape[1] + epsilon)
         y_ref[...] = (x * scale * gain).astype(BF16)
-        for delta in range(4):
-            outs[delta][rows, :] = y_ref[:, pl.ds(pl.multiple_of((chip ^ delta) * depth, 128), depth)]
+        for to, out, base in zip(order(chip, core), (first_ref, first_ref, second_ref, own_ref), (0, rows, 0, 0)):
+            out[base + at : base + at + step, :] = y_ref[:, pl.ds(pl.multiple_of(to * depth, 128), depth)]
 
 
 def norm(x, gain, steps, after):
     rows, cols = x.shape
-    shape = jax.ShapeDtypeStruct((rows, cols // CHIPS), x.dtype)
-    return call(
-        functools.partial(norm_kernel, steps), (x, gain[None, :]), [HBM, VMEM], (shape,) * 4, after,
+    depth = cols // CHIPS
+    shape = jax.ShapeDtypeStruct((rows, depth), x.dtype)
+    return call(
+        functools.partial(norm_kernel, steps), (x, gain), [HBM, VMEM],
+        (jax.ShapeDtypeStruct((2 * rows, depth), x.dtype), shape, shape), after,
         scratch=[
             pltpu.VMEM((rows, cols), BF16),
             pltpu.VMEM((rows // steps, cols), BF16),
             pltpu.SemaphoreType.DMA((steps,)),
         ],
-        out_specs=(VMEM,) * 4, name="norm", grant=60, flops=x.size * 4, moved=x.size * 4,
-    )
-
-
-def arrange_kernel(q_ref, k_ref, v_ref, o_ref, mine_ref, theirs_ref, sems):
-    chip = lax.shift_right_logical(lax.axis_index("wide"), 1)
-    own = lax.axis_index("wide") & 1
+        out_specs=(VMEM,) * 3, name="norm", grant=60, flops=x.size * 4, moved=x.size * 4,
+    )
+
+
+def arrange_kernel(q_hbm, k_hbm, v_hbm, o_hbm, mine_ref, theirs_ref, q_ref, k_ref, v_ref, o_ref, in_sems, sems):
+    me = lax.axis_index("wide")
+    chip, own = lax.shift_right_logical(me, 1), me & 1
     d = HEAD_DIM
+    loads = [
+        pltpu.make_async_copy(source, target, in_sems.at[i])
+        for i, (source, target) in enumerate(
+            ((q_hbm, q_ref), (k_hbm, k_ref), (v_hbm, v_ref), (o_hbm, o_ref))
+        )
+    ]
+    for one in loads:
+        one.start()
     copies = []
 
     def copy(ref, at, out, to, width):
@@ -128,10 +140,13 @@
         copies.append(pltpu.make_async_copy(source, out.at[:, pl.ds(to, width)], sems.at[len(copies)]))
         copies[-1].start()
 
+    for load, ref, width, at in zip(loads, (q_ref, k_ref, v_ref), (2 * d, d, d), (0, 2 * d, 3 * d)):
+        load.wait()
+        for core, out in ((1 - own, theirs_ref), (own, mine_ref)):
+            for place, to in enumerate(order(chip, core)):
+                copy(ref, to * width, out, 4 * place * d + at, width)
+    loads[3].wait()
     for core, out in ((1 - own, theirs_ref), (own, mine_ref)):
-        for place, to in enumerate(order(chip, core)):
-            for ref, width, at in ((q_ref, 2 * d, 0), (k_ref, d, 2 * d), (v_ref, d, 3 * d)):
-                copy(ref, to * width, out, 4 * place * d + at, width)
         for place, source in enumerate(near(chip, core)):
             copy(o_ref, (2 * source + core) * d, out, (4 * CHIPS + place) * d, d)
     for one in copies:
@@ -141,8 +156,10 @@
 def arrange(q, k, v, o, after):
     shape = jax.ShapeDtypeStruct((q.shape[0], 5 * CHIPS * HEAD_DIM), BF16)
     return call(
-        arrange_kernel, (q, k, v, o), [ANY] * 4, (shape, shape), after,
-        scratch=[pltpu.SemaphoreType.DMA((32,))], out_specs=(ANY, ANY), name="arrange", moved=q.size * 16,
+        arrange_kernel, (q, k, v, o), [HBM] * 4, (shape, shape), after,
+        scratch=[pltpu.VMEM(x.shape, BF16) for x in (q, k, v, o)]
+        + [pltpu.SemaphoreType.DMA((4,)), pltpu.SemaphoreType.DMA((32,))],
+        out_specs=(ANY, ANY), name="arrange", grant=60, moved=q.size * 16,
     )
 
 
@@ -153,14 +170,17 @@
     return adapter
 
 
-def pick_kernel(prompts, chosen_ref, down_hbm, upo_hbm, pack_ref, down_ref, upo_ref, sems):
+def pick_kernel(prompts, chosen_ref, down_hbm, other_hbm, upo_hbm, pack_ref, down_ref, other_ref, upo_ref, sems):
     me, z = lax.axis_index("wide"), lax.axis_index("narrow")
     chip = lax.shift_right_logical(me, 1)
     core = me & 1
     n_codes = prompts * RANK
     local = down_ref.shape[0] // (3 * RANK)
     rows = down_ref.shape[1]
-    copies = [pltpu.make_async_copy(down_hbm, down_ref, sems.at[prompts])]
+    copies = [
+        pltpu.make_async_copy(down_hbm, down_ref, sems.at[prompts]),
+        pltpu.make_async_copy(other_hbm, other_ref, sems.at[prompts + 1]),
+    ]
     for p in range(prompts):
         at = pl.ds(pl.multiple_of(chosen_ref[p] * RANK, RANK), RANK)
         copies.append(pltpu.make_async_copy(upo_hbm.at[at, :], upo_ref.at[pl.ds(p * RANK, RANK), :], sems.at[p]))
@@ -170,29 +190,35 @@
     row = lax.broadcasted_iota(jnp.int32, shape, 0)
     col = lax.broadcasted_iota(jnp.int32, shape, 1)
     adapter = choose(shape, (row % n_codes) // RANK, chosen_ref, prompts)
-    wanted = (adapter - z * local) * (3 * RANK) + (row // n_codes) * RANK + row % RANK
-    inside = jnp.logical_and(adapter >= z * local, adapter < (z + 1) * local)
-    pick = jnp.where(jnp.logical_and(inside, col == wanted), 1.0, 0.0).astype(BF16)
+
+    def pick_of(plane_at):
+        wanted = (adapter - plane_at * local) * (3 * RANK) + (row // n_codes) * RANK + row % RANK
+        inside = jnp.logical_and(adapter >= plane_at * local, adapter < (plane_at + 1) * local)
+        return jnp.where(jnp.logical_and(inside, col == wanted), 1.0, 0.0).astype(BF16)
+
+    mine, theirs = pick_of(z), pick_of(z ^ 1)
     for copy in copies:
         copy.wait()
-    down = jnp.dot(pick, down_ref[...], preferred_element_type=F32)
+    down = jnp.dot(mine, down_ref[...], preferred_element_type=F32)
+    down = down + jnp.dot(theirs, other_ref[...], preferred_element_type=F32)
     pack_ref[: 3 * n_codes, :] = down.astype(BF16)
     both = upo_ref[...].astype(F32) * adapter_scale
     part = jnp.where(core == 0, both[:, :rows], both[:, rows:])
     pack_ref[3 * n_codes :, :] = jnp.where(z == chip, part, 0.0).astype(BF16)
 
 
-def pick(chosen, down, upo, after):
+def pick(chosen, down, other, upo, after):
     prompts = chosen.shape[0]
     n_codes = prompts * RANK
     return call(
-        functools.partial(pick_kernel, prompts), (chosen, down, upo), [SMEM, HBM, HBM],
+        functools.partial(pick_kernel, prompts), (chosen, down, other, upo), [SMEM, HBM, HBM, HBM],
         jax.ShapeDtypeStruct((4 * n_codes, down.shape[1]), BF16),
         after,
         scratch=[
             pltpu.VMEM(down.shape, BF16),
+            pltpu.VMEM(down.shape, BF16),
             pltpu.VMEM((n_codes, upo.shape[1]), BF16),
-            pltpu.SemaphoreType.DMA((prompts + 1,)),
+            pltpu.SemaphoreType.DMA((prompts + 2,)),
         ],
         out_specs=VMEM, name="pick", grant=60, flops=down.size * 400, moved=down.size * 6,
     )
@@ -287,10 +313,10 @@
     out_ref[...] = jnp.concatenate([left, right], axis=1).astype(out_ref.dtype)
 
 
-def join(mine, other):
+def join(mine, other, after=()):
     rows, cols = mine.shape
     return call(
-        join_kernel, (mine, other), [VMEM, VMEM], jax.ShapeDtypeStruct((rows, 2 * cols), mine.dtype),
+        join_kernel, (mine, other), [VMEM, VMEM], jax.ShapeDtypeStruct((rows, 2 * cols), mine.dtype), after,
         out_specs=VMEM, name="join", flops=rows * cols * 4, moved=rows * cols * 8,
     )
 
@@ -305,16 +331,16 @@
     rows = x_ref.shape[0]
     half = send_ref.shape[1]
     n_codes = prompts * RANK
-    for k in range(4):
-
-        @pl.when((chip ^ chunk) == k)
+    for k, held in enumerate((chip ^ (1 + core), chip ^ 3, chip ^ (2 - core), chip)):
+
+        @pl.when(held == chunk)
         def _():
-            pltpu.make_async_copy(x_refs[k], x_ref, sem).start()
-
-    pltpu.make_async_copy(x_refs[0], x_ref, sem).wait()
+            pltpu.make_async_copy(x_refs[k].at[pl.ds(0, rows), :], x_ref, sem).start()
+
+    pltpu.make_async_copy(x_refs[3], x_ref, sem).wait()
     x = x_ref[...]
     codes = lax.dot_general(
-        x, pack_ref[: 3 * n_codes, :], (((1,), (1,)), ((), ())), preferred_element_type=F32
+        x, pack_ref[...], (((1,), (1,)), ((), ())), preferred_element_type=F32
     )
     places = (2 * chunk + core) * rows + lax.broadcasted_iota(jnp.int32, (rows, 1), 0)
     prompt, _ = prompt_of(places, lengths_ref, prompts)
@@ -329,7 +355,7 @@
 
 
 def project(lengths, pieces, w, pack, up, chunk, after, carry=()):
-    rows, depth = pieces[0].shape
+    rows, depth = pieces[3].shape
     half = w.shape[1] // 2
     n = len(after) + 8
     out = call(
@@ -500,75 +526,66 @@
     )
 
 
-def output_kernel(group, prompts, lengths_ref, *refs):
+def output_kernel(before, count, prompts, lengths_ref, *refs):
     blocks = refs[:4]
-    weights = refs[4:7]
-    pack_ref, keep_ref, send_ref, acc_ref = refs[7:]
-    me, z = lax.axis_index("wide"), lax.axis_index("narrow")
-    core = me & 1
+    weights = refs[4 : 4 + count]
+    up_ref, keep_ref, send_ref, acc_ref = refs[4 + count :]
+    z = lax.axis_index("narrow")
+    core = lax.axis_index("wide") & 1
     rows, cols = acc_ref.shape
     d = HEAD_DIM
-    count, part = keep_ref.shape[1:3]
+    chips, part = keep_ref.shape[:2]
+    codes = None
+    for k in range(count):
+        a = jnp.concatenate([blocks[r][:, k * d : (k + 1) * d] for r in range(4)], axis=1)
+        product = lax.dot_general(a, weights[k][:cols, :], (((1,), (1,)), ((), ())), preferred_element_type=F32)
+        terms = lax.dot_general(a, weights[k][cols:, :], (((1,), (1,)), ((), ())), preferred_element_type=F32)
+        if k == 0:
+            acc_ref[...] = product
+            codes = terms
+        else:
+            acc_ref[...] += product
+            codes = codes + terms
     row = lax.broadcasted_iota(jnp.int32, (rows, 1), 0)
-    up = pack_ref[3 * prompts * RANK :, :]
-
-    def times(k, w_ref):
-        a = jnp.concatenate([blocks[r][:, k * d : (k + 1) * d] for r in range(4)], axis=1)
-        product = lax.dot_general(a, w_ref[:cols, :], (((1,), (1,)), ((), ())), preferred_element_type=F32)
-        codes = lax.dot_general(a, w_ref[cols:, :], (((1,), (1,)), ((), ())), preferred_element_type=F32)
-        return product, codes
-
-    def leave(slot, codes, plane):
-        places = (2 * count * group + row // part) * (4 * part) + plane * part + row % part
-        prompt, _ = prompt_of(places, lengths_ref, prompts)
-        lane = lax.broadcasted_iota(jnp.int32, codes.shape, 1)
-        codes = jnp.where(lane // RANK == prompt, codes, 0.0).astype(BF16)
-        acc_ref[...] += jnp.dot(codes, up, preferred_element_type=F32)
-        for i in range(count):
-            mine = pl.multiple_of(i * 2 * part + core * part, part)
-            theirs = pl.multiple_of(i * 2 * part + (1 - core) * part, part)
-            keep_ref[slot, i] = acc_ref[pl.ds(mine, part), :]
-            send_ref[slot, i] = acc_ref[pl.ds(theirs, part), :].astype(BF16)
-
-    product, codes = times(3, weights[0])
-    acc_ref[...] = product
-    leave(1, codes, plane(BEFORE, z))
-    product, codes = times(0, weights[0])
-    acc_ref[...] = product
-    for k in (1, 2):
-        product, terms = times(k, weights[k])
-        acc_ref[...] += product
-        codes = codes + terms
-    leave(0, codes, z)
-
-
-def output(lengths, blocks, weights, pack, group, part, after):
+    places = (row // part) * (4 * part) + (plane(BEFORE, z) if before else z) * part + row % part
+    prompt, _ = prompt_of(places, lengths_ref, prompts)
+    lane = lax.broadcasted_iota(jnp.int32, codes.shape, 1)
+    codes = jnp.where(lane // RANK == prompt, codes, 0.0).astype(BF16)
+    acc_ref[...] += jnp.dot(codes, up_ref[...], preferred_element_type=F32)
+    for i in range(chips):
+        mine = pl.multiple_of(i * 2 * part + core * part, part)
+        theirs = pl.multiple_of(i * 2 * part + (1 - core) * part, part)
+        keep_ref[i] = acc_ref[pl.ds(mine, part), :]
+        send_ref[i] = acc_ref[pl.ds(theirs, part), :].astype(BF16)
+
+
+def output(lengths, blocks, weights, up, before, after):
     rows = blocks[0].shape[0]
-    cols = pack.shape[1]
-    shape = (2, rows // (2 * part), part, cols)
-    return call(
-        functools.partial(output_kernel, group, lengths.shape[0]),
-        (lengths, *blocks, *weights, pack),
-        [SMEM] + [VMEM] * 8,
+    cols = up.shape[1]
+    shape = (CHIPS, rows // (2 * CHIPS), cols)
+    return call(
+        functools.partial(output_kernel, before, len(weights), lengths.shape[0]),
+        (lengths, *blocks, *weights, up),
+        [SMEM] + [VMEM] * (5 + len(weights)),
         (jax.ShapeDtypeStruct(shape, F32), jax.ShapeDtypeStruct(shape, BF16)),
         after,
         scratch=[pltpu.VMEM((rows, cols), F32)],
         out_specs=(VMEM, VMEM), name="output",
-        flops=2 * rows * 2048 * cols, moved=2048 * cols * 2 + rows * 2048 * 2 + rows * cols * 3,
-    )
-
-
-def fold_kernel(keep_ref, got_ref, out_ref, send_ref):
-    out_ref[...] = keep_ref[0] + got_ref[0].astype(F32)
-    send_ref[...] = (keep_ref[1] + got_ref[1].astype(F32)).astype(BF16)
-
-
-def fold(keep, got):
-    shape = keep.shape[1:]
-    return call(
-        fold_kernel, (keep, got), [VMEM, VMEM],
-        (jax.ShapeDtypeStruct(shape, F32), jax.ShapeDtypeStruct(shape, BF16)),
-        out_specs=(VMEM, VMEM), name="fold", flops=keep.size, moved=keep.size * 8,
+        flops=2 * rows * 512 * len(weights) * cols, moved=2048 * cols * 2 + rows * 2048 * 2 + rows * cols * 3,
+    )
+
+
+def fold_kernel(*refs):
+    total = refs[0][...]
+    for ref in refs[1:-1]:
+        total = total + ref[...].astype(F32)
+    refs[-1][...] = total.astype(BF16)
+
+
+def fold(keep, *got):
+    return call(
+        fold_kernel, (keep, *got), [VMEM] * (1 + len(got)), jax.ShapeDtypeStruct(keep.shape, BF16),
+        out_specs=VMEM, name="fold", flops=keep.size, moved=keep.size * 8,
     )
 
 
@@ -641,19 +658,25 @@
     cosine = jnp.concatenate([cosine, cosine], axis=1)
     sine = jnp.concatenate([-sine, sine], axis=1)
 
-    pack = pick(prompt_adapters, adapter_down.T, adapter_up_out, ())
-    cut = norm(residual, pre_gain, 4, (pack,))
-    pieces = [cut[0]] + [lax.ppermute(cut[delta], "wide", flip(2 * delta)) for delta in (1, 2, 3)]
-    pack = merge(pack, lax.ppermute(pack, "narrow", zflip(1)), cut)
-    w_mine, w_theirs = arrange(
-        query_weight, key_weight, value_weight, output_weight.T, (pack, pieces[1])
-    )
+    down = adapter_down.T
+    down_other = lax.ppermute(down, "narrow", zflip(1))
+    first, second, own = norm(residual, pre_gain, 4, ())
+    w_mine, w_theirs = arrange(query_weight, key_weight, value_weight, output_weight.T, (own,))
+    first = lax.ppermute(first, "wide", first_leg)
+    second = lax.ppermute(second, "wide", second_leg)
+    third = lax.ppermute(first[tok:], "wide", second_leg)
+    pieces = (first, third, second, own)
+
+    pack = pick(prompt_adapters, down, down_other, adapter_up_out, (w_mine,))
     up, out_down = ups(
-        prompt_adapters, adapter_up_query, adapter_up_key, adapter_up_value, adapter_down_out, (w_mine,)
+        prompt_adapters, adapter_up_query, adapter_up_key, adapter_up_value, adapter_down_out, (own,)
     )
     w, ring0 = stack(w_mine, lax.ppermute(w_theirs, "wide", across), out_down, (up,))
     pack = merge(pack, lax.ppermute(pack, "narrow", zflip(2)), (w, cosine, sine))
-    pack = join(pack, lax.ppermute(pack, "wide", across))
+    n_down = 3 * prompts * RANK
+    up_out = pack[n_down:]
+    up_out = up_out + lax.ppermute(up_out, "narrow", zflip(1))
+    pack = join(pack[:n_down], lax.ppermute(pack[:n_down], "wide", across))
     ring1 = lax.ppermute(ring0, "narrow", to_next)
 
     tables = (cosine, sine)
@@ -681,49 +704,36 @@
     def attend_chunk(chunk, after, before=(), carry=()):
         return attend(prompt_lengths, sink_logits, mine, other, chunk, after, before, carry)
 
-    def gather_group(sub, after):
-        near0 = beside(
-            (
-                sub[0],
-                lax.ppermute(sub[1], "narrow", to_next),
-                lax.ppermute(sub[2], "narrow", to_second),
-                sub[3],
-            ),
-            after,
-        )
+    def gather(near0):
         near1 = lax.ppermute(near0, "wide", first_leg)
         near2 = lax.ppermute(near0, "wide", second_leg)
-        near3 = lax.ppermute(near1, "wide", second_leg)
-        return near0, near1, near2, near3
-
-    product(0, (cosine, sine))
-    product(1, (sends[0],))
-    (out0,) = pass_on(0, (sends[1],))
-    product(2, (out0,))
-    (out1,) = pass_on(1, (sends[2],))
+        return near0, near1, near2, lax.ppermute(near1, "wide", second_leg)
+
+    product(0, ())
+    for chunk in range(1, CHUNKS):
+        product(chunk, (sends[-1],))
+    up_out = join(up_out, lax.ppermute(up_out, "wide", across), (sends[-1],))
+    (out0,) = pass_on(0, (sends[-1],))
+    (out1,) = pass_on(1, (out0,))
     q0 = rotate_chunk(0, (out1,))
-    product(3, (q0,))
-    out2, ring1 = pass_on(2, (sends[3],), (ring1,))
+    out2, ring1 = pass_on(2, (q0,), (ring1,))
     ring2 = lax.ppermute(ring1, "narrow", to_next)
     q1 = rotate_chunk(1, (out2,))
     sub0, _ = attend_chunk(0, (q1,))
     (out3,) = pass_on(3, (sub0[0],))
     q2 = rotate_chunk(2, (out3,))
     sub1, _ = attend_chunk(1, (q2,), sub0)
-    q3 = rotate_chunk(3, (sub1[0],))
-    sub2, _ = attend_chunk(2, (q3,))
-    sub3, _ = attend_chunk(3, (sub2[0],), sub2)
-    out_weights = (ring0, ring1, ring2)
-    halves = []
-    before = sub3[0]
-    for group, sub in enumerate((sub1, sub3)):
-        keep, send = output(
-            prompt_lengths, gather_group(sub, (sub3[0],)), out_weights, pack, group, part, (before,)
-        )
-        main, extra = fold(keep, lax.ppermute(send, "wide", across))
-        halves.append(merge(main, lax.ppermute(extra, "narrow", to_before)))
-        before = keep
-    total = jnp.concatenate(halves)
+    sub2, _ = attend_chunk(2, (sub1[0],), sub1)
+    q3 = rotate_chunk(3, (sub2[0],))
+    sub3, (ring2,) = attend_chunk(3, (q3,), sub2, (ring2,))
+    aside = gather(sub3[3])
+    keep, send = output(prompt_lengths, aside, (ring0,), up_out, True, ())
+    extra = lax.ppermute(fold(keep, lax.ppermute(send, "wide", across)), "narrow", to_before)
+    near0 = beside(
+        (sub3[0], lax.ppermute(sub3[1], "narrow", to_next), lax.ppermute(sub3[2], "narrow", to_second)), ()
+    )
+    keep, send = output(prompt_lengths, gather(near0), (ring0, ring1, ring2), up_out, False, ())
+    total = fold(keep, lax.ppermute(send, "wide", across), extra)
     rows_of = lambda to: lax.dynamic_index_in_dim(total, to, 0, keepdims=False)
     full = [rows_of(chip)] + [
         lax.ppermute(rows_of(chip ^ delta), "wide", flip(2 * delta)) for delta in (1, 2, 3)

time: 184 us -> 168 us (0.913)
  starting transfers between devices: 55.4 us -> 49.2 us
  waiting for transfers between devices: 67.6 us -> 61.4 us
  local copies, waits for them, and re-layouts: 6.41 us -> 2.42 us
    ppermute x19 -> x18, waiting for transfers between devices: 36.7 us -> 29.2 us  [the longest x2 7.29 us: gather(): return (near0, near1, near2, lax.ppermute(near1, 'wide', second_leg))]
    ppermute x1, waiting for transfers between devices: 6.82 us -> 0.01 us  [per_device_heads(): lax.ppermute(pack, 'narrow', zflip(2))]
    ppermute x19 -> x18, starting transfers between devices: 27.8 us -> 21 us  [the longest x1 3.17 us: per_device_heads(): lax.ppermute(fold(keep, lax.ppermute(send, 'wide', across)), 'narrow', to...]
    ppermute x4, waiting for transfers between devices: 5.83 us -> 12.3 us  [pass_on(): twos.append(lax.ppermute(out, 'wide', second_leg))]
    unnamed x36 -> x28, local copies, waits for them, and re-layouts: 3.93 us -> 1.11 us
    pallas_call x33 -> x30, Pallas kernels: 47.9 us -> 48.9 us  [call(): pl.pallas_call(lambda *refs: kernel(*refs[n:]), out_shape=out_shape, in_s...]
  transfers between devices with their start and end apart: 41 -> 40, of which waited for: 22 -> 21; matrix products, arithmetic and copies ran while one was open for 3% -> 3% of each run, Pallas kernels for 21% -> 21%
where the time goes in v3:
time: 168 us
  waiting for transfers between devices  61.4 us (37%)
  starting transfers between devices  49.2 us (29%)
  Pallas kernels  48.9 us (29%)
  other arithmetic  5.07 us (3%)
  local copies, waits for them, and re-layouts  2.42 us (1%)
    pallas_call x30, Pallas kernels, call(): pl.pallas_call(lambda *refs: kernel(*refs[n:]), out_shape=out_shape, in_s...  48.9 us
    ppermute x4, waiting for transfers between devices, pass_on(): twos.append(lax.ppermute(out, 'wide', second_leg))  12.3 us
    ppermute x2, waiting for transfers between devices, gather(): return (near0, near1, near2, lax.ppermute(near1, 'wide', second_leg))  7.29 us
    ppermute x3, starting transfers between devices, per_device_heads(): finals.append(piece if k == 0 else lax.ppermute(piece, 'narrow', shift(k)))  6.42 us
    ppermute x1, waiting for transfers between devices, per_device_heads(): first = lax.ppermute(first, 'wide', first_leg)  6.29 us
    ppermute x3, waiting for transfers between devices, per_device_heads(): lax.ppermute(rows_of(chip ^ delta), 'wide', flip(2 * delta))  6.12 us
    ppermute x3, waiting for transfers between devices, per_device_heads(): finals.append(piece if k == 0 else lax.ppermute(piece, 'narrow', shift(k)))  5.83 us
    ppermute x4, starting transfers between devices, product(): ones.append(lax.ppermute(send, 'wide', first_leg))  5.28 us
  transfers between devices with their start and end apart: 40, of which 21 were waited for; matrix products, arithmetic and copies ran while one was open for 3% of the time, Pallas kernels for 21%

profile of v3, /device:TPU:0, one launch (start us, length us, event | category | flops | bytes accessed | tf_op | source)
XLA Modules:
  0.0 167.6 jit_solution(16315566771076823111)
XLA Ops:
  0.0 4.6 %norm.1 = (bf16[512,1152]{1,0:T(8,128)(2,1)}, bf16[256,1152]{1,0:T(8,128)(2,1)}, bf16[256,1152]{1,0:T(8,128)(2,1)}) custom-call(bf16[256,4608]{1,0:T(8,128)(2,1)} %refs_0_.4, bf16[4608]{0:T(1024)(128)(2,1)} %refs_1_.11), custom_call_target="tpu_custom_call" | custom-call | flops 73728 | bytes 73728 | tf_op jit(solution)/shard_map/norm/pallas_call | solution.py:44
  4.7 4.3 %arrange.1 = (bf16[576,2560]{1,0:T(8,128)(2,1)}, bf16[576,2560]{1,0:T(8,128)(2,1)}) custom-call(bf16[256,1152]{1,0:T(8,128)(2,1)} %get-tuple-element.55.refs_0_.refs_4_.refs_5_, bf16[576,1024]{1,0:T(8,128)(2,1)} %refs_1_.13, bf16[576,512]{1,0:T(8,128)(2,1)} %refs_2_.7, bf16[576,512]{1,0:T(8,128)(2,1)} %refs_3_.3, bf16[576,1024]{1,0:T(8,128)(2,1)} %bitcast.23), custom_call_target="tpu_custom_call" | custom-call | bytes 147456 | tf_op jit(solution)/shard_map/arrange/pallas_call | solution.py:44
  9.5 2.6 %collective-permute-start = (bf16[512,1152]{1,0:T(8,128)(2,1)S(1)}, bf16[512,1152]{1,0:T(8,128)(2,1)S(1)}, u32[]{:S(2)}, u32[]{:S(2)}) collective-permute-start(bf16[512,1152]{1,0:T(8,128)(2,1)S(1)} %copy-done.13), channel_id=1, source_target_pairs={{0,8},{4,20},{8,0},{12,28},{16,24},{20,4},{24,16},{28,12},{1,9},{5... | collective-permute-start | bytes 3538952 | tf_op jit(solution)/shard_map/ppermute | solution.py:665
  15.5 4.6 %collective-permute-done.4.refs_3_ = bf16[192,576]{1,0:T(8,128)(2,1)S(1)} collective-permute-done((bf16[192,576]{1,0:T(8,128)(2,1)S(1)}, bf16[192,576]{1,0:T(8,128)(2,1)S(1)}, u32[]{:S(2)}, u32[]{:S(2)}) %collective-permute-start.4) | collective-permute-done | bytes 221216 | tf_op jit(solution)/shard_map/ppermute | solution.py:662
  20.8 2.8 %pick.1.refs_3_ = bf16[256,576]{1,0:T(8,128)(2,1)} custom-call(bf16[576,2560]{1,0:T(8,128)(2,1)} %get-tuple-element.57.refs_1_.refs_0_, s32[4]{0:T(128)} %refs_1_.14, bf16[192,576]{1,0:T(8,128)(2,1)} %bitcast.30, bf16[192,576]{1,0:T(8,128)(2,1)} %copy-done.11, bf16[256,1152]{1,0:T(8,128)(2,1)} %refs_4_.3), custom_call_target="tpu_custom_call" | custom-call | flops 691200 | bytes 10368 | tf_op jit(solution)/shard_map/pick/pallas_call | solution.py:44
  23.7 2.6 %collective-permute-start.5 = (bf16[256,576]{1,0:T(8,128)(2,1)}, bf16[256,576]{1,0:T(8,128)(2,1)S(1)}, u32[]{:S(2)}, u32[]{:S(2)}) collective-permute-start(bf16[256,576]{1,0:T(8,128)(2,1)} %pick.1.refs_3_), channel_id=1, source_target_pairs={{0,2},{1,3},{2,0},{3,1},{4,6},{5,7},{6,4},{7,5},{8,10},{9,11},{10,... | collective-permute-start | bytes 884744 | tf_op jit(solution)/shard_map/ppermute | solution.py:675
  26.3 6.3 %collective-permute-done.refs_1_.refs_2_ = bf16[512,1152]{1,0:T(8,128)(2,1)S(1)} collective-permute-done((bf16[512,1152]{1,0:T(8,128)(2,1)S(1)}, bf16[512,1152]{1,0:T(8,128)(2,1)S(1)}, u32[]{:S(2)}, u32[]{:S(2)}) %collective-permute-start) | collective-permute-done | bytes 1179680 | tf_op jit(solution)/shard_map/ppermute | solution.py:665
  34.8 3.7 %fusion.2 = (f32[2048,64]{1,0:T(8,128)S(1)}, f32[2048,64]{1,0:T(8,128)S(1)}, f32[2048,64]{1,0:T(8,128)S(1)}) fusion(f32[64]{0:T(128)S(1)} %negate_power_fusion, f32[2048]{0:T(1024)S(1)} %subtract_convert_fusion), kind=kLoop, calls=%fused_computation.9 | loop fusion | flops 262144 | bytes 1581312 | tf_op jit(solution)/shard_map/neg | solution.py:659
  39.4 2.3 %stack.18 = (bf16[1152,2048]{1,0:T(8,128)(2,1)S(1)}, bf16[1216,512]{1,0:T(8,128)(2,1)S(1)}) custom-call(bf16[192,2048]{1,0:T(8,128)(2,1)S(1)} %get-tuple-element.56.refs_0_.refs_7_.refs_8_, bf16[576,2560]{1,0:T(8,128)(2,1)S(1)} %copy-done.1, bf16[576,2560]{1,0:T(8,128)(2,1)} %collective-permute-done.3.refs_2_, bf16[64,512]{1,0:T(8,128)(2,1)S(1)} %get-tuple-element.59.refs_3_), custom_call_target="tpu_custom_call" | custom-call | bytes 184320 | tf_op jit(solution)/shard_map/stack/pallas_call | solution.py:44
  46.2 2.8 %project.4 = (bf16[256,1024]{1,0:T(8,128)(2,1)S(1)}, f32[256,1024]{1,0:T(8,128)S(1)}) custom-call(s32[4]{0:T(128)S(1)} %copy-done.7, bf16[512,1152]{1,0:T(8,128)(2,1)S(1)} %collective-permute-done.refs_1_.refs_2_, bf16[256,1152]{1,0:T(8,128)(2,1)S(1)} %collective-permute-done.1.refs_2_.refs_3_, bf16[256,1152]{1,0:T(8,128)(2,1)S(1)} %collective-permute-done.2.refs_3_.refs_4_, ...), custom_call_target="tpu_custom_call" | custom-call | flops 18874368 | bytes 107520 | tf_op jit(solution)/shard_map/project/pallas_call | solution.py:44
  50.7 2.9 %project.5 = (bf16[256,1024]{1,0:T(8,128)(2,1)S(1)}, f32[256,1024]{1,0:T(8,128)S(1)}) custom-call(bf16[256,1024]{1,0:T(8,128)(2,1)S(1)} %get-tuple-element.61.refs_0_, s32[4]{0:T(128)S(1)} %copy-done.7, bf16[512,1152]{1,0:T(8,128)(2,1)S(1)} %collective-permute-done.refs_1_.refs_2_, bf16[256,1152]{1,0:T(8,128)(2,1)S(1)} %collective-permute-done.1.refs_2_.refs_3_, ...), custom_call_target="tpu_custom_call" | custom-call | flops 18874368 | bytes 107520 | tf_op jit(solution)/shard_map/project/pallas_call | solution.py:44
  54.0 3.0 %project.6 = (bf16[256,1024]{1,0:T(8,128)(2,1)S(1)}, f32[256,1024]{1,0:T(8,128)S(1)}) custom-call(bf16[256,1024]{1,0:T(8,128)(2,1)S(1)} %get-tuple-element.62.refs_0_, s32[4]{0:T(128)S(1)} %copy-done.7, bf16[512,1152]{1,0:T(8,128)(2,1)S(1)} %collective-permute-done.refs_1_.refs_2_, bf16[256,1152]{1,0:T(8,128)(2,1)S(1)} %collective-permute-done.1.refs_2_.refs_3_, ...), custom_call_target="tpu_custom_call" | custom-call | flops 18874368 | bytes 107520 | tf_op jit(solution)/shard_map/project/pallas_call | solution.py:44
  58.7 2.8 %project.7 = (bf16[256,1024]{1,0:T(8,128)(2,1)S(1)}, f32[256,1024]{1,0:T(8,128)S(1)}) custom-call(bf16[256,1024]{1,0:T(8,128)(2,1)S(1)} %get-tuple-element.63.refs_0_, s32[4]{0:T(128)S(1)} %copy-done.7, bf16[512,1152]{1,0:T(8,128)(2,1)S(1)} %collective-permute-done.refs_1_.refs_2_, bf16[256,1152]{1,0:T(8,128)(2,1)S(1)} %collective-permute-done.1.refs_2_.refs_3_, ...), custom_call_target="tpu_custom_call" | custom-call | flops 18874368 | bytes 107520 | tf_op jit(solution)/shard_map/project/pallas_call | solution.py:44
  62.2 2.8 %collective-permute-done.8.refs_2_ = bf16[256,1024]{1,0:T(8,128)(2,1)S(1)} collective-permute-done((bf16[256,1024]{1,0:T(8,128)(2,1)S(1)}, bf16[256,1024]{1,0:T(8,128)(2,1)S(1)}, u32[]{:S(2)}, u32[]{:S(2)}) %collective-permute-start.8) | collective-permute-done | bytes 524320 | tf_op jit(solution)/shard_map/ppermute | solution.py:690
  65.1 5.8 %collective-permute-done.9.refs_3_ = bf16[256,512]{1,0:T(8,128)(2,1)S(1)} collective-permute-done((bf16[256,512]{1,0:T(8,128)(2,1)S(1)}, bf16[256,512]{1,0:T(8,128)(2,1)S(1)}, u32[]{:S(2)}, u32[]{:S(2)}) %collective-permute-start.9) | collective-permute-done | bytes 262176 | tf_op jit(solution)/shard_map/ppermute | solution.py:695
  72.4 2.7 %collective-permute-start.20 = (bf16[1216,512]{1,0:T(8,128)(2,1)S(1)}, bf16[1216,512]{1,0:T(8,128)(2,1)S(1)}, u32[]{:S(2)}, u32[]{:S(2)}) collective-permute-start(bf16[1216,512]{1,0:T(8,128)(2,1)S(1)} %get-tuple-element.91.refs_6_), channel_id=1, source_target_pairs={{0,1},{1,3},{2,0},{3,2},{4,5},{5,7},{6,4},{7,6},{8,9},{9,11},{10,8... | collective-permute-start | bytes 3735560 | tf_op jit(solution)/shard_map/ppermute | solution.py:720
  78.6 6.5 %collective-permute-done.12.refs_3_ = bf16[256,512]{1,0:T(8,128)(2,1)S(1)} collective-permute-done((bf16[256,512]{1,0:T(8,128)(2,1)S(1)}, bf16[256,512]{1,0:T(8,128)(2,1)S(1)}, u32[]{:S(2)}, u32[]{:S(2)}) %collective-permute-start.12) | collective-permute-done | bytes 262176 | tf_op jit(solution)/shard_map/ppermute | solution.py:695
  92.0 2.7 %attend.5 = (bf16[256,128]{1,0:T(8,128)(2,1)S(1)}, bf16[256,128]{1,0:T(8,128)(2,1)S(1)}, bf16[256,128]{1,0:T(8,128)(2,1)S(1)}, bf16[256,128]{1,0:T(8,128)(2,1)S(1)}) custom-call(bf16[256,384]{1,0:T(8,128)(2,1)S(1)} %get-tuple-element.75.refs_0_.refs_5_, s32[4]{0:T(128)S(1)} %copy-done.7, f32[8]{0:T(128)S(1)} %copy-done.8, ...), custom_call_target="tpu_custom_call" | custom-call | flops 3145728 | bytes 8192 | tf_op jit(solution)/shard_map/attend/pallas_call | solution.py:44
  94.7 4.1 %attend.6 = (bf16[384,128]{1,0:T(8,128)(2,1)S(1)}, bf16[384,128]{1,0:T(8,128)(2,1)S(1)}, bf16[384,128]{1,0:T(8,128)(2,1)S(1)}, bf16[384,128]{1,0:T(8,128)(2,1)S(1)}) custom-call(bf16[256,128]{1,0:T(8,128)(2,1)S(1)} %get-tuple-element.80.refs_0_.refs_9_, s32[4]{0:T(128)S(1)} %copy-done.7, f32[8]{0:T(128)S(1)} %copy-done.8, ...), custom_call_target="tpu_custom_call" | custom-call | flops 3145728 | bytes 12288 | tf_op jit(solution)/shard_map/attend/pallas_call | solution.py:44
  101.9 4.2 %attend.7 = (bf16[1216,512]{1,0:T(8,128)(2,1)S(1)}, bf16[512,128]{1,0:T(8,128)(2,1)S(1)}, bf16[512,128]{1,0:T(8,128)(2,1)S(1)}, bf16[512,128]{1,0:T(8,128)(2,1)S(1)}, bf16[512,128]{1,0:T(8,128)(2,1)S(1)}) custom-call(bf16[256,384]{1,0:T(8,128)(2,1)S(1)} %get-tuple-element.86.refs_0_.refs_6_, s32[4]{0:T(128)S(1)} %copy-done.7, ...), custom_call_target="tpu_custom_call", output_to_operand_aliasing={{0}: (15, {})} | custom-call | flops 3145728 | bytes 16384 | tf_op jit(solution)/shard_map/attend/pallas_call | solution.py:44
  111.8 3.8 %collective-permute-done.21.refs_1_ = bf16[512,128]{1,0:T(8,128)(2,1)S(1)} collective-permute-done((bf16[512,128]{1,0:T(8,128)(2,1)S(1)}, bf16[512,128]{1,0:T(8,128)(2,1)S(1)}, u32[]{:S(2)}, u32[]{:S(2)}) %collective-permute-start.21) | collective-permute-done | bytes 131104 | tf_op jit(solution)/shard_map/ppermute | solution.py:733
  119.1 3.1 %collective-permute-done.31.refs_4_ = bf16[512,128]{1,0:T(8,128)(2,1)S(1)} collective-permute-done((bf16[512,128]{1,0:T(8,128)(2,1)S(1)}, bf16[512,128]{1,0:T(8,128)(2,1)S(1)}, u32[]{:S(2)}, u32[]{:S(2)}) %collective-permute-start.31) | collective-permute-done | bytes 131104 | tf_op jit(solution)/shard_map/ppermute | solution.py:710
  122.1 2.4 %output.3 = (f32[4,64,1152]{2,1,0:T(8,128)S(1)}, bf16[4,64,1152]{2,1,0:T(8,128)(2,1)S(1)}) custom-call(s32[4]{0:T(128)S(1)} %copy-done.7, bf16[512,128]{1,0:T(8,128)(2,1)S(1)} %get-tuple-element.98.refs_1_, bf16[512,128]{1,0:T(8,128)(2,1)S(1)} %collective-permute-done.29.refs_2_, bf16[512,128]{1,0:T(8,128)(2,1)S(1)} %collective-permute-done.30.refs_3_, ...), custom_call_target="tpu_custom_call" | custom-call | flops 9437184 | bytes 134144 | tf_op jit(solution)/shard_map/output/pallas_call | solution.py:44
  126.8 3.2 %collective-permute-start.33 = (bf16[4,64,1152]{2,1,0:T(8,128)(2,1)S(1)}, bf16[4,64,1152]{2,1,0:T(8,128)(2,1)S(1)}, u32[]{:S(2)}, u32[]{:S(2)}) collective-permute-start(bf16[4,64,1152]{2,1,0:T(8,128)(2,1)S(1)} %fold.2), channel_id=1, source_target_pairs={{0,2},{1,0},{2,3},{3,1},{4,6},{5,4},{6,7},{7,5},{8,10},{9,8},{10,1... | collective-permute-start | bytes 1769480 | tf_op jit(solution)/shard_map/ppermute | solution.py:731
  130.0 2.5 %collective-permute-done.24.refs_3_ = bf16[512,384]{1,0:T(8,128)(2,1)S(1)} collective-permute-done((bf16[512,384]{1,0:T(8,128)(2,1)S(1)}, bf16[512,384]{1,0:T(8,128)(2,1)S(1)}, u32[]{:S(2)}, u32[]{:S(2)}) %collective-permute-start.24) | collective-permute-done | bytes 393248 | tf_op jit(solution)/shard_map/ppermute | solution.py:709
  132.4 4.2 %collective-permute-done.25.refs_4_ = bf16[512,384]{1,0:T(8,128)(2,1)S(1)} collective-permute-done((bf16[512,384]{1,0:T(8,128)(2,1)S(1)}, bf16[512,384]{1,0:T(8,128)(2,1)S(1)}, u32[]{:S(2)}, u32[]{:S(2)}) %collective-permute-start.25) | collective-permute-done | bytes 393248 | tf_op jit(solution)/shard_map/ppermute | solution.py:710
  136.6 4.0 %output.2 = (f32[4,64,1152]{2,1,0:T(8,128)S(1)}, bf16[4,64,1152]{2,1,0:T(8,128)(2,1)S(1)}) custom-call(s32[4]{0:T(128)S(1)} %copy-done.7, bf16[512,384]{1,0:T(8,128)(2,1)S(1)} %beside.1.refs_1_, bf16[512,384]{1,0:T(8,128)(2,1)S(1)} %collective-permute-done.23.refs_2_, bf16[512,384]{1,0:T(8,128)(2,1)S(1)} %collective-permute-done.24.refs_3_, ...), custom_call_target="tpu_custom_call" | custom-call | flops 28311552 | bytes 134144 | tf_op jit(solution)/shard_map/output/pallas_call | solution.py:44
  146.6 3.2 %collective-permute-done.34 = bf16[64,1152]{1,0:T(8,128)(2,1)S(1)} collective-permute-done((bf16[64,1152]{1,0:T(8,128)(2,1)S(1)}, bf16[64,1152]{1,0:T(8,128)(2,1)S(1)}, u32[]{:S(2)}, u32[]{:S(2)}) %collective-permute-start.34) | collective-permute-done | bytes 147488 | tf_op jit(solution)/shard_map/ppermute | solution.py:739
  149.8 2.9 %collective-permute-done.35 = bf16[64,1152]{1,0:T(8,128)(2,1)S(1)} collective-permute-done((bf16[64,1152]{1,0:T(8,128)(2,1)S(1)}, bf16[64,1152]{1,0:T(8,128)(2,1)S(1)}, u32[]{:S(2)}, u32[]{:S(2)}) %collective-permute-start.35) | collective-permute-done | bytes 147488 | tf_op jit(solution)/shard_map/ppermute | solution.py:739
  153.2 2.4 %collective-permute-start.37 = (bf16[64,1152]{1,0:T(8,128)(2,1)S(1)}, bf16[64,1152]{1,0:T(8,128)(2,1)S(1)}, u32[]{:S(2)}, u32[]{:S(2)}) collective-permute-start(bf16[64,1152]{1,0:T(8,128)(2,1)S(1)} %get-tuple-element.103), channel_id=1, source_target_pairs={{0,1},{1,2},{2,3},{3,0},{4,5},{5,6},{6,7},{7,4},{8,9},{9,10},{10,1... | collective-permute-start | bytes 442376 | tf_op jit(solution)/shard_map/ppermute | solution.py:748
  156.8 2.8 %collective-permute-start.39 = (bf16[64,1152]{1,0:T(8,128)(2,1)S(1)}, bf16[64,1152]{1,0:T(8,128)(2,1)S(1)}, u32[]{:S(2)}, u32[]{:S(2)}) collective-permute-start(bf16[64,1152]{1,0:T(8,128)(2,1)S(1)} %get-tuple-element.101), channel_id=1, source_target_pairs={{0,3},{1,0},{2,1},{3,2},{4,7},{5,4},{6,5},{7,6},{8,11},{9,8},{10,9... | collective-permute-start | bytes 442376 | tf_op jit(solution)/shard_map/ppermute | solution.py:748
  161.9 4.7 %collective-permute-done.38.refs_4_ = bf16[64,1152]{1,0:T(8,128)(2,1)S(1)} collective-permute-done((bf16[64,1152]{1,0:T(8,128)(2,1)S(1)}, bf16[64,1152]{1,0:T(8,128)(2,1)S(1)}, u32[]{:S(2)}, u32[]{:S(2)}) %collective-permute-start.38) | collective-permute-done | bytes 147488 | tf_op jit(solution)/shard_map/ppermute | solution.py:748
  (124 shorter events, 53.5 us)
Async XLA Ops:
  9.0 30.4 %collective-permute-start.3 = (bf16[576,2560]{1,0:T(8,128)(2,1)}, bf16[576,2560]{1,0:T(8,128)(2,1)}, u32[]{:S(2)}, u32[]{:S(2)}) collective-permute-start(bf16[576,2560]{1,0:T(8,128)(2,1)} %get-tuple-element.58), channel_id=1, source_target_pairs={{0,4},{4,0},{8,12},{12,8},{16,20},{20,16},{24,28},{28,24},{1,5},{5... | collective-permute-start | bytes 8847368 | tf_op jit(solution)/shard_map/ppermute | solution.py:674
  9.5 23.1 %collective-permute-start = (bf16[512,1152]{1,0:T(8,128)(2,1)S(1)}, bf16[512,1152]{1,0:T(8,128)(2,1)S(1)}, u32[]{:S(2)}, u32[]{:S(2)}) collective-permute-start(bf16[512,1152]{1,0:T(8,128)(2,1)S(1)} %copy-done.13), channel_id=1, source_target_pairs={{0,8},{4,20},{8,0},{12,28},{16,24},{20,4},{24,16},{28,12},{1,9},{5... | collective-permute-start | bytes 3538952 | tf_op jit(solution)/shard_map/ppermute | solution.py:665
  12.1 8.0 %collective-permute-start.4 = (bf16[192,576]{1,0:T(8,128)(2,1)S(1)}, bf16[192,576]{1,0:T(8,128)(2,1)S(1)}, u32[]{:S(2)}, u32[]{:S(2)}) collective-permute-start(bf16[192,576]{1,0:T(8,128)(2,1)S(1)} %bitcast.31), channel_id=1, source_target_pairs={{0,1},{1,0},{2,3},{3,2},{4,5},{5,4},{6,7},{7,6},{8,9},{9,8},{10,11... | collective-permute-start | bytes 663560 | tf_op jit(solution)/shard_map/ppermute | solution.py:662
  13.7 32.5 %collective-permute-start.2 = (bf16[256,1152]{1,0:T(8,128)(2,1)}, bf16[256,1152]{1,0:T(8,128)(2,1)S(1)}, u32[]{:S(2)}, u32[]{:S(2)}) collective-permute-start(bf16[256,1152]{1,0:T(8,128)(2,1)} %get-tuple-element.54), channel_id=1, source_target_pairs={{0,16},{4,12},{8,24},{12,4},{16,0},{20,28},{24,8},{28,20},{1,17},{... | collective-permute-start | bytes 1769480 | tf_op jit(solution)/shard_map/ppermute | solution.py:666
  23.7 20.3 %collective-permute-start.5 = (bf16[256,576]{1,0:T(8,128)(2,1)}, bf16[256,576]{1,0:T(8,128)(2,1)S(1)}, u32[]{:S(2)}, u32[]{:S(2)}) collective-permute-start(bf16[256,576]{1,0:T(8,128)(2,1)} %pick.1.refs_3_), channel_id=1, source_target_pairs={{0,2},{1,3},{2,0},{3,1},{4,6},{5,7},{6,4},{7,5},{8,10},{9,11},{10,... | collective-permute-start | bytes 884744 | tf_op jit(solution)/shard_map/ppermute | solution.py:675
  32.7 13.4 %collective-permute-start.1 = (bf16[256,1152]{1,0:T(8,128)(2,1)S(1)}, bf16[256,1152]{1,0:T(8,128)(2,1)S(1)}, u32[]{:S(2)}, u32[]{:S(2)}) collective-permute-start(bf16[256,1152]{1,0:T(8,128)(2,1)S(1)} %slice.13), channel_id=1, source_target_pairs={{0,16},{4,12},{8,24},{12,4},{16,0},{20,28},{24,8},{28,20},{1,17},{... | collective-permute-start | bytes 1769480 | tf_op jit(solution)/shard_map/ppermute | solution.py:667
  41.8 30.5 %collective-permute-start.11 = (bf16[1216,512]{1,0:T(8,128)(2,1)S(1)}, bf16[1216,512]{1,0:T(8,128)(2,1)S(1)}, u32[]{:S(2)}, u32[]{:S(2)}) collective-permute-start(bf16[1216,512]{1,0:T(8,128)(2,1)S(1)} %get-tuple-element.69.refs_5_), channel_id=1, source_target_pairs={{0,1},{1,3},{2,0},{3,2},{4,5},{5,7},{6,4},{7,6},{8,9},{9,11},{10,8... | collective-permute-start | bytes 3735560 | tf_op jit(solution)/shard_map/ppermute | solution.py:680
  49.0 12.6 %collective-permute-start.7 = (bf16[256,1024]{1,0:T(8,128)(2,1)S(1)}, bf16[256,1024]{1,0:T(8,128)(2,1)S(1)}, u32[]{:S(2)}, u32[]{:S(2)}) collective-permute-start(bf16[256,1024]{1,0:T(8,128)(2,1)S(1)} %get-tuple-element.61.refs_0_), channel_id=1, source_target_pairs={{0,8},{4,20},{8,0},{12,28},{16,24},{20,4},{24,16},{28,12},{1,9},{5... | collective-permute-start | bytes 1572872 | tf_op jit(solution)/shard_map/ppermute | solution.py:690
  53.5 11.5 %collective-permute-start.8 = (bf16[256,1024]{1,0:T(8,128)(2,1)S(1)}, bf16[256,1024]{1,0:T(8,128)(2,1)S(1)}, u32[]{:S(2)}, u32[]{:S(2)}) collective-permute-start(bf16[256,1024]{1,0:T(8,128)(2,1)S(1)} %get-tuple-element.62.refs_0_), channel_id=1, source_target_pairs={{0,8},{4,20},{8,0},{12,28},{16,24},{20,4},{24,16},{28,12},{1,9},{5... | collective-permute-start | bytes 1572872 | tf_op jit(solution)/shard_map/ppermute | solution.py:690
  57.1 15.2 %collective-permute-start.10 = (bf16[256,1024]{1,0:T(8,128)(2,1)S(1)}, bf16[256,1024]{1,0:T(8,128)(2,1)S(1)}, u32[]{:S(2)}, u32[]{:S(2)}) collective-permute-start(bf16[256,1024]{1,0:T(8,128)(2,1)S(1)} %get-tuple-element.63.refs_0_), channel_id=1, source_target_pairs={{0,8},{4,20},{8,0},{12,28},{16,24},{20,4},{24,16},{28,12},{1,9},{5... | collective-permute-start | bytes 1572872 | tf_op jit(solution)/shard_map/ppermute | solution.py:690
  61.6 9.3 %collective-permute-start.9 = (bf16[256,512]{1,0:T(8,128)(2,1)S(1)}, bf16[256,512]{1,0:T(8,128)(2,1)S(1)}, u32[]{:S(2)}, u32[]{:S(2)}) collective-permute-start(bf16[256,512]{1,0:T(8,128)(2,1)S(1)} %onward.4.refs_0_), channel_id=1, source_target_pairs={{0,16},{4,12},{8,24},{12,4},{16,0},{20,28},{24,8},{28,20},{1,17},{... | collective-permute-start | bytes 786440 | tf_op jit(solution)/shard_map/ppermute | solution.py:695
  72.4 29.5 %collective-permute-start.20 = (bf16[1216,512]{1,0:T(8,128)(2,1)S(1)}, bf16[1216,512]{1,0:T(8,128)(2,1)S(1)}, u32[]{:S(2)}, u32[]{:S(2)}) collective-permute-start(bf16[1216,512]{1,0:T(8,128)(2,1)S(1)} %get-tuple-element.91.refs_6_), channel_id=1, source_target_pairs={{0,1},{1,3},{2,0},{3,2},{4,5},{5,7},{6,4},{7,6},{8,9},{9,11},{10,8... | collective-permute-start | bytes 3735560 | tf_op jit(solution)/shard_map/ppermute | solution.py:720
  75.1 13.2 %collective-permute-start.14 = (bf16[256,1024]{1,0:T(8,128)(2,1)S(1)}, bf16[256,1024]{1,0:T(8,128)(2,1)S(1)}, u32[]{:S(2)}, u32[]{:S(2)}) collective-permute-start(bf16[256,1024]{1,0:T(8,128)(2,1)S(1)} %get-tuple-element.64.refs_0_), channel_id=1, source_target_pairs={{0,8},{4,20},{8,0},{12,28},{16,24},{20,4},{24,16},{28,12},{1,9},{5... | collective-permute-start | bytes 1572872 | tf_op jit(solution)/shard_map/ppermute | solution.py:690
  76.6 8.5 %collective-permute-start.12 = (bf16[256,512]{1,0:T(8,128)(2,1)S(1)}, bf16[256,512]{1,0:T(8,128)(2,1)S(1)}, u32[]{:S(2)}, u32[]{:S(2)}) collective-permute-start(bf16[256,512]{1,0:T(8,128)(2,1)S(1)} %onward.5.refs_0_), channel_id=1, source_target_pairs={{0,16},{4,12},{8,24},{12,4},{16,0},{20,28},{24,8},{28,20},{1,17},{... | collective-permute-start | bytes 786440 | tf_op jit(solution)/shard_map/ppermute | solution.py:695
  77.1 13.4 %collective-permute-start.15 = (bf16[256,512]{1,0:T(8,128)(2,1)S(1)}, bf16[256,512]{1,0:T(8,128)(2,1)S(1)}, u32[]{:S(2)}, u32[]{:S(2)}) collective-permute-start(bf16[256,512]{1,0:T(8,128)(2,1)S(1)} %get-tuple-element.70.refs_0_), channel_id=1, source_target_pairs={{0,16},{4,12},{8,24},{12,4},{16,0},{20,28},{24,8},{28,20},{1,17},{... | collective-permute-start | bytes 786440 | tf_op jit(solution)/shard_map/ppermute | solution.py:695
  78.6 6.7 %collective-permute-start.13 = (bf16[256,384]{1,0:T(8,128)(2,1)S(1)}, bf16[256,384]{1,0:T(8,128)(2,1)S(1)}, u32[]{:S(2)}, u32[]{:S(2)}) collective-permute-start(bf16[256,384]{1,0:T(8,128)(2,1)S(1)} %get-tuple-element.72), channel_id=1, source_target_pairs={{0,4},{4,0},{8,12},{12,8},{16,20},{20,16},{24,28},{28,24},{1,5},{5... | collective-permute-start | bytes 589832 | tf_op jit(solution)/shard_map/ppermute | solution.py:701
  88.4 10.4 %collective-permute-start.18 = (bf16[256,512]{1,0:T(8,128)(2,1)S(1)}, bf16[256,512]{1,0:T(8,128)(2,1)S(1)}, u32[]{:S(2)}, u32[]{:S(2)}) collective-permute-start(bf16[256,512]{1,0:T(8,128)(2,1)S(1)} %onward.7.refs_0_), channel_id=1, source_target_pairs={{0,16},{4,12},{8,24},{12,4},{16,0},{20,28},{24,8},{28,20},{1,17},{... | collective-permute-start | bytes 786440 | tf_op jit(solution)/shard_map/ppermute | solution.py:695
  106.1 9.5 %collective-permute-start.21 = (bf16[512,128]{1,0:T(8,128)(2,1)S(1)}, bf16[512,128]{1,0:T(8,128)(2,1)S(1)}, u32[]{:S(2)}, u32[]{:S(2)}) collective-permute-start(bf16[512,128]{1,0:T(8,128)(2,1)S(1)} %get-tuple-element.93), channel_id=1, source_target_pairs={{0,1},{1,3},{2,0},{3,2},{4,5},{5,7},{6,4},{7,6},{8,9},{9,11},{10,8... | collective-permute-start | bytes 393224 | tf_op jit(solution)/shard_map/ppermute | solution.py:733
  107.9 7.6 %collective-permute-start.22 = (bf16[512,128]{1,0:T(8,128)(2,1)S(1)}, bf16[512,128]{1,0:T(8,128)(2,1)S(1)}, u32[]{:S(2)}, u32[]{:S(2)}) collective-permute-start(bf16[512,128]{1,0:T(8,128)(2,1)S(1)} %get-tuple-element.94), channel_id=1, source_target_pairs={{0,3},{1,2},{2,1},{3,0},{4,7},{5,6},{6,5},{7,4},{8,11},{9,10},{10,... | collective-permute-start | bytes 393224 | tf_op jit(solution)/shard_map/ppermute | solution.py:733
  108.8 8.4 %collective-permute-start.29 = (bf16[512,128]{1,0:T(8,128)(2,1)S(1)}, bf16[512,128]{1,0:T(8,128)(2,1)S(1)}, u32[]{:S(2)}, u32[]{:S(2)}) collective-permute-start(bf16[512,128]{1,0:T(8,128)(2,1)S(1)} %get-tuple-element.98.refs_1_), channel_id=1, source_target_pairs={{0,8},{4,20},{8,0},{12,28},{16,24},{20,4},{24,16},{28,12},{1,9},{5... | collective-permute-start | bytes 393224 | tf_op jit(solution)/shard_map/ppermute | solution.py:708
  110.3 7.3 %collective-permute-start.26 = (bf16[64,576]{1,0:T(8,128)(2,1)S(1)}, bf16[64,576]{1,0:T(8,128)(2,1)S(1)}, u32[]{:S(2)}, u32[]{:S(2)}) collective-permute-start(bf16[64,576]{1,0:T(8,128)(2,1)S(1)} %slice.15), channel_id=1, source_target_pairs={{0,1},{1,0},{2,3},{3,2},{4,5},{5,4},{6,7},{7,6},{8,9},{9,8},{10,11... | collective-permute-start | bytes 221192 | tf_op jit(solution)/shard_map/ppermute | solution.py:678
  111.3 7.8 %collective-permute-start.30 = (bf16[512,128]{1,0:T(8,128)(2,1)S(1)}, bf16[512,128]{1,0:T(8,128)(2,1)S(1)}, u32[]{:S(2)}, u32[]{:S(2)}) collective-permute-start(bf16[512,128]{1,0:T(8,128)(2,1)S(1)} %get-tuple-element.98.refs_1_), channel_id=1, source_target_pairs={{0,16},{4,12},{8,24},{12,4},{16,0},{20,28},{24,8},{28,20},{1,17},{... | collective-permute-start | bytes 393224 | tf_op jit(solution)/shard_map/ppermute | solution.py:709
  115.6 9.4 %collective-permute-start.23 = (bf16[512,384]{1,0:T(8,128)(2,1)S(1)}, bf16[512,384]{1,0:T(8,128)(2,1)S(1)}, u32[]{:S(2)}, u32[]{:S(2)}) collective-permute-start(bf16[512,384]{1,0:T(8,128)(2,1)S(1)} %beside.1.refs_1_), channel_id=1, source_target_pairs={{0,8},{4,20},{8,0},{12,28},{16,24},{20,4},{24,16},{28,12},{1,9},{5... | collective-permute-start | bytes 1179656 | tf_op jit(solution)/shard_map/ppermute | solution.py:708
  124.6 7.8 %collective-permute-start.24 = (bf16[512,384]{1,0:T(8,128)(2,1)S(1)}, bf16[512,384]{1,0:T(8,128)(2,1)S(1)}, u32[]{:S(2)}, u32[]{:S(2)}) collective-permute-start(bf16[512,384]{1,0:T(8,128)(2,1)S(1)} %beside.1.refs_1_), channel_id=1, source_target_pairs={{0,16},{4,12},{8,24},{12,4},{16,0},{20,28},{24,8},{28,20},{1,17},{... | collective-permute-start | bytes 1179656 | tf_op jit(solution)/shard_map/ppermute | solution.py:709
  125.1 11.6 %collective-permute-start.25 = (bf16[512,384]{1,0:T(8,128)(2,1)S(1)}, bf16[512,384]{1,0:T(8,128)(2,1)S(1)}, u32[]{:S(2)}, u32[]{:S(2)}) collective-permute-start(bf16[512,384]{1,0:T(8,128)(2,1)S(1)} %collective-permute-done.23.refs_2_), channel_id=1, source_target_pairs={{0,16},{4,12},{8,24},{12,4},{16,0},{20,28},{24,8},{28,20},{1,17},{... | collective-permute-start | bytes 1179656 | tf_op jit(solution)/shard_map/ppermute | solution.py:710
  126.8 16.0 %collective-permute-start.33 = (bf16[4,64,1152]{2,1,0:T(8,128)(2,1)S(1)}, bf16[4,64,1152]{2,1,0:T(8,128)(2,1)S(1)}, u32[]{:S(2)}, u32[]{:S(2)}) collective-permute-start(bf16[4,64,1152]{2,1,0:T(8,128)(2,1)S(1)} %fold.2), channel_id=1, source_target_pairs={{0,2},{1,0},{2,3},{3,1},{4,6},{5,4},{6,7},{7,5},{8,10},{9,8},{10,1... | collective-permute-start | bytes 1769480 | tf_op jit(solution)/shard_map/ppermute | solution.py:731
  143.0 6.8 %collective-permute-start.34 = (bf16[64,1152]{1,0:T(8,128)(2,1)S(1)}, bf16[64,1152]{1,0:T(8,128)(2,1)S(1)}, u32[]{:S(2)}, u32[]{:S(2)}) collective-permute-start(bf16[64,1152]{1,0:T(8,128)(2,1)S(1)} %get-tuple-element.108), channel_id=1, source_target_pairs={{0,8},{4,12},{8,0},{12,4},{16,24},{20,28},{24,16},{28,20},{1,9},{5... | collective-permute-start | bytes 442376 | tf_op jit(solution)/shard_map/ppermute | solution.py:739
  144.5 8.2 %collective-permute-start.35 = (bf16[64,1152]{1,0:T(8,128)(2,1)S(1)}, bf16[64,1152]{1,0:T(8,128)(2,1)S(1)}, u32[]{:S(2)}, u32[]{:S(2)}) collective-permute-start(bf16[64,1152]{1,0:T(8,128)(2,1)S(1)} %get-tuple-element.107), channel_id=1, source_target_pairs={{0,16},{4,20},{8,24},{12,28},{16,0},{20,4},{24,8},{28,12},{1,17},{... | collective-permute-start | bytes 442376 | tf_op jit(solution)/shard_map/ppermute | solution.py:739
  145.1 7.6 %collective-permute-start.36 = (bf16[64,1152]{1,0:T(8,128)(2,1)S(1)}, bf16[64,1152]{1,0:T(8,128)(2,1)S(1)}, u32[]{:S(2)}, u32[]{:S(2)}) collective-permute-start(bf16[64,1152]{1,0:T(8,128)(2,1)S(1)} %get-tuple-element.106), channel_id=1, source_target_pairs={{0,24},{4,28},{8,16},{12,20},{16,8},{20,12},{24,0},{28,4},{1,25},{... | collective-permute-start | bytes 442376 | tf_op jit(solution)/shard_map/ppermute | solution.py:739
  153.2 8.6 %collective-permute-start.37 = (bf16[64,1152]{1,0:T(8,128)(2,1)S(1)}, bf16[64,1152]{1,0:T(8,128)(2,1)S(1)}, u32[]{:S(2)}, u32[]{:S(2)}) collective-permute-start(bf16[64,1152]{1,0:T(8,128)(2,1)S(1)} %get-tuple-element.103), channel_id=1, source_target_pairs={{0,1},{1,2},{2,3},{3,0},{4,5},{5,6},{6,7},{7,4},{8,9},{9,10},{10,1... | collective-permute-start | bytes 442376 | tf_op jit(solution)/shard_map/ppermute | solution.py:748
  155.6 11.0 %collective-permute-start.38 = (bf16[64,1152]{1,0:T(8,128)(2,1)S(1)}, bf16[64,1152]{1,0:T(8,128)(2,1)S(1)}, u32[]{:S(2)}, u32[]{:S(2)}) collective-permute-start(bf16[64,1152]{1,0:T(8,128)(2,1)S(1)} %get-tuple-element.102), channel_id=1, source_target_pairs={{0,2},{1,3},{2,0},{3,1},{4,6},{5,7},{6,4},{7,5},{8,10},{9,11},{10,... | collective-permute-start | bytes 442376 | tf_op jit(solution)/shard_map/ppermute | solution.py:748
  156.8 9.8 %collective-permute-start.39 = (bf16[64,1152]{1,0:T(8,128)(2,1)S(1)}, bf16[64,1152]{1,0:T(8,128)(2,1)S(1)}, u32[]{:S(2)}, u32[]{:S(2)}) collective-permute-start(bf16[64,1152]{1,0:T(8,128)(2,1)S(1)} %get-tuple-element.101), channel_id=1, source_target_pairs={{0,3},{1,0},{2,1},{3,2},{4,7},{5,4},{6,5},{7,6},{8,11},{9,8},{10,9... | collective-permute-start | bytes 442376 | tf_op jit(solution)/shard_map/ppermute | solution.py:748
  (22 other events, 94.2 us)

commit v4 on v3

--- a/solution.py
+++ b/solution.py
@@ -17,7 +17,10 @@
 score_scale = 1.0 / 12.0
 
 CHIPS = 4
-CHUNKS = 4
+CHUNKS = 2
+SPAN = CHIPS // CHUNKS
+STEP = 256
+LOG2E = 1.4426950408889634
 F32 = jnp.float32
 BF16 = jnp.bfloat16
 SMEM = pl.BlockSpec(memory_space=pltpu.SMEM)
@@ -48,7 +51,7 @@
         scratch_shapes=list(scratch),
         name=name,
         compiler_params=pltpu.CompilerParams(vmem_limit_bytes=grant * 1024 * 1024),
-        cost_estimate=pl.CostEstimate(flops=flops // 64, bytes_accessed=moved // 64, transcendentals=transcendentals // 64),
+        cost_estimate=pl.CostEstimate(flops=flops, bytes_accessed=moved, transcendentals=transcendentals),
         **more,
     )(*after, *operands)
 
@@ -82,27 +85,33 @@
 
 
 def norm_kernel(steps, x_hbm, gain_ref, *refs):
-    (first_ref, second_ref, own_ref), (x_ref, y_ref, sems) = refs[:3], refs[3:]
+    (first_ref, second_ref, own_ref), (x_ref, y_ref, in_sems, out_sems) = refs[:3], refs[3:]
     me = lax.axis_index("wide")
     chip, core = lax.shift_right_logical(me, 1), me & 1
     depth = own_ref.shape[1]
     rows = x_ref.shape[0]
     step = rows // steps
-    copies = [
-        pltpu.make_async_copy(x_hbm.at[pl.ds(i * step, step), :], x_ref.at[pl.ds(i * step, step), :], sems.at[i])
+    loads = [
+        pltpu.make_async_copy(x_hbm.at[pl.ds(i * step, step), :], x_ref.at[pl.ds(i * step, step), :], in_sems.at[i])
         for i in range(steps)
     ]
-    for copy in copies:
-        copy.start()
+    for load in loads:
+        load.start()
     gain = gain_ref[...].astype(F32).reshape(1, -1)
+    copies = []
     for i in range(steps):
-        copies[i].wait()
+        loads[i].wait()
         at = i * step
         x = x_ref[at : at + step, :].astype(F32)
         scale = lax.rsqrt(jnp.sum(x * x, axis=1, keepdims=True) / x.shape[1] + epsilon)
-        y_ref[...] = (x * scale * gain).astype(BF16)
+        y_ref[at : at + step, :] = (x * scale * gain).astype(BF16)
         for to, out, base in zip(order(chip, core), (first_ref, first_ref, second_ref, own_ref), (0, rows, 0, 0)):
-            out[base + at : base + at + step, :] = y_ref[:, pl.ds(pl.multiple_of(to * depth, 128), depth)]
+            source = y_ref.at[pl.ds(at, step), pl.ds(pl.multiple_of(to * depth, 128), depth)]
+            target = out.at[pl.ds(base + at, step), :]
+            copies.append(pltpu.make_async_copy(source, target, out_sems.at[len(copies)]))
+            copies[-1].start()
+    for copy in copies:
+        copy.wait()
 
 
 def norm(x, gain, steps, after):
@@ -114,14 +123,15 @@
         (jax.ShapeDtypeStruct((2 * rows, depth), x.dtype), shape, shape), after,
         scratch=[
             pltpu.VMEM((rows, cols), BF16),
-            pltpu.VMEM((rows // steps, cols), BF16),
+            pltpu.VMEM((rows, cols), BF16),
             pltpu.SemaphoreType.DMA((steps,)),
+            pltpu.SemaphoreType.DMA((4 * steps,)),
         ],
-        out_specs=(VMEM,) * 3, name="norm", grant=60, flops=x.size * 4, moved=x.size * 4,
-    )
-
-
-def arrange_kernel(q_hbm, k_hbm, v_hbm, o_hbm, mine_ref, theirs_ref, q_ref, k_ref, v_ref, o_ref, in_sems, sems):
+        out_specs=(ANY,) * 3, name="norm", grant=60, flops=x.size * 4, moved=x.size * 4,
+    )
+
+
+def arrange_kernel(q_hbm, k_hbm, v_hbm, o_hbm, theirs_ref, q_ref, k_ref, v_ref, o_ref, in_sems, sems):
     me = lax.axis_index("wide")
     chip, own = lax.shift_right_logical(me, 1), me & 1
     d = HEAD_DIM
@@ -134,32 +144,49 @@
     for one in loads:
         one.start()
     copies = []
-
-    def copy(ref, at, out, to, width):
-        source = ref.at[:, pl.ds(pl.multiple_of(at, d), width)]
-        copies.append(pltpu.make_async_copy(source, out.at[:, pl.ds(to, width)], sems.at[len(copies)]))
-        copies[-1].start()
-
-    for load, ref, width, at in zip(loads, (q_ref, k_ref, v_ref), (2 * d, d, d), (0, 2 * d, 3 * d)):
+    for load, ref, part in zip(loads, (q_ref, k_ref, v_ref, o_ref), range(4)):
         load.wait()
-        for core, out in ((1 - own, theirs_ref), (own, mine_ref)):
-            for place, to in enumerate(order(chip, core)):
-                copy(ref, to * width, out, 4 * place * d + at, width)
-    loads[3].wait()
-    for core, out in ((1 - own, theirs_ref), (own, mine_ref)):
-        for place, source in enumerate(near(chip, core)):
-            copy(o_ref, (2 * source + core) * d, out, (4 * CHIPS + place) * d, d)
+        for source, target in column_copies(ref, theirs_ref, part, chip, 1 - own):
+            copies.append(pltpu.make_async_copy(source, target, sems.at[len(copies)]))
+            copies[-1].start()
     for one in copies:
         one.wait()
 
 
+def column_copies(ref, out, part, chip, core):
+    d = HEAD_DIM
+    if part == 3:
+        pairs = [((2 * source + core) * d, (4 * CHIPS + place) * d) for place, source in enumerate(near(chip, core))]
+        width = d
+    else:
+        width, at = ((2 * d, 0), (d, 2 * d), (d, 3 * d))[part]
+        pairs = [(to * width, 4 * place * d + at) for place, to in enumerate(order(chip, core))]
+    return [
+        (ref.at[:, pl.ds(pl.multiple_of(a, d), width)], out.at[:, pl.ds(b, width)]) for a, b in pairs
+    ]
+
+
 def arrange(q, k, v, o, after):
-    shape = jax.ShapeDtypeStruct((q.shape[0], 5 * CHIPS * HEAD_DIM), BF16)
-    return call(
-        arrange_kernel, (q, k, v, o), [HBM] * 4, (shape, shape), after,
+    return call(
+        arrange_kernel, (q, k, v, o), [HBM] * 4,
+        jax.ShapeDtypeStruct((q.shape[0], 5 * CHIPS * HEAD_DIM), BF16), after,
         scratch=[pltpu.VMEM(x.shape, BF16) for x in (q, k, v, o)]
-        + [pltpu.SemaphoreType.DMA((4,)), pltpu.SemaphoreType.DMA((32,))],
-        out_specs=(ANY, ANY), name="arrange", grant=60, moved=q.size * 16,
+        + [pltpu.SemaphoreType.DMA((4,)), pltpu.SemaphoreType.DMA((16,))],
+        out_specs=ANY, name="arrange", grant=60, moved=q.size * 16,
+    )
+
+
+def lower_kernel(x_ref, out_ref, sem):
+    rows = out_ref.shape[0]
+    copy = pltpu.make_async_copy(x_ref.at[pl.ds(x_ref.shape[0] - rows, rows), :], out_ref, sem)
+    copy.start()
+    copy.wait()
+
+
+def lower(x, after):
+    return call(
+        lower_kernel, (x,), [ANY], jax.ShapeDtypeStruct((x.shape[0] // 2, x.shape[1]), x.dtype), after,
+        scratch=[pltpu.SemaphoreType.DMA(())], out_specs=ANY, name="lower", moved=x.size * 2,
     )
 
 
@@ -274,34 +301,45 @@
     )
 
 
-def stack_kernel(mine_ref, got_ref, down_ref, w_ref, ring_ref, sems):
-    core = lax.axis_index("wide") & 1
-    rows = mine_ref.shape[0]
+def stack_kernel(q_ref, k_ref, v_ref, o_ref, got_ref, down_ref, w_ref, ring_ref, sems):
+    me = lax.axis_index("wide")
+    chip, core = lax.shift_right_logical(me, 1), me & 1
+    rows = got_ref.shape[0]
     cols = w_ref.shape[1]
     width = ring_ref.shape[1]
     copies = []
-    for i, (ref, at) in enumerate(((mine_ref, core), (got_ref, 1 - core))):
-        to = pl.ds(pl.multiple_of(at * rows, 16), rows)
-        copies.append(pltpu.make_async_copy(ref.at[:, pl.ds(cols, width)], ring_ref.at[to, :], sems.at[2 * i]))
-        copies.append(pltpu.make_async_copy(ref.at[:, pl.ds(0, cols)], w_ref.at[to, :], sems.at[2 * i + 1]))
-    copies.append(pltpu.make_async_copy(down_ref, ring_ref.at[pl.ds(2 * rows, down_ref.shape[0]), :], sems.at[4]))
-    for copy in copies:
-        copy.start()
-    for copy in copies:
-        copy.wait()
-
-
-def stack(mine, got, down, after):
-    rows, cols = mine.shape
+
+    def copy(source, target):
+        copies.append(pltpu.make_async_copy(source, target, sems.at[len(copies)]))
+        copies[-1].start()
+
+    mine = pl.ds(pl.multiple_of(core * rows, 16), rows)
+    theirs = pl.ds(pl.multiple_of((1 - core) * rows, 16), rows)
+    for part, ref in enumerate((q_ref, k_ref, v_ref)):
+        for source, target in column_copies(ref, w_ref.at[mine, :], part, chip, core):
+            copy(source, target)
+    d = HEAD_DIM
+    for place, source in enumerate(near(chip, core)):
+        at = pl.multiple_of((2 * source + core) * d, d)
+        copy(o_ref.at[:, pl.ds(at, d)], ring_ref.at[mine, pl.ds(place * d, d)])
+    copy(got_ref.at[:, pl.ds(0, cols)], w_ref.at[theirs, :])
+    copy(got_ref.at[:, pl.ds(cols, width)], ring_ref.at[theirs, :])
+    copy(down_ref, ring_ref.at[pl.ds(2 * rows, down_ref.shape[0]), :])
+    for one in copies:
+        one.wait()
+
+
+def stack(q, k, v, o, got, down, after):
+    rows, cols = got.shape
     width = down.shape[1]
     return call(
-        stack_kernel, (mine, got, down), [ANY] * 3,
+        stack_kernel, (q, k, v, o, got, down), [ANY] * 6,
         (
-            jax.ShapeDtypeStruct((2 * rows, cols - width), mine.dtype),
-            jax.ShapeDtypeStruct((2 * rows + down.shape[0], width), mine.dtype),
+            jax.ShapeDtypeStruct((2 * rows, cols - width), got.dtype),
+            jax.ShapeDtypeStruct((2 * rows + down.shape[0], width), got.dtype),
         ),
         after,
-        scratch=[pltpu.SemaphoreType.DMA((5,))], out_specs=(ANY, ANY), name="stack", moved=rows * cols * 8,
+        scratch=[pltpu.SemaphoreType.DMA((19,))], out_specs=(ANY, ANY), name="stack", moved=rows * cols * 8,
     )
 
 
@@ -329,20 +367,26 @@
     chip = lax.shift_right_logical(me, 1)
     core = me & 1
     rows = x_ref.shape[0]
+    tok = rows // SPAN
     half = send_ref.shape[1]
     n_codes = prompts * RANK
-    for k, held in enumerate((chip ^ (1 + core), chip ^ 3, chip ^ (2 - core), chip)):
-
-        @pl.when(held == chunk)
-        def _():
-            pltpu.make_async_copy(x_refs[k].at[pl.ds(0, rows), :], x_ref, sem).start()
-
-    pltpu.make_async_copy(x_refs[3], x_ref, sem).wait()
+    for i in range(SPAN):
+        for k, held in enumerate((chip ^ (1 + core), chip ^ 3, chip ^ (2 - core), chip)):
+
+            @pl.when(held == SPAN * chunk + i)
+            def _():
+                pltpu.make_async_copy(
+                    x_refs[k].at[pl.ds(0, tok), :], x_ref.at[pl.ds(i * tok, tok), :], sem.at[i]
+                ).start()
+
+    for i in range(SPAN):
+        pltpu.make_async_copy(x_refs[3], x_ref.at[pl.ds(i * tok, tok), :], sem.at[i]).wait()
     x = x_ref[...]
     codes = lax.dot_general(
         x, pack_ref[...], (((1,), (1,)), ((), ())), preferred_element_type=F32
     )
-    places = (2 * chunk + core) * rows + lax.broadcasted_iota(jnp.int32, (rows, 1), 0)
+    row = lax.broadcasted_iota(jnp.int32, (rows, 1), 0)
+    places = (2 * (SPAN * chunk + row // tok) + core) * tok + row % tok
     prompt, _ = prompt_of(places, lengths_ref, prompts)
     lane = lax.broadcasted_iota(jnp.int32, codes.shape, 1)
     owner = (lane % n_codes) // RANK
@@ -355,7 +399,7 @@
 
 
 def project(lengths, pieces, w, pack, up, chunk, after, carry=()):
-    rows, depth = pieces[3].shape
+    rows, depth = SPAN * pieces[3].shape[0], pieces[3].shape[1]
     half = w.shape[1] // 2
     n = len(after) + 8
     out = call(
@@ -365,7 +409,7 @@
         tuple(jax.ShapeDtypeStruct(c.shape, c.dtype) for c in carry)
         + (jax.ShapeDtypeStruct((rows, half), BF16), jax.ShapeDtypeStruct((rows, half), F32)),
         after,
-        scratch=[pltpu.VMEM((rows, depth), BF16), pltpu.SemaphoreType.DMA(())],
+        scratch=[pltpu.VMEM((rows, depth), BF16), pltpu.SemaphoreType.DMA((SPAN,))],
         out_specs=(ANY,) * len(carry) + (VMEM, VMEM), name="project",
         input_output_aliases={n + i: i for i in range(len(carry))},
         flops=2 * rows * depth * w.shape[1], moved=rows * depth * 2 + w.size * 2 + rows * half * 6,
@@ -393,34 +437,41 @@
     return out[-1], out[:-1]
 
 
-def finish_kernel(chunk, keep_ref, first_ref, second_ref, cos_ref, sin_ref, own_ref, send_ref):
-    rows = own_ref.shape[0]
+def finish_kernel(chunk, keep_ref, first_ref, second_ref, cos_ref, sin_ref, *refs):
+    own_ref, send_ref = refs[-2:]
+    tok = own_ref.shape[0] // SPAN
     d = HEAD_DIM
     own = keep_ref.shape[1] // 2
     core = lax.axis_index("wide") & 1
-    at = pl.ds(pl.multiple_of((2 * chunk + core) * rows, rows), rows)
-    cosine, sine = cos_ref[at, :], sin_ref[at, :]
-
-    def turned(x):
-        return x * cosine + pltpu.roll(x, d // 2, 1) * sine
-
-    total = keep_ref[:, own:] + first_ref[:, :own].astype(F32) + second_ref[...].astype(F32)
-    q0, q1, k = (turned(total[:, i * d : (i + 1) * d]) for i in range(3))
-    own_ref[:, :d] = jnp.where(core == 0, q0, q1).astype(BF16)
-    send_ref[:, :d] = jnp.where(core == 0, q1, q0).astype(BF16)
-    both = jnp.concatenate([k, total[:, 3 * d :]], axis=1).astype(BF16)
-    own_ref[:, d:] = both
-    send_ref[:, d:] = both
-
-
-def finish(keep, first, second, tables, chunk, after):
+    for i in range(SPAN):
+        at = pl.ds(pl.multiple_of((2 * (SPAN * chunk + i) + core) * tok, tok), tok)
+        rows = slice(i * tok, (i + 1) * tok)
+        cosine, sine = cos_ref[at, :], sin_ref[at, :]
+        total = keep_ref[rows, own:] + first_ref[rows, :own].astype(F32) + second_ref[rows, :].astype(F32)
+        q0, q1, k = (
+            x * cosine + pltpu.roll(x, d // 2, 1) * sine for x in (total[:, n * d : (n + 1) * d] for n in range(3))
+        )
+        q0, q1 = q0 * (score_scale * LOG2E), q1 * (score_scale * LOG2E)
+        own_ref[rows, :d] = jnp.where(core == 0, q0, q1).astype(BF16)
+        send_ref[rows, :d] = jnp.where(core == 0, q1, q0).astype(BF16)
+        both = jnp.concatenate([k, total[:, 3 * d :]], axis=1).astype(BF16)
+        own_ref[rows, d:] = both
+        send_ref[rows, d:] = both
+
+
+def finish(keep, first, second, tables, chunk, after, carry=()):
     rows = keep.shape[0]
     shape = jax.ShapeDtypeStruct((rows, 3 * HEAD_DIM), BF16)
-    return call(
+    n = len(after) + 5
+    out = call(
         functools.partial(finish_kernel, chunk),
-        (keep, first, second, *tables), [VMEM] * 5, (shape, shape), after,
-        out_specs=(VMEM, VMEM), name="finish", flops=rows * 2048, moved=rows * 8192,
-    )
+        (keep, first, second, *tables, *carry), [VMEM] * 5 + [ANY] * len(carry),
+        tuple(jax.ShapeDtypeStruct(c.shape, c.dtype) for c in carry) + (shape, shape), after,
+        out_specs=(ANY,) * len(carry) + (VMEM, VMEM), name="finish",
+        input_output_aliases={n + i: i for i in range(len(carry))},
+        flops=rows * 2048, moved=rows * 8192,
+    )
+    return out[-2], out[-1], out[:-2]
 
 
 def attend_kernel(chunk, prompts, n_before, n_carry, lengths_ref, sink_ref, *refs):
@@ -429,70 +480,90 @@
     befores = refs[2 * count : 2 * count + n_before]
     outs = refs[2 * count + n_before + 2 * n_carry :][:4]
     q_ref, k_ref, v_ref, out_ref = refs[-4:]
-    step = mine_refs[0].shape[0]
+    step = mine_refs[0].shape[0] // SPAN
     d = HEAD_DIM
     here, z = lax.axis_index("wide"), lax.axis_index("narrow")
     core = here & 1
-    for i in range(count):
-        mine, other = mine_refs[i][...], other_refs[i][...]
-        for half, block in enumerate((jnp.where(core == 0, mine, other), jnp.where(core == 0, other, mine))):
-            at = pl.ds((2 * i + half) * step, step)
-            k_ref[at, :] = block[:, d : 2 * d]
-            v_ref[at, :] = block[:, 2 * d :]
-            if i == chunk:
-                q_ref[half] = block[:, :d]
-    sink = sink_ref[here]
-    to = (z, plane(NEXT, z), 3 - z, plane(BEFORE, z))
-    part = step // 4
+    for c in range(count):
+        for i in range(SPAN):
+            mine, other = (refs_of[c][i * step : (i + 1) * step, :] for refs_of in (mine_refs, other_refs))
+            for half, block in enumerate((jnp.where(core == 0, mine, other), jnp.where(core == 0, other, mine))):
+                at = pl.ds((2 * (SPAN * c + i) + half) * step, step)
+                k_ref[at, :] = block[:, d : 2 * d]
+                v_ref[at, :] = block[:, 2 * d :]
+                if c == chunk:
+                    q_ref[(2 * i + half) * step : (2 * i + half + 1) * step, :] = block[:, :d]
     shift = 0
     for k in range(n_before):
         shift = befores[k].shape[0]
         outs[k][:shift, :] = befores[k][...]
-    for block in range(2):
-        base = (2 * chunk + block) * step
-        q = q_ref[block]
-        places = base + lax.broadcasted_iota(jnp.int32, (step, 1), 0)
-        _, starts = prompt_of(places, lengths_ref, prompts)
-        end = jnp.int32(0)
-        low = jnp.int32(0)
-        for p in range(prompts - 1):
-            end = end + lengths_ref[p]
-            low = jnp.where(base >= end, end, low)
-
-        def body(i, carry):
+    for i in range(SPAN):
+        attend_block(
+            SPAN * chunk + i, prompts, step, lengths_ref, sink_ref, q_ref.at[pl.ds(2 * i * step, 2 * step), :],
+            k_ref, v_ref, out_ref, outs, shift + i * step // 2,
+        )
+
+
+def attend_block(chip, prompts, step, lengths_ref, sink_ref, q_ref, k_ref, v_ref, out_ref, outs, shift):
+    d = HEAD_DIM
+    here, z = lax.axis_index("wide"), lax.axis_index("narrow")
+    top = sink_ref[here] * LOG2E
+    to = (z, plane(NEXT, z), 3 - z, plane(BEFORE, z))
+    part = step // 4
+    rows = 2 * step
+    base = chip * rows
+    q = q_ref[...]
+    places = base + lax.broadcasted_iota(jnp.int32, (rows, 1), 0)
+    _, starts = prompt_of(places, lengths_ref, prompts)
+    end = jnp.int32(0)
+    low = jnp.int32(0)
+    high = jnp.int32(0)
+    for p in range(prompts - 1):
+        end = end + lengths_ref[p]
+        low = jnp.where(base >= end, end, low)
+        high = jnp.where(base + rows > end, end, high)
+
+    def body(masked):
+        def one(i, carry):
             top, total, summed = carry
-            at = pl.multiple_of(i * step, step)
-            k = k_ref[pl.ds(at, step), :]
-            v = v_ref[pl.ds(at, step), :]
-            scores = lax.dot_general(q, k, (((1,), (1,)), ((), ())), preferred_element_type=F32) * score_scale
-            keys = at + lax.broadcasted_iota(jnp.int32, (step, step), 1)
-            allowed = jnp.logical_and(keys >= starts, keys <= places)
-            scores = jnp.where(allowed, scores, -1e30)
+            at = pl.multiple_of(i * STEP, STEP)
+            k = k_ref[pl.ds(at, STEP), :]
+            v = v_ref[pl.ds(at, STEP), :]
+            scores = lax.dot_general(q, k, (((1,), (1,)), ((), ())), preferred_element_type=F32)
+            if masked:
+                keys = at + lax.broadcasted_iota(jnp.int32, scores.shape, 1)
+                scores = jnp.where(jnp.logical_and(keys >= starts, keys <= places), scores, -1e30)
             fresh = jnp.maximum(top, jnp.max(scores, axis=1, keepdims=True))
-            factor = jnp.exp(top - fresh)
-            weights = jnp.exp(scores - fresh)
+            factor = jnp.exp2(top - fresh)
+            weights = jnp.exp2(scores - fresh)
             total = total * factor + jnp.sum(weights, axis=1, keepdims=True)
             summed = summed * factor + jnp.dot(weights.astype(BF16), v, preferred_element_type=F32)
             return fresh, total, summed
 
-        top = jnp.full((step, 1), sink, F32)
-        total = jnp.ones((step, 1), F32)
-        summed = jnp.zeros((step, d), F32)
-        top, total, summed = lax.fori_loop(
-            low // step, 2 * chunk + block + 1, body, (top, total, summed)
-        )
-        out_ref[...] = (summed / total).astype(BF16)
+        return one
+
+    carry = (jnp.full((rows, 1), top, F32), jnp.ones((rows, 1), F32), jnp.zeros((rows, d), F32))
+    first = low // STEP
+    last = base // STEP
+    whole = jnp.minimum((high + STEP - 1) // STEP, last)
+    carry = lax.fori_loop(first, whole, body(True), carry)
+    carry = lax.fori_loop(whole, last, body(False), carry)
+    for i in range(last, (base + rows) // STEP):
+        carry = body(True)(i, carry)
+    _, total, summed = carry
+    out_ref[...] = (summed / total).astype(BF16)
+    for block in range(2):
         for k in range(4):
-            at = pl.multiple_of(to[k] * part, part)
+            at = pl.multiple_of(block * step + to[k] * part, part)
             first = shift + block * part
             outs[k][first : first + part, :] = out_ref[pl.ds(at, part), :]
 
 
 def attend(lengths, sinks, mine, other, chunk, after, before=(), carry=()):
-    step = mine[0].shape[0]
+    step = mine[0].shape[0] // SPAN
     d = HEAD_DIM
     count = chunk + 1
-    rows = step // 2 + (before[0].shape[0] if before else 0)
+    rows = SPAN * step // 2 + (before[0].shape[0] if before else 0)
     n = len(after) + 2 + 2 * count + len(before)
     out = call(
         functools.partial(attend_kernel, chunk, lengths.shape[0], len(before), len(carry)),
@@ -501,12 +572,12 @@
         tuple(jax.ShapeDtypeStruct(c.shape, c.dtype) for c in carry)
         + (jax.ShapeDtypeStruct((rows, d), BF16),) * 4,
         after,
-        scratch=[pltpu.VMEM((2, step, d), BF16)]
-        + [pltpu.VMEM((2 * count * step, d), BF16)] * 2
-        + [pltpu.VMEM((step, d), BF16)],
+        scratch=[pltpu.VMEM((2 * SPAN * step, d), BF16)]
+        + [pltpu.VMEM((2 * SPAN * count * step, d), BF16)] * 2
+        + [pltpu.VMEM((2 * step, d), BF16)],
         out_specs=(ANY,) * len(carry) + (VMEM,) * 4, name="attend",
         input_output_aliases={n + i: i for i in range(len(carry))},
-        flops=2 * step * 768 * 4 * d, moved=step * d * 8 * count, transcendentals=2 * step * 768,
+        flops=2 * SPAN * step * 768 * 4 * d, moved=step * d * 8 * count, transcendentals=2 * SPAN * step * 768,
     )
     return out[len(carry) :], out[: len(carry)]
 
@@ -523,6 +594,19 @@
     return call(
         beside_kernel, parts, [VMEM] * len(parts), jax.ShapeDtypeStruct((rows, cols * len(parts)), BF16), after,
         out_specs=VMEM, name="beside", moved=rows * cols * len(parts) * 4,
+    )
+
+
+def hold_kernel(*refs):
+    pass
+
+
+def hold(arrays, after):
+    n = len(after)
+    return call(
+        hold_kernel, arrays, [ANY] * len(arrays), tuple(jax.ShapeDtypeStruct(a.shape, a.dtype) for a in arrays),
+        after, out_specs=(ANY,) * len(arrays), name="hold",
+        input_output_aliases={n + i: i for i in range(len(arrays))},
     )
 
 
@@ -661,17 +745,18 @@
     down = adapter_down.T
     down_other = lax.ppermute(down, "narrow", zflip(1))
     first, second, own = norm(residual, pre_gain, 4, ())
-    w_mine, w_theirs = arrange(query_weight, key_weight, value_weight, output_weight.T, (own,))
+    w_theirs = arrange(query_weight, key_weight, value_weight, output_weight.T, (own,))
     first = lax.ppermute(first, "wide", first_leg)
     second = lax.ppermute(second, "wide", second_leg)
-    third = lax.ppermute(first[tok:], "wide", second_leg)
+    pack = pick(prompt_adapters, down, down_other, adapter_up_out, (w_theirs,))
+    up, out_down = ups(
+        prompt_adapters, adapter_up_query, adapter_up_key, adapter_up_value, adapter_down_out, (w_theirs,)
+    )
+    w, ring0 = stack(
+        query_weight, key_weight, value_weight, output_weight.T, lax.ppermute(w_theirs, "wide", across), out_down, (up,)
+    )
+    third = lax.ppermute(lower(first, (w,)), "wide", second_leg)
     pieces = (first, third, second, own)
-
-    pack = pick(prompt_adapters, down, down_other, adapter_up_out, (w_mine,))
-    up, out_down = ups(
-        prompt_adapters, adapter_up_query, adapter_up_key, adapter_up_value, adapter_down_out, (own,)
-    )
-    w, ring0 = stack(w_mine, lax.ppermute(w_theirs, "wide", across), out_down, (up,))
     pack = merge(pack, lax.ppermute(pack, "narrow", zflip(2)), (w, cosine, sine))
     n_down = 3 * prompts * RANK
     up_out = pack[n_down:]
@@ -695,11 +780,11 @@
         twos.append(lax.ppermute(out, "wide", second_leg))
         return (out, *carried)
 
-    def rotate_chunk(chunk, after):
-        own, send = finish(keeps[chunk], ones[chunk], twos[chunk], tables, chunk, after)
+    def rotate_chunk(chunk, after, carry=()):
+        own, send, carried = finish(keeps[chunk], ones[chunk], twos[chunk], tables, chunk, after, carry)
         mine.append(own)
         other.append(lax.ppermute(send, "wide", across))
-        return own
+        return (own, *carried)
 
     def attend_chunk(chunk, after, before=(), carry=()):
         return attend(prompt_lengths, sink_logits, mine, other, chunk, after, before, carry)
@@ -710,27 +795,21 @@
         return near0, near1, near2, lax.ppermute(near1, "wide", second_leg)
 
     product(0, ())
-    for chunk in range(1, CHUNKS):
-        product(chunk, (sends[-1],))
+    product(1, (sends[-1],))
     up_out = join(up_out, lax.ppermute(up_out, "wide", across), (sends[-1],))
-    (out0,) = pass_on(0, (sends[-1],))
-    (out1,) = pass_on(1, (out0,))
-    q0 = rotate_chunk(0, (out1,))
-    out2, ring1 = pass_on(2, (q0,), (ring1,))
+    out0, ring1 = pass_on(0, (sends[-1],), (ring1,))
     ring2 = lax.ppermute(ring1, "narrow", to_next)
-    q1 = rotate_chunk(1, (out2,))
-    sub0, _ = attend_chunk(0, (q1,))
-    (out3,) = pass_on(3, (sub0[0],))
-    q2 = rotate_chunk(2, (out3,))
-    sub1, _ = attend_chunk(1, (q2,), sub0)
-    sub2, _ = attend_chunk(2, (sub1[0],), sub1)
-    q3 = rotate_chunk(3, (sub2[0],))
-    sub3, (ring2,) = attend_chunk(3, (q3,), sub2, (ring2,))
-    aside = gather(sub3[3])
+    (q0,) = rotate_chunk(0, (out0,))
+    (out1,) = pass_on(1, (q0,))
+    sub0, _ = attend_chunk(0, (out1,))
+    (q1,) = rotate_chunk(1, (sub0[0],))
+    sub, _ = attend_chunk(1, (q1,), sub0)
+    aside = gather(sub[3])
+    sub = hold(sub[:3], (ring2,))
     keep, send = output(prompt_lengths, aside, (ring0,), up_out, True, ())
     extra = lax.ppermute(fold(keep, lax.ppermute(send, "wide", across)), "narrow", to_before)
     near0 = beside(
-        (sub3[0], lax.ppermute(sub3[1], "narrow", to_next), lax.ppermute(sub3[2], "narrow", to_second)), ()
+        (sub[0], lax.ppermute(sub[1], "narrow", to_next), lax.ppermute(sub[2], "narrow", to_second)), ()
     )
     keep, send = output(prompt_lengths, gather(near0), (ring0, ring1, ring2), up_out, False, ())
     total = fold(keep, lax.ppermute(send, "wide", across), extra)

time: 168 us -> 164 us (0.976)
  starting transfers between devices: 49.2 us -> 37.9 us
  waiting for transfers between devices: 61.4 us -> 71.8 us
  Pallas kernels: 48.9 us -> 40.6 us
  local copies, waits for them, and re-layouts: 2.42 us -> 7.39 us
    ppermute x1, waiting for transfers between devices: 0.01 us -> 16 us  [per_device_heads(): ring1 = lax.ppermute(ring0, 'narrow', to_next)]
    pallas_call x30 -> x24, Pallas kernels: 48.9 us -> 40.6 us  [call(): pl.pallas_call(lambda *refs: kernel(*refs[n:]), out_shape=out_shape, in_s...]
    ppermute x1, waiting for transfers between devices: 6.29 us -> 0.98 us  [per_device_heads(): first = lax.ppermute(first, 'wide', first_leg)]
    unnamed x28 -> x36, local copies, waits for them, and re-layouts: 1.11 us -> 6.13 us
    ppermute x4 -> x2, waiting for transfers between devices: 4.7 us -> 0.01 us  [product(): ones.append(lax.ppermute(send, 'wide', first_leg))]
    ppermute x4 -> x2, starting transfers between devices: 4.73 us -> 0.14 us  [pass_on(): twos.append(lax.ppermute(out, 'wide', second_leg))]
    ppermute x1, waiting for transfers between devices: 1.31 us -> 5.65 us  [per_device_heads(): ring2 = lax.ppermute(ring1, 'narrow', to_next)]
    ppermute x1, waiting for transfers between devices: 4.62 us -> 1.28 us  [per_device_heads(): down_other = lax.ppermute(down, 'narrow', zflip(1))]
  transfers between devices with their start and end apart: 40 -> 34, of which waited for: 21 -> 22; matrix products, arithmetic and copies ran while one was open for 3% -> 4% of each run, Pallas kernels for 21% -> 20%
where the time goes in v4:
time: 164 us; the launch traced here: 163 us
  waiting for transfers between devices  71.8 us (44%)
  Pallas kernels  40.6 us (25%)
  starting transfers between devices  37.9 us (23%)
  local copies, waits for them, and re-layouts  7.39 us (5%)
  other arithmetic  5.08 us (3%)
    pallas_call x24, Pallas kernels, call(): pl.pallas_call(lambda *refs: kernel(*refs[n:]), out_shape=out_shape, in_s...  40.6 us
    ppermute x1, waiting for transfers between devices, per_device_heads(): ring1 = lax.ppermute(ring0, 'narrow', to_next)  16 us
    ppermute x2, waiting for transfers between devices, pass_on(): twos.append(lax.ppermute(out, 'wide', second_leg))  11.9 us
    ppermute x2, waiting for transfers between devices, gather(): return (near0, near1, near2, lax.ppermute(near1, 'wide', second_leg))  9.15 us
    ppermute x3, starting transfers between devices, per_device_heads(): finals.append(piece if k == 0 else lax.ppermute(piece, 'narrow', shift(k)))  6.89 us
    unnamed x36, local copies, waits for them, and re-layouts  6.13 us
    ppermute x1, waiting for transfers between devices, per_device_heads(): ring2 = lax.ppermute(ring1, 'narrow', to_next)  5.65 us
    ppermute x3, waiting for transfers between devices, per_device_heads(): finals.append(piece if k == 0 else lax.ppermute(piece, 'narrow', shift(k)))  5.48 us
  transfers between devices with their start and end apart: 34, of which 22 were waited for; matrix products, arithmetic and copies ran while one was open for 4% of the time, Pallas kernels for 20%

profile of v4, /device:TPU:0, one launch (start us, length us, event | category | flops | bytes accessed | tf_op | source)
XLA Modules:
  0.0 163.3 jit_solution(13560002350489653863)
XLA Ops:
  0.0 4.0 %norm.1 = (bf16[512,1152]{1,0:T(8,128)(2,1)}, bf16[256,1152]{1,0:T(8,128)(2,1)}, bf16[256,1152]{1,0:T(8,128)(2,1)}) custom-call(bf16[256,4608]{1,0:T(8,128)(2,1)} %refs_0_.4, bf16[4608]{0:T(1024)(128)(2,1)} %refs_1_.8), custom_call_target="tpu_custom_call" | custom-call | flops 4718592 | bytes 4718592 | tf_op jit(solution)/shard_map/norm/pallas_call | solution.py:47
  4.1 3.2 %arrange.1.refs_0_ = bf16[576,2560]{1,0:T(8,128)(2,1)} custom-call(bf16[256,1152]{1,0:T(8,128)(2,1)} %get-tuple-element.38.refs_0_.refs_4_.refs_5_, bf16[576,1024]{1,0:T(8,128)(2,1)} %refs_1_.11, bf16[576,512]{1,0:T(8,128)(2,1)} %refs_2_.7, bf16[576,512]{1,0:T(8,128)(2,1)} %refs_3_.5, bf16[576,1024]{1,0:T(8,128)(2,1)} %bitcast.22), custom_call_target="tpu_custom_call" | custom-call | bytes 9437184 | tf_op jit(solution)/shard_map/arrange/pallas_call | solution.py:47
  7.8 2.6 %collective-permute-start = (bf16[512,1152]{1,0:T(8,128)(2,1)}, bf16[512,1152]{1,0:T(8,128)(2,1)S(1)}, u32[]{:S(2)}, u32[]{:S(2)}) collective-permute-start(bf16[512,1152]{1,0:T(8,128)(2,1)} %get-tuple-element.37), channel_id=1, source_target_pairs={{0,8},{4,20},{8,0},{12,28},{16,24},{20,4},{24,16},{28,12},{1,9},{5... | collective-permute-start | bytes 3538952 | tf_op jit(solution)/shard_map/ppermute | solution.py:749
  13.7 1.8 %copy-done = bf16[576,2560]{1,0:T(8,128)(2,1)S(1)} copy-done((bf16[576,2560]{1,0:T(8,128)(2,1)S(1)}, bf16[576,2560]{1,0:T(8,128)(2,1)}, u32[]{:S(2)}) %copy-start) | copy-done | bytes 2949144
  18.8 2.8 %pick.1.refs_3_ = bf16[256,576]{1,0:T(8,128)(2,1)} custom-call(bf16[576,2560]{1,0:T(8,128)(2,1)} %arrange.1.refs_0_, s32[4]{0:T(128)} %refs_1_.12, bf16[192,576]{1,0:T(8,128)(2,1)} %bitcast.3.refs_2_, bf16[192,576]{1,0:T(8,128)(2,1)} %collective-permute-done.4.refs_3_, bf16[256,1152]{1,0:T(8,128)(2,1)} %refs_4_.3), custom_call_target="tpu_custom_call" | custom-call | flops 44236800 | bytes 663552 | tf_op jit(solution)/shard_map/pick/pallas_call | solution.py:47
  21.6 2.7 %collective-permute-start.5 = (bf16[256,576]{1,0:T(8,128)(2,1)}, bf16[256,576]{1,0:T(8,128)(2,1)S(1)}, u32[]{:S(2)}, u32[]{:S(2)}) collective-permute-start(bf16[256,576]{1,0:T(8,128)(2,1)} %pick.1.refs_3_), channel_id=1, source_target_pairs={{0,2},{1,3},{2,0},{3,1},{4,6},{5,7},{6,4},{7,5},{8,10},{9,11},{10,... | collective-permute-start | bytes 884744 | tf_op jit(solution)/shard_map/ppermute | solution.py:760
  27.5 2.6 %stack.18 = (bf16[1152,2048]{1,0:T(8,128)(2,1)S(1)}, bf16[1216,512]{1,0:T(8,128)(2,1)S(1)}) custom-call(bf16[192,2048]{1,0:T(8,128)(2,1)S(1)} %copy-done.4, bf16[576,1024]{1,0:T(8,128)(2,1)S(1)} %copy-done.1, bf16[576,512]{1,0:T(8,128)(2,1)S(1)} %copy-done.6, bf16[576,512]{1,0:T(8,128)(2,1)S(1)} %copy-done.7, bf16[576,1024]{1,0:T(8,128)(2,1)S(1)} %bitcast.23, ...), custom_call_target="tpu_custom_call" | custom-call | bytes 11796480 | tf_op jit(solution)/shard_map/stack/pallas_call | solution.py:47
  31.3 2.1 %collective-permute-start.2 = (bf16[256,1152]{1,0:T(8,128)(2,1)S(1)}, bf16[256,1152]{1,0:T(8,128)(2,1)S(1)}, u32[]{:S(2)}, u32[]{:S(2)}) collective-permute-start(bf16[256,1152]{1,0:T(8,128)(2,1)S(1)} %lower.1), channel_id=1, source_target_pairs={{0,16},{4,12},{8,24},{12,4},{16,0},{20,28},{24,8},{28,20},{1,17},{... | collective-permute-start | bytes 1769480 | tf_op jit(solution)/shard_map/ppermute | solution.py:758
  33.4 3.7 %fusion.2 = (f32[2048,64]{1,0:T(8,128)S(1)}, f32[2048,64]{1,0:T(8,128)S(1)}, f32[2048,64]{1,0:T(8,128)S(1)}) fusion(f32[64]{0:T(128)S(1)} %negate_power_fusion, f32[2048]{0:T(1024)S(1)} %subtract_convert_fusion), kind=kLoop, calls=%fused_computation.9 | loop fusion | flops 262144 | bytes 1581312 | tf_op jit(solution)/shard_map/neg | solution.py:743
  41.2 4.6 %project.2 = (bf16[512,1024]{1,0:T(8,128)(2,1)S(1)}, f32[512,1024]{1,0:T(8,128)S(1)}) custom-call(s32[4]{0:T(128)S(1)} %copy-done.15, bf16[512,1152]{1,0:T(8,128)(2,1)S(1)} %collective-permute-done.refs_1_.refs_2_, bf16[256,1152]{1,0:T(8,128)(2,1)S(1)} %collective-permute-done.2.refs_2_.refs_3_, bf16[256,1152]{1,0:T(8,128)(2,1)} %collective-permute-done.3.refs_3_.refs_4_, ...), custom_call_target="tpu_custom_call" | custom-call | flops 2415919104 | bytes 9043968 | tf_op jit(solution)/shard_map/project/pallas_call | solution.py:47
  45.9 2.1 %collective-permute-start.7 = (bf16[512,1024]{1,0:T(8,128)(2,1)S(1)}, bf16[512,1024]{1,0:T(8,128)(2,1)S(1)}, u32[]{:S(2)}, u32[]{:S(2)}) collective-permute-start(bf16[512,1024]{1,0:T(8,128)(2,1)S(1)} %get-tuple-element.43.refs_0_), channel_id=1, source_target_pairs={{0,8},{4,20},{8,0},{12,28},{16,24},{20,4},{24,16},{28,12},{1,9},{5... | collective-permute-start | bytes 3145736 | tf_op jit(solution)/shard_map/ppermute | solution.py:775
  47.9 5.4 %project.3 = (bf16[512,1024]{1,0:T(8,128)(2,1)S(1)}, f32[512,1024]{1,0:T(8,128)S(1)}) custom-call(bf16[512,1024]{1,0:T(8,128)(2,1)S(1)} %get-tuple-element.43.refs_0_, s32[4]{0:T(128)S(1)} %copy-done.15, bf16[512,1152]{1,0:T(8,128)(2,1)S(1)} %collective-permute-done.refs_1_.refs_2_, bf16[256,1152]{1,0:T(8,128)(2,1)S(1)} %collective-permute-done.2.refs_2_.refs_3_, ...), custom_call_target="tpu_custom_call" | custom-call | flops 2415919104 | bytes 9043968 | tf_op jit(solution)/shard_map/project/pallas_call | solution.py:47
  53.6 16.0 %collective-permute-done.8.refs_3_ = bf16[1216,512]{1,0:T(8,128)(2,1)S(1)} collective-permute-done((bf16[1216,512]{1,0:T(8,128)(2,1)S(1)}, bf16[1216,512]{1,0:T(8,128)(2,1)S(1)}, u32[]{:S(2)}, u32[]{:S(2)}) %collective-permute-start.8) | collective-permute-done | bytes 1245216 | tf_op jit(solution)/shard_map/ppermute | solution.py:765
  70.5 8.4 %collective-permute-done.10.refs_3_ = bf16[512,512]{1,0:T(8,128)(2,1)S(1)} collective-permute-done((bf16[512,512]{1,0:T(8,128)(2,1)S(1)}, bf16[512,512]{1,0:T(8,128)(2,1)S(1)}, u32[]{:S(2)}, u32[]{:S(2)}) %collective-permute-start.10) | collective-permute-done | bytes 524320 | tf_op jit(solution)/shard_map/ppermute | solution.py:780
  81.5 3.8 %attend.2 = (bf16[256,128]{1,0:T(8,128)(2,1)S(1)}, bf16[256,128]{1,0:T(8,128)(2,1)S(1)}, bf16[256,128]{1,0:T(8,128)(2,1)S(1)}, bf16[256,128]{1,0:T(8,128)(2,1)S(1)}) custom-call(bf16[512,512]{1,0:T(8,128)(2,1)S(1)} %onward.3.refs_0_, s32[4]{0:T(128)S(1)} %copy-done.15, f32[8]{0:T(128)S(1)} %copy-done.16, ...), custom_call_target="tpu_custom_call" | custom-call | flops 402653184 | bytes 262144 | tf_op jit(solution)/shard_map/attend/pallas_call | solution.py:47
  85.3 3.5 %collective-permute-done.13.refs_3_ = bf16[512,512]{1,0:T(8,128)(2,1)S(1)} collective-permute-done((bf16[512,512]{1,0:T(8,128)(2,1)S(1)}, bf16[512,512]{1,0:T(8,128)(2,1)S(1)}, u32[]{:S(2)}, u32[]{:S(2)}) %collective-permute-start.13) | collective-permute-done | bytes 524320 | tf_op jit(solution)/shard_map/ppermute | solution.py:780
  91.0 4.1 %attend.3 = (bf16[512,128]{1,0:T(8,128)(2,1)S(1)}, bf16[512,128]{1,0:T(8,128)(2,1)S(1)}, bf16[512,128]{1,0:T(8,128)(2,1)S(1)}, bf16[512,128]{1,0:T(8,128)(2,1)S(1)}) custom-call(bf16[512,384]{1,0:T(8,128)(2,1)S(1)} %get-tuple-element.53.refs_0_.refs_4_, s32[4]{0:T(128)S(1)} %copy-done.15, f32[8]{0:T(128)S(1)} %copy-done.16, ...), custom_call_target="tpu_custom_call" | custom-call | flops 402653184 | bytes 524288 | tf_op jit(solution)/shard_map/attend/pallas_call | solution.py:47
  95.1 5.7 %collective-permute-done.9.refs_0_.refs_7_ = bf16[1216,512]{1,0:T(8,128)(2,1)S(1)} collective-permute-done((bf16[1216,512]{1,0:T(8,128)(2,1)S(1)}, bf16[1216,512]{1,0:T(8,128)(2,1)S(1)}, u32[]{:S(2)}, u32[]{:S(2)}) %collective-permute-start.9) | collective-permute-done | bytes 1245216 | tf_op jit(solution)/shard_map/ppermute | solution.py:801
  101.3 2.8 %collective-permute-start.16 = (bf16[512,128]{1,0:T(8,128)(2,1)S(1)}, bf16[512,128]{1,0:T(8,128)(2,1)S(1)}, u32[]{:S(2)}, u32[]{:S(2)}) collective-permute-start(bf16[512,128]{1,0:T(8,128)(2,1)S(1)} %get-tuple-element.63), channel_id=1, source_target_pairs={{0,3},{1,2},{2,1},{3,0},{4,7},{5,6},{6,5},{7,4},{8,11},{9,10},{10,... | collective-permute-start | bytes 393224 | tf_op jit(solution)/shard_map/ppermute | solution.py:812
  107.7 3.6 %collective-permute-done.16.refs_2_ = bf16[512,128]{1,0:T(8,128)(2,1)S(1)} collective-permute-done((bf16[512,128]{1,0:T(8,128)(2,1)S(1)}, bf16[512,128]{1,0:T(8,128)(2,1)S(1)}, u32[]{:S(2)}, u32[]{:S(2)}) %collective-permute-start.16) | collective-permute-done | bytes 131104 | tf_op jit(solution)/shard_map/ppermute | solution.py:812
  113.3 4.9 %collective-permute-done.25.refs_4_ = bf16[512,128]{1,0:T(8,128)(2,1)S(1)} collective-permute-done((bf16[512,128]{1,0:T(8,128)(2,1)S(1)}, bf16[512,128]{1,0:T(8,128)(2,1)S(1)}, u32[]{:S(2)}, u32[]{:S(2)}) %collective-permute-start.25) | collective-permute-done | bytes 131104 | tf_op jit(solution)/shard_map/ppermute | solution.py:795
  118.3 2.4 %output.3 = (f32[4,64,1152]{2,1,0:T(8,128)S(1)}, bf16[4,64,1152]{2,1,0:T(8,128)(2,1)S(1)}) custom-call(s32[4]{0:T(128)S(1)} %copy-done.15, bf16[512,128]{1,0:T(8,128)(2,1)S(1)} %get-tuple-element.66.refs_1_, bf16[512,128]{1,0:T(8,128)(2,1)S(1)} %collective-permute-done.23.refs_2_, bf16[512,128]{1,0:T(8,128)(2,1)S(1)} %collective-permute-done.24.refs_3_, ...), custom_call_target="tpu_custom_call" | custom-call | flops 603979776 | bytes 8585216 | tf_op jit(solution)/shard_map/output/pallas_call | solution.py:47
  120.8 2.0 %collective-permute-start.19 = (bf16[512,384]{1,0:T(8,128)(2,1)S(1)}, bf16[512,384]{1,0:T(8,128)(2,1)S(1)}, u32[]{:S(2)}, u32[]{:S(2)}) collective-permute-start(bf16[512,384]{1,0:T(8,128)(2,1)S(1)} %collective-permute-done.17.refs_2_), channel_id=1, source_target_pairs={{0,16},{4,12},{8,24},{12,4},{16,0},{20,28},{24,8},{28,20},{1,17},{... | collective-permute-start | bytes 1179656 | tf_op jit(solution)/shard_map/ppermute | solution.py:795
  122.9 3.9 %collective-permute-start.27 = (bf16[4,64,1152]{2,1,0:T(8,128)(2,1)S(1)}, bf16[4,64,1152]{2,1,0:T(8,128)(2,1)S(1)}, u32[]{:S(2)}, u32[]{:S(2)}) collective-permute-start(bf16[4,64,1152]{2,1,0:T(8,128)(2,1)S(1)} %fold.2), channel_id=1, source_target_pairs={{0,2},{1,0},{2,3},{3,1},{4,6},{5,4},{6,7},{7,5},{8,10},{9,8},{10,1... | collective-permute-start | bytes 1769480 | tf_op jit(solution)/shard_map/ppermute | solution.py:810
  128.5 4.2 %collective-permute-done.19.refs_4_ = bf16[512,384]{1,0:T(8,128)(2,1)S(1)} collective-permute-done((bf16[512,384]{1,0:T(8,128)(2,1)S(1)}, bf16[512,384]{1,0:T(8,128)(2,1)S(1)}, u32[]{:S(2)}, u32[]{:S(2)}) %collective-permute-start.19) | collective-permute-done | bytes 393248 | tf_op jit(solution)/shard_map/ppermute | solution.py:795
  132.8 4.0 %output.2 = (f32[4,64,1152]{2,1,0:T(8,128)S(1)}, bf16[4,64,1152]{2,1,0:T(8,128)(2,1)S(1)}) custom-call(s32[4]{0:T(128)S(1)} %copy-done.15, bf16[512,384]{1,0:T(8,128)(2,1)S(1)} %beside.1.refs_1_, bf16[512,384]{1,0:T(8,128)(2,1)S(1)} %collective-permute-done.17.refs_2_, bf16[512,384]{1,0:T(8,128)(2,1)S(1)} %collective-permute-done.18.refs_3_, ...), custom_call_target="tpu_custom_call" | custom-call | flops 1811939328 | bytes 8585216 | tf_op jit(solution)/shard_map/output/pallas_call | solution.py:47
  136.9 2.7 %collective-permute-done.27.refs_2_ = bf16[4,64,1152]{2,1,0:T(8,128)(2,1)S(1)} collective-permute-done((bf16[4,64,1152]{2,1,0:T(8,128)(2,1)S(1)}, bf16[4,64,1152]{2,1,0:T(8,128)(2,1)S(1)}, u32[]{:S(2)}, u32[]{:S(2)}) %collective-permute-start.27) | collective-permute-done | bytes 589856 | tf_op jit(solution)/shard_map/ppermute | solution.py:810
  140.3 3.0 %collective-permute-start.30 = (bf16[64,1152]{1,0:T(8,128)(2,1)S(1)}, bf16[64,1152]{1,0:T(8,128)(2,1)S(1)}, u32[]{:S(2)}, u32[]{:S(2)}) collective-permute-start(bf16[64,1152]{1,0:T(8,128)(2,1)S(1)} %get-tuple-element.74), channel_id=1, source_target_pairs={{0,24},{4,28},{8,16},{12,20},{16,8},{20,12},{24,0},{28,4},{1,25},{... | collective-permute-start | bytes 442376 | tf_op jit(solution)/shard_map/ppermute | solution.py:818
  143.4 3.2 %collective-permute-done.28 = bf16[64,1152]{1,0:T(8,128)(2,1)S(1)} collective-permute-done((bf16[64,1152]{1,0:T(8,128)(2,1)S(1)}, bf16[64,1152]{1,0:T(8,128)(2,1)S(1)}, u32[]{:S(2)}, u32[]{:S(2)}) %collective-permute-start.28) | collective-permute-done | bytes 147488 | tf_op jit(solution)/shard_map/ppermute | solution.py:818
  148.8 2.4 %collective-permute-start.31 = (bf16[64,1152]{1,0:T(8,128)(2,1)S(1)}, bf16[64,1152]{1,0:T(8,128)(2,1)S(1)}, u32[]{:S(2)}, u32[]{:S(2)}) collective-permute-start(bf16[64,1152]{1,0:T(8,128)(2,1)S(1)} %get-tuple-element.71), channel_id=1, source_target_pairs={{0,1},{1,2},{2,3},{3,0},{4,5},{5,6},{6,7},{7,4},{8,9},{9,10},{10,1... | collective-permute-start | bytes 442376 | tf_op jit(solution)/shard_map/ppermute | solution.py:827
  152.8 2.8 %collective-permute-start.33 = (bf16[64,1152]{1,0:T(8,128)(2,1)S(1)}, bf16[64,1152]{1,0:T(8,128)(2,1)S(1)}, u32[]{:S(2)}, u32[]{:S(2)}) collective-permute-start(bf16[64,1152]{1,0:T(8,128)(2,1)S(1)} %get-tuple-element.69), channel_id=1, source_target_pairs={{0,3},{1,0},{2,1},{3,2},{4,7},{5,4},{6,5},{7,6},{8,11},{9,8},{10,9... | collective-permute-start | bytes 442376 | tf_op jit(solution)/shard_map/ppermute | solution.py:827
  157.3 5.0 %collective-permute-done.32.refs_4_ = bf16[64,1152]{1,0:T(8,128)(2,1)S(1)} collective-permute-done((bf16[64,1152]{1,0:T(8,128)(2,1)S(1)}, bf16[64,1152]{1,0:T(8,128)(2,1)S(1)}, u32[]{:S(2)}, u32[]{:S(2)}) %collective-permute-start.32) | collective-permute-done | bytes 147488 | tf_op jit(solution)/shard_map/ppermute | solution.py:827
  (113 shorter events, 36.7 us)
Async XLA Ops:
  7.3 16.9 %collective-permute-start.1 = (bf16[576,2560]{1,0:T(8,128)(2,1)}, bf16[576,2560]{1,0:T(8,128)(2,1)}, u32[]{:S(2)}, u32[]{:S(2)}) collective-permute-start(bf16[576,2560]{1,0:T(8,128)(2,1)} %arrange.1.refs_0_), channel_id=1, source_target_pairs={{0,4},{4,0},{8,12},{12,8},{16,20},{20,16},{24,28},{28,24},{1,5},{5... | collective-permute-start | bytes 8847368 | tf_op jit(solution)/shard_map/ppermute | solution.py:756
  7.8 23.3 %collective-permute-start = (bf16[512,1152]{1,0:T(8,128)(2,1)}, bf16[512,1152]{1,0:T(8,128)(2,1)S(1)}, u32[]{:S(2)}, u32[]{:S(2)}) collective-permute-start(bf16[512,1152]{1,0:T(8,128)(2,1)} %get-tuple-element.37), channel_id=1, source_target_pairs={{0,8},{4,20},{8,0},{12,28},{16,24},{20,4},{24,16},{28,12},{1,9},{5... | collective-permute-start | bytes 3538952 | tf_op jit(solution)/shard_map/ppermute | solution.py:749
  10.4 8.4 %collective-permute-start.4 = (bf16[192,576]{1,0:T(8,128)(2,1)}, bf16[192,576]{1,0:T(8,128)(2,1)}, u32[]{:S(2)}, u32[]{:S(2)}) collective-permute-start(bf16[192,576]{1,0:T(8,128)(2,1)} %bitcast.3.refs_2_), channel_id=1, source_target_pairs={{0,1},{1,0},{2,3},{3,2},{4,5},{5,4},{6,7},{7,6},{8,9},{9,8},{10,11... | collective-permute-start | bytes 663560 | tf_op jit(solution)/shard_map/ppermute | solution.py:746
  12.0 28.7 %collective-permute-start.3 = (bf16[256,1152]{1,0:T(8,128)(2,1)}, bf16[256,1152]{1,0:T(8,128)(2,1)}, u32[]{:S(2)}, u32[]{:S(2)}) collective-permute-start(bf16[256,1152]{1,0:T(8,128)(2,1)} %get-tuple-element.42), channel_id=1, source_target_pairs={{0,16},{4,12},{8,24},{12,4},{16,0},{20,28},{24,8},{28,20},{1,17},{... | collective-permute-start | bytes 1769480 | tf_op jit(solution)/shard_map/ppermute | solution.py:750
  21.6 17.2 %collective-permute-start.5 = (bf16[256,576]{1,0:T(8,128)(2,1)}, bf16[256,576]{1,0:T(8,128)(2,1)S(1)}, u32[]{:S(2)}, u32[]{:S(2)}) collective-permute-start(bf16[256,576]{1,0:T(8,128)(2,1)} %pick.1.refs_3_), channel_id=1, source_target_pairs={{0,2},{1,3},{2,0},{3,1},{4,6},{5,7},{6,4},{7,5},{8,10},{9,11},{10,... | collective-permute-start | bytes 884744 | tf_op jit(solution)/shard_map/ppermute | solution.py:760
  31.3 10.0 %collective-permute-start.2 = (bf16[256,1152]{1,0:T(8,128)(2,1)S(1)}, bf16[256,1152]{1,0:T(8,128)(2,1)S(1)}, u32[]{:S(2)}, u32[]{:S(2)}) collective-permute-start(bf16[256,1152]{1,0:T(8,128)(2,1)S(1)} %lower.1), channel_id=1, source_target_pairs={{0,16},{4,12},{8,24},{12,4},{16,0},{20,28},{24,8},{28,20},{1,17},{... | collective-permute-start | bytes 1769480 | tf_op jit(solution)/shard_map/ppermute | solution.py:758
  39.0 30.7 %collective-permute-start.8 = (bf16[1216,512]{1,0:T(8,128)(2,1)S(1)}, bf16[1216,512]{1,0:T(8,128)(2,1)S(1)}, u32[]{:S(2)}, u32[]{:S(2)}) collective-permute-start(bf16[1216,512]{1,0:T(8,128)(2,1)S(1)} %get-tuple-element.46.refs_5_), channel_id=1, source_target_pairs={{0,1},{1,3},{2,0},{3,2},{4,5},{5,7},{6,4},{7,6},{8,9},{9,11},{10,8... | collective-permute-start | bytes 3735560 | tf_op jit(solution)/shard_map/ppermute | solution.py:765
  45.9 23.8 %collective-permute-start.7 = (bf16[512,1024]{1,0:T(8,128)(2,1)S(1)}, bf16[512,1024]{1,0:T(8,128)(2,1)S(1)}, u32[]{:S(2)}, u32[]{:S(2)}) collective-permute-start(bf16[512,1024]{1,0:T(8,128)(2,1)S(1)} %get-tuple-element.43.refs_0_), channel_id=1, source_target_pairs={{0,8},{4,20},{8,0},{12,28},{16,24},{20,4},{24,16},{28,12},{1,9},{5... | collective-permute-start | bytes 3145736 | tf_op jit(solution)/shard_map/ppermute | solution.py:775
  53.4 26.0 %collective-permute-start.11 = (bf16[512,1024]{1,0:T(8,128)(2,1)S(1)}, bf16[512,1024]{1,0:T(8,128)(2,1)S(1)}, u32[]{:S(2)}, u32[]{:S(2)}) collective-permute-start(bf16[512,1024]{1,0:T(8,128)(2,1)S(1)} %get-tuple-element.44.refs_0_), channel_id=1, source_target_pairs={{0,8},{4,20},{8,0},{12,28},{16,24},{20,4},{24,16},{28,12},{1,9},{5... | collective-permute-start | bytes 3145736 | tf_op jit(solution)/shard_map/ppermute | solution.py:775
  69.7 9.2 %collective-permute-start.10 = (bf16[512,512]{1,0:T(8,128)(2,1)S(1)}, bf16[512,512]{1,0:T(8,128)(2,1)S(1)}, u32[]{:S(2)}, u32[]{:S(2)}) collective-permute-start(bf16[512,512]{1,0:T(8,128)(2,1)S(1)} %get-tuple-element.48.refs_0_), channel_id=1, source_target_pairs={{0,16},{4,12},{8,24},{12,4},{16,0},{20,28},{24,8},{28,20},{1,17},{... | collective-permute-start | bytes 1572872 | tf_op jit(solution)/shard_map/ppermute | solution.py:780
  69.8 30.9 %collective-permute-start.9 = (bf16[1216,512]{1,0:T(8,128)(2,1)S(1)}, bf16[1216,512]{1,0:T(8,128)(2,1)S(1)}, u32[]{:S(2)}, u32[]{:S(2)}) collective-permute-start(bf16[1216,512]{1,0:T(8,128)(2,1)S(1)} %get-tuple-element.47.refs_6_), channel_id=1, source_target_pairs={{0,1},{1,3},{2,0},{3,2},{4,5},{5,7},{6,4},{7,6},{8,9},{9,11},{10,8... | collective-permute-start | bytes 3735560 | tf_op jit(solution)/shard_map/ppermute | solution.py:801
  79.5 9.2 %collective-permute-start.13 = (bf16[512,512]{1,0:T(8,128)(2,1)S(1)}, bf16[512,512]{1,0:T(8,128)(2,1)S(1)}, u32[]{:S(2)}, u32[]{:S(2)}) collective-permute-start(bf16[512,512]{1,0:T(8,128)(2,1)S(1)} %onward.3.refs_0_), channel_id=1, source_target_pairs={{0,16},{4,12},{8,24},{12,4},{16,0},{20,28},{24,8},{28,20},{1,17},{... | collective-permute-start | bytes 1572872 | tf_op jit(solution)/shard_map/ppermute | solution.py:780
  79.6 1.9 %collective-permute-start.12 = (bf16[512,384]{1,0:T(8,128)(2,1)S(1)}, bf16[512,384]{1,0:T(8,128)(2,1)S(1)}, u32[]{:S(2)}, u32[]{:S(2)}) collective-permute-start(bf16[512,384]{1,0:T(8,128)(2,1)S(1)} %get-tuple-element.51), channel_id=1, source_target_pairs={{0,4},{4,0},{8,12},{12,8},{16,20},{20,16},{24,28},{28,24},{1,5},{5... | collective-permute-start | bytes 1179656 | tf_op jit(solution)/shard_map/ppermute | solution.py:786
  89.2 1.8 %collective-permute-start.14 = (bf16[512,384]{1,0:T(8,128)(2,1)S(1)}, bf16[512,384]{1,0:T(8,128)(2,1)S(1)}, u32[]{:S(2)}, u32[]{:S(2)}) collective-permute-start(bf16[512,384]{1,0:T(8,128)(2,1)S(1)} %get-tuple-element.54), channel_id=1, source_target_pairs={{0,4},{4,0},{8,12},{12,8},{16,20},{20,16},{24,28},{28,24},{1,5},{5... | collective-permute-start | bytes 1179656 | tf_op jit(solution)/shard_map/ppermute | solution.py:786
  100.7 7.0 %collective-permute-start.15 = (bf16[512,128]{1,0:T(8,128)(2,1)S(1)}, bf16[512,128]{1,0:T(8,128)(2,1)S(1)}, u32[]{:S(2)}, u32[]{:S(2)}) collective-permute-start(bf16[512,128]{1,0:T(8,128)(2,1)S(1)} %get-tuple-element.62), channel_id=1, source_target_pairs={{0,1},{1,3},{2,0},{3,2},{4,5},{5,7},{6,4},{7,6},{8,9},{9,11},{10,8... | collective-permute-start | bytes 393224 | tf_op jit(solution)/shard_map/ppermute | solution.py:812
  101.3 9.9 %collective-permute-start.16 = (bf16[512,128]{1,0:T(8,128)(2,1)S(1)}, bf16[512,128]{1,0:T(8,128)(2,1)S(1)}, u32[]{:S(2)}, u32[]{:S(2)}) collective-permute-start(bf16[512,128]{1,0:T(8,128)(2,1)S(1)} %get-tuple-element.63), channel_id=1, source_target_pairs={{0,3},{1,2},{2,1},{3,0},{4,7},{5,6},{6,5},{7,4},{8,11},{9,10},{10,... | collective-permute-start | bytes 393224 | tf_op jit(solution)/shard_map/ppermute | solution.py:812
  104.2 7.7 %collective-permute-start.23 = (bf16[512,128]{1,0:T(8,128)(2,1)S(1)}, bf16[512,128]{1,0:T(8,128)(2,1)S(1)}, u32[]{:S(2)}, u32[]{:S(2)}) collective-permute-start(bf16[512,128]{1,0:T(8,128)(2,1)S(1)} %get-tuple-element.66.refs_1_), channel_id=1, source_target_pairs={{0,8},{4,20},{8,0},{12,28},{16,24},{20,4},{24,16},{28,12},{1,9},{5... | collective-permute-start | bytes 393224 | tf_op jit(solution)/shard_map/ppermute | solution.py:793
  105.3 6.5 %collective-permute-start.20 = (bf16[64,576]{1,0:T(8,128)(2,1)S(1)}, bf16[64,576]{1,0:T(8,128)(2,1)S(1)}, u32[]{:S(2)}, u32[]{:S(2)}) collective-permute-start(bf16[64,576]{1,0:T(8,128)(2,1)S(1)} %slice.10), channel_id=1, source_target_pairs={{0,1},{1,0},{2,3},{3,2},{4,5},{5,4},{6,7},{7,6},{8,9},{9,8},{10,11... | collective-permute-start | bytes 221192 | tf_op jit(solution)/shard_map/ppermute | solution.py:763
  105.9 7.4 %collective-permute-start.24 = (bf16[512,128]{1,0:T(8,128)(2,1)S(1)}, bf16[512,128]{1,0:T(8,128)(2,1)S(1)}, u32[]{:S(2)}, u32[]{:S(2)}) collective-permute-start(bf16[512,128]{1,0:T(8,128)(2,1)S(1)} %get-tuple-element.66.refs_1_), channel_id=1, source_target_pairs={{0,16},{4,12},{8,24},{12,4},{16,0},{20,28},{24,8},{28,20},{1,17},{... | collective-permute-start | bytes 393224 | tf_op jit(solution)/shard_map/ppermute | solution.py:794
  111.4 9.4 %collective-permute-start.17 = (bf16[512,384]{1,0:T(8,128)(2,1)S(1)}, bf16[512,384]{1,0:T(8,128)(2,1)S(1)}, u32[]{:S(2)}, u32[]{:S(2)}) collective-permute-start(bf16[512,384]{1,0:T(8,128)(2,1)S(1)} %beside.1.refs_1_), channel_id=1, source_target_pairs={{0,8},{4,20},{8,0},{12,28},{16,24},{20,4},{24,16},{28,12},{1,9},{5... | collective-permute-start | bytes 1179656 | tf_op jit(solution)/shard_map/ppermute | solution.py:793
  111.8 6.4 %collective-permute-start.25 = (bf16[512,128]{1,0:T(8,128)(2,1)S(1)}, bf16[512,128]{1,0:T(8,128)(2,1)S(1)}, u32[]{:S(2)}, u32[]{:S(2)}) collective-permute-start(bf16[512,128]{1,0:T(8,128)(2,1)S(1)} %collective-permute-done.23.refs_2_), channel_id=1, source_target_pairs={{0,16},{4,12},{8,24},{12,4},{16,0},{20,28},{24,8},{28,20},{1,17},{... | collective-permute-start | bytes 393224 | tf_op jit(solution)/shard_map/ppermute | solution.py:795
  120.6 2.2 %collective-permute-start.26 = (bf16[4,64,1152]{2,1,0:T(8,128)(2,1)S(1)}, bf16[4,64,1152]{2,1,0:T(8,128)(2,1)S(1)}, u32[]{:S(2)}, u32[]{:S(2)}) collective-permute-start(bf16[4,64,1152]{2,1,0:T(8,128)(2,1)S(1)} %get-tuple-element.68), channel_id=1, source_target_pairs={{0,4},{4,0},{8,12},{12,8},{16,20},{20,16},{24,28},{28,24},{1,5},{5... | collective-permute-start | bytes 1769480 | tf_op jit(solution)/shard_map/ppermute | solution.py:810
  120.7 7.8 %collective-permute-start.18 = (bf16[512,384]{1,0:T(8,128)(2,1)S(1)}, bf16[512,384]{1,0:T(8,128)(2,1)S(1)}, u32[]{:S(2)}, u32[]{:S(2)}) collective-permute-start(bf16[512,384]{1,0:T(8,128)(2,1)S(1)} %beside.1.refs_1_), channel_id=1, source_target_pairs={{0,16},{4,12},{8,24},{12,4},{16,0},{20,28},{24,8},{28,20},{1,17},{... | collective-permute-start | bytes 1179656 | tf_op jit(solution)/shard_map/ppermute | solution.py:794
  120.8 12.0 %collective-permute-start.19 = (bf16[512,384]{1,0:T(8,128)(2,1)S(1)}, bf16[512,384]{1,0:T(8,128)(2,1)S(1)}, u32[]{:S(2)}, u32[]{:S(2)}) collective-permute-start(bf16[512,384]{1,0:T(8,128)(2,1)S(1)} %collective-permute-done.17.refs_2_), channel_id=1, source_target_pairs={{0,16},{4,12},{8,24},{12,4},{16,0},{20,28},{24,8},{28,20},{1,17},{... | collective-permute-start | bytes 1179656 | tf_op jit(solution)/shard_map/ppermute | solution.py:795
  122.9 16.6 %collective-permute-start.27 = (bf16[4,64,1152]{2,1,0:T(8,128)(2,1)S(1)}, bf16[4,64,1152]{2,1,0:T(8,128)(2,1)S(1)}, u32[]{:S(2)}, u32[]{:S(2)}) collective-permute-start(bf16[4,64,1152]{2,1,0:T(8,128)(2,1)S(1)} %fold.2), channel_id=1, source_target_pairs={{0,2},{1,0},{2,3},{3,1},{4,6},{5,4},{6,7},{7,5},{8,10},{9,8},{10,1... | collective-permute-start | bytes 1769480 | tf_op jit(solution)/shard_map/ppermute | solution.py:810
  136.8 2.8 %collective-permute-start.22 = (bf16[4,64,1152]{2,1,0:T(8,128)(2,1)S(1)}, bf16[4,64,1152]{2,1,0:T(8,128)(2,1)S(1)}, u32[]{:S(2)}, u32[]{:S(2)}) collective-permute-start(bf16[4,64,1152]{2,1,0:T(8,128)(2,1)S(1)} %get-tuple-element.65), channel_id=1, source_target_pairs={{0,4},{4,0},{8,12},{12,8},{16,20},{20,16},{24,28},{28,24},{1,5},{5... | collective-permute-start | bytes 1769480 | tf_op jit(solution)/shard_map/ppermute | solution.py:815
  139.8 6.8 %collective-permute-start.28 = (bf16[64,1152]{1,0:T(8,128)(2,1)S(1)}, bf16[64,1152]{1,0:T(8,128)(2,1)S(1)}, u32[]{:S(2)}, u32[]{:S(2)}) collective-permute-start(bf16[64,1152]{1,0:T(8,128)(2,1)S(1)} %get-tuple-element.76), channel_id=1, source_target_pairs={{0,8},{4,12},{8,0},{12,4},{16,24},{20,28},{24,16},{28,20},{1,9},{5... | collective-permute-start | bytes 442376 | tf_op jit(solution)/shard_map/ppermute | solution.py:818
  140.3 8.0 %collective-permute-start.29 = (bf16[64,1152]{1,0:T(8,128)(2,1)S(1)}, bf16[64,1152]{1,0:T(8,128)(2,1)S(1)}, u32[]{:S(2)}, u32[]{:S(2)}) collective-permute-start(bf16[64,1152]{1,0:T(8,128)(2,1)S(1)} %get-tuple-element.75), channel_id=1, source_target_pairs={{0,16},{4,20},{8,24},{12,28},{16,0},{20,4},{24,8},{28,12},{1,17},{... | collective-permute-start | bytes 442376 | tf_op jit(solution)/shard_map/ppermute | solution.py:818
  140.3 8.0 %collective-permute-start.30 = (bf16[64,1152]{1,0:T(8,128)(2,1)S(1)}, bf16[64,1152]{1,0:T(8,128)(2,1)S(1)}, u32[]{:S(2)}, u32[]{:S(2)}) collective-permute-start(bf16[64,1152]{1,0:T(8,128)(2,1)S(1)} %get-tuple-element.74), channel_id=1, source_target_pairs={{0,24},{4,28},{8,16},{12,20},{16,8},{20,12},{24,0},{28,4},{1,25},{... | collective-permute-start | bytes 442376 | tf_op jit(solution)/shard_map/ppermute | solution.py:818
  148.8 8.5 %collective-permute-start.31 = (bf16[64,1152]{1,0:T(8,128)(2,1)S(1)}, bf16[64,1152]{1,0:T(8,128)(2,1)S(1)}, u32[]{:S(2)}, u32[]{:S(2)}) collective-permute-start(bf16[64,1152]{1,0:T(8,128)(2,1)S(1)} %get-tuple-element.71), channel_id=1, source_target_pairs={{0,1},{1,2},{2,3},{3,0},{4,5},{5,6},{6,7},{7,4},{8,9},{9,10},{10,1... | collective-permute-start | bytes 442376 | tf_op jit(solution)/shard_map/ppermute | solution.py:827
  151.2 11.0 %collective-permute-start.32 = (bf16[64,1152]{1,0:T(8,128)(2,1)S(1)}, bf16[64,1152]{1,0:T(8,128)(2,1)S(1)}, u32[]{:S(2)}, u32[]{:S(2)}) collective-permute-start(bf16[64,1152]{1,0:T(8,128)(2,1)S(1)} %get-tuple-element.70), channel_id=1, source_target_pairs={{0,2},{1,3},{2,0},{3,1},{4,6},{5,7},{6,4},{7,5},{8,10},{9,11},{10,... | collective-permute-start | bytes 442376 | tf_op jit(solution)/shard_map/ppermute | solution.py:827
  152.8 9.4 %collective-permute-start.33 = (bf16[64,1152]{1,0:T(8,128)(2,1)S(1)}, bf16[64,1152]{1,0:T(8,128)(2,1)S(1)}, u32[]{:S(2)}, u32[]{:S(2)}) collective-permute-start(bf16[64,1152]{1,0:T(8,128)(2,1)S(1)} %get-tuple-element.69), channel_id=1, source_target_pairs={{0,3},{1,0},{2,1},{3,2},{4,7},{5,4},{6,5},{7,6},{8,11},{9,8},{10,9... | collective-permute-start | bytes 442376 | tf_op jit(solution)/shard_map/ppermute | solution.py:827
  (20 other events, 92.6 us)

commit v5 on v4

--- a/solution.py
+++ b/solution.py
@@ -197,17 +197,14 @@
     return adapter
 
 
-def pick_kernel(prompts, chosen_ref, down_hbm, other_hbm, upo_hbm, pack_ref, down_ref, other_ref, upo_ref, sems):
+def pick_kernel(prompts, chosen_ref, down_ref, other_ref, upo_hbm, pack_ref, upo_ref, sems):
     me, z = lax.axis_index("wide"), lax.axis_index("narrow")
     chip = lax.shift_right_logical(me, 1)
     core = me & 1
     n_codes = prompts * RANK
     local = down_ref.shape[0] // (3 * RANK)
     rows = down_ref.shape[1]
-    copies = [
-        pltpu.make_async_copy(down_hbm, down_ref, sems.at[prompts]),
-        pltpu.make_async_copy(other_hbm, other_ref, sems.at[prompts + 1]),
-    ]
+    copies = []
     for p in range(prompts):
         at = pl.ds(pl.multiple_of(chosen_ref[p] * RANK, RANK), RANK)
         copies.append(pltpu.make_async_copy(upo_hbm.at[at, :], upo_ref.at[pl.ds(p * RANK, RANK), :], sems.at[p]))
@@ -238,16 +235,14 @@
     prompts = chosen.shape[0]
     n_codes = prompts * RANK
     return call(
-        functools.partial(pick_kernel, prompts), (chosen, down, other, upo), [SMEM, HBM, HBM, HBM],
+        functools.partial(pick_kernel, prompts), (chosen, down, other, upo), [SMEM, VMEM, VMEM, ANY],
         jax.ShapeDtypeStruct((4 * n_codes, down.shape[1]), BF16),
         after,
         scratch=[
-            pltpu.VMEM(down.shape, BF16),
-            pltpu.VMEM(down.shape, BF16),
             pltpu.VMEM((n_codes, upo.shape[1]), BF16),
-            pltpu.SemaphoreType.DMA((prompts + 2,)),
+            pltpu.SemaphoreType.DMA((prompts,)),
         ],
-        out_specs=VMEM, name="pick", grant=60, flops=down.size * 400, moved=down.size * 6,
+        out_specs=VMEM, name="pick", flops=down.size * 400, moved=down.size * 6,
     )
 
 
@@ -673,6 +668,44 @@
     )
 
 
+def total_kernel(keep_ref, got_ref, extra_ref, *outs):
+    chip = lax.shift_right_logical(lax.axis_index("wide"), 1)
+    for delta in range(CHIPS):
+        at = chip ^ delta
+        outs[delta][...] = (keep_ref[at] + got_ref[at].astype(F32) + extra_ref[at].astype(F32)).astype(BF16)
+
+
+def total_rows(keep, got, extra):
+    shape = jax.ShapeDtypeStruct(keep.shape[1:], BF16)
+    return call(
+        total_kernel, (keep, got, extra), [VMEM] * 3, (shape,) * CHIPS,
+        out_specs=(VMEM,) * CHIPS, name="total_rows", flops=keep.size, moved=keep.size * 8,
+    )
+
+
+def settle_kernel(*refs):
+    pieces, outs, held = refs[:4], refs[4:8], refs[8]
+    chip, z = lax.shift_right_logical(lax.axis_index("wide"), 1), lax.axis_index("narrow")
+    count = 4 * held.shape[2]
+    total = 0.0
+    for ref in pieces:
+        x = ref[...].astype(F32)
+        total = total + jnp.sum(x * x, axis=1, keepdims=True)
+    scale = lax.rsqrt(total / count + epsilon)
+    for delta, ref in enumerate(pieces):
+        held[delta] = (ref[...].astype(F32) * scale).astype(BF16)
+    for k in range(4):
+        outs[k][...] = held[chip ^ ((z + k) & 3)]
+
+
+def settle(pieces):
+    shape = jax.ShapeDtypeStruct(pieces[0].shape, BF16)
+    return call(
+        settle_kernel, pieces, [VMEM] * 4, (shape,) * 4, scratch=[pltpu.VMEM((4, *shape.shape), BF16)],
+        out_specs=(VMEM,) * 4, name="settle", flops=shape.size * 16, moved=shape.size * 16,
+    )
+
+
 def close_kernel(stream_ref, gain_ref, *refs):
     pieces = refs[:4]
     out_ref = refs[4]
@@ -812,19 +845,10 @@
         (sub[0], lax.ppermute(sub[1], "narrow", to_next), lax.ppermute(sub[2], "narrow", to_second)), ()
     )
     keep, send = output(prompt_lengths, gather(near0), (ring0, ring1, ring2), up_out, False, ())
-    total = fold(keep, lax.ppermute(send, "wide", across), extra)
-    rows_of = lambda to: lax.dynamic_index_in_dim(total, to, 0, keepdims=False)
-    full = [rows_of(chip)] + [
-        lax.ppermute(rows_of(chip ^ delta), "wide", flip(2 * delta)) for delta in (1, 2, 3)
-    ]
-    full = jnp.stack(full)
-    wide_rows = full.astype(F32)
-    mean_square = jnp.sum(wide_rows * wide_rows, axis=(0, 2)) / features
-    scaled = (wide_rows * lax.rsqrt(mean_square + epsilon)[None, :, None]).astype(BF16)
-    finals = []
-    for k in range(4):
-        piece = lax.dynamic_index_in_dim(scaled, chip ^ ((z + k) & 3), 0, keepdims=False)
-        finals.append(piece if k == 0 else lax.ppermute(piece, "narrow", shift(k)))
+    cuts = total_rows(keep, lax.ppermute(send, "wide", across), extra)
+    full = [cuts[0]] + [lax.ppermute(cuts[delta], "wide", flip(2 * delta)) for delta in (1, 2, 3)]
+    scaled = settle(full)
+    finals = [scaled[0]] + [lax.ppermute(scaled[k], "narrow", shift(k)) for k in (1, 2, 3)]
     own_width = post_gain.shape[0]
     own_stream = lax.dynamic_slice_in_dim(residual, z * own_width, own_width, 1)
     return close(own_stream, post_gain, finals)

time: 164 us -> 163 us (level)
  local copies, waits for them, and re-layouts: 7.39 us -> 3.06 us
    ppermute x1, waiting for transfers between devices: 0.98 us -> 5.29 us  [per_device_heads(): first = lax.ppermute(first, 'wide', first_leg)]
    unnamed x36 -> x30, local copies, waits for them, and re-layouts: 6.13 us -> 1.91 us
    ppermute x1, waiting for transfers between devices: 5.65 us -> 3.53 us  [per_device_heads(): ring2 = lax.ppermute(ring1, 'narrow', to_next)]
    pallas_call x24 -> x25, Pallas kernels: 40.6 us -> 41.8 us  [call(): pl.pallas_call(lambda *refs: kernel(*refs[n:]), out_shape=out_shape, in_s...]
  transfers between devices with their start and end apart: 34 -> 34, of which waited for: 22 -> 21; matrix products, arithmetic and copies ran while one was open for 4% -> 4% of each run, Pallas kernels for 20% -> 20%
where the time goes in v5:
time: 163 us; the launch traced here: 162 us
  waiting for transfers between devices  72.9 us (45%)
  Pallas kernels  41.8 us (26%)
  starting transfers between devices  39 us (24%)
  other arithmetic  4.64 us (3%)
  local copies, waits for them, and re-layouts  3.06 us (2%)
    pallas_call x25, Pallas kernels, call(): pl.pallas_call(lambda *refs: kernel(*refs[n:]), out_shape=out_shape, in_s...  41.8 us
    ppermute x1, waiting for transfers between devices, per_device_heads(): ring1 = lax.ppermute(ring0, 'narrow', to_next)  15.6 us
    ppermute x2, waiting for transfers between devices, pass_on(): twos.append(lax.ppermute(out, 'wide', second_leg))  10.4 us
    ppermute x2, waiting for transfers between devices, gather(): return (near0, near1, near2, lax.ppermute(near1, 'wide', second_leg))  9.03 us
    ppermute x3, starting transfers between devices, per_device_heads(): lax.ppermute(scaled[k], 'narrow', shift(k))  6.68 us
    ppermute x3, waiting for transfers between devices, per_device_heads(): lax.ppermute(scaled[k], 'narrow', shift(k))  5.48 us
    ppermute x1, waiting for transfers between devices, per_device_heads(): first = lax.ppermute(first, 'wide', first_leg)  5.29 us
    ppermute x3, waiting for transfers between devices, per_device_heads(): lax.ppermute(cuts[delta], 'wide', flip(2 * delta))  5.14 us
  transfers between devices with their start and end apart: 34, of which 21 were waited for; matrix products, arithmetic and copies ran while one was open for 4% of the time, Pallas kernels for 20%

profile of v5, /device:TPU:0, one launch (start us, length us, event | category | flops | bytes accessed | tf_op | source)
XLA Modules:
  0.0 161.9 jit_solution(13098802222406654764)
XLA Ops:
  0.0 4.0 %norm.1 = (bf16[512,1152]{1,0:T(8,128)(2,1)}, bf16[256,1152]{1,0:T(8,128)(2,1)}, bf16[256,1152]{1,0:T(8,128)(2,1)}) custom-call(bf16[256,4608]{1,0:T(8,128)(2,1)} %refs_0_.4, bf16[4608]{0:T(1024)(128)(2,1)} %refs_1_.8), custom_call_target="tpu_custom_call" | custom-call | flops 4718592 | bytes 4718592 | tf_op jit(solution)/shard_map/norm/pallas_call | solution.py:47
  4.1 3.2 %arrange.1.refs_0_ = bf16[576,2560]{1,0:T(8,128)(2,1)} custom-call(bf16[256,1152]{1,0:T(8,128)(2,1)} %get-tuple-element.46.refs_0_.refs_4_.refs_5_, bf16[576,1024]{1,0:T(8,128)(2,1)} %refs_1_.11, bf16[576,512]{1,0:T(8,128)(2,1)} %refs_2_.7, bf16[576,512]{1,0:T(8,128)(2,1)} %refs_3_.5, bf16[576,1024]{1,0:T(8,128)(2,1)} %bitcast.5), custom_call_target="tpu_custom_call" | custom-call | bytes 9437184 | tf_op jit(solution)/shard_map/arrange/pallas_call | solution.py:47
  7.9 2.6 %collective-permute-start = (bf16[512,1152]{1,0:T(8,128)(2,1)}, bf16[512,1152]{1,0:T(8,128)(2,1)S(1)}, u32[]{:S(2)}, u32[]{:S(2)}) collective-permute-start(bf16[512,1152]{1,0:T(8,128)(2,1)} %get-tuple-element.45), channel_id=1, source_target_pairs={{0,8},{4,20},{8,0},{12,28},{16,24},{20,4},{24,16},{28,12},{1,9},{5... | collective-permute-start | bytes 3538952 | tf_op jit(solution)/shard_map/ppermute | solution.py:782
  16.5 2.2 %collective-permute-done.4.refs_3_ = bf16[192,576]{1,0:T(8,128)(2,1)} collective-permute-done((bf16[192,576]{1,0:T(8,128)(2,1)}, bf16[192,576]{1,0:T(8,128)(2,1)}, u32[]{:S(2)}, u32[]{:S(2)}) %collective-permute-start.4) | collective-permute-done | bytes 221216 | tf_op jit(solution)/shard_map/ppermute | solution.py:779
  20.5 2.7 %collective-permute-start.5 = (bf16[256,576]{1,0:T(8,128)(2,1)S(1)}, bf16[256,576]{1,0:T(8,128)(2,1)S(1)}, u32[]{:S(2)}, u32[]{:S(2)}) collective-permute-start(bf16[256,576]{1,0:T(8,128)(2,1)S(1)} %pick.1.refs_3_), channel_id=1, source_target_pairs={{0,2},{1,3},{2,0},{3,1},{4,6},{5,7},{6,4},{7,5},{8,10},{9,11},{10,... | collective-permute-start | bytes 884744 | tf_op jit(solution)/shard_map/ppermute | solution.py:793
  23.2 2.6 %stack.1 = (bf16[1152,2048]{1,0:T(8,128)(2,1)S(1)}, bf16[1216,512]{1,0:T(8,128)(2,1)S(1)}) custom-call(bf16[192,2048]{1,0:T(8,128)(2,1)S(1)} %get-tuple-element.47.refs_0_.refs_7_.refs_8_, bf16[576,1024]{1,0:T(8,128)(2,1)S(1)} %copy-done.1, bf16[576,512]{1,0:T(8,128)(2,1)S(1)} %copy-done.3, bf16[576,512]{1,0:T(8,128)(2,1)S(1)} %copy-done.4, ...), custom_call_target="tpu_custom_call" | custom-call | bytes 11796480 | tf_op jit(solution)/shard_map/stack/pallas_call | solution.py:47
  25.8 5.3 %collective-permute-done.refs_1_.refs_2_ = bf16[512,1152]{1,0:T(8,128)(2,1)S(1)} collective-permute-done((bf16[512,1152]{1,0:T(8,128)(2,1)}, bf16[512,1152]{1,0:T(8,128)(2,1)S(1)}, u32[]{:S(2)}, u32[]{:S(2)}) %collective-permute-start) | collective-permute-done | bytes 1179680 | tf_op jit(solution)/shard_map/ppermute | solution.py:782
  31.3 2.1 %collective-permute-start.2 = (bf16[256,1152]{1,0:T(8,128)(2,1)S(1)}, bf16[256,1152]{1,0:T(8,128)(2,1)S(1)}, u32[]{:S(2)}, u32[]{:S(2)}) collective-permute-start(bf16[256,1152]{1,0:T(8,128)(2,1)S(1)} %lower.1), channel_id=1, source_target_pairs={{0,16},{4,12},{8,24},{12,4},{16,0},{20,28},{24,8},{28,20},{1,17},{... | collective-permute-start | bytes 1769480 | tf_op jit(solution)/shard_map/ppermute | solution.py:791
  33.4 3.7 %fusion = (f32[2048,64]{1,0:T(8,128)S(1)}, f32[2048,64]{1,0:T(8,128)S(1)}, f32[2048,64]{1,0:T(8,128)S(1)}) fusion(f32[64]{0:T(128)S(1)} %negate_power_fusion, f32[2048]{0:T(1024)S(1)} %subtract_convert_fusion), kind=kLoop, calls=%fused_computation.4 | loop fusion | flops 262144 | bytes 1581312 | tf_op jit(solution)/shard_map/neg | solution.py:776
  41.3 4.7 %project.2 = (bf16[512,1024]{1,0:T(8,128)(2,1)S(1)}, f32[512,1024]{1,0:T(8,128)S(1)}) custom-call(s32[4]{0:T(128)S(1)} %copy-done.12, bf16[512,1152]{1,0:T(8,128)(2,1)S(1)} %collective-permute-done.refs_1_.refs_2_, bf16[256,1152]{1,0:T(8,128)(2,1)S(1)} %collective-permute-done.2.refs_2_.refs_3_, ...), custom_call_target="tpu_custom_call" | custom-call | flops 2415919104 | bytes 9043968 | tf_op jit(solution)/shard_map/project/pallas_call | solution.py:47
  46.0 2.1 %collective-permute-start.7 = (bf16[512,1024]{1,0:T(8,128)(2,1)S(1)}, bf16[512,1024]{1,0:T(8,128)(2,1)S(1)}, u32[]{:S(2)}, u32[]{:S(2)}) collective-permute-start(bf16[512,1024]{1,0:T(8,128)(2,1)S(1)} %get-tuple-element.51.refs_0_), channel_id=1, source_target_pairs={{0,8},{4,20},{8,0},{12,28},{16,24},{20,4},{24,16},{28,12},{1,9},{5... | collective-permute-start | bytes 3145736 | tf_op jit(solution)/shard_map/ppermute | solution.py:808
  48.0 4.9 %project.3 = (bf16[512,1024]{1,0:T(8,128)(2,1)S(1)}, f32[512,1024]{1,0:T(8,128)S(1)}) custom-call(bf16[512,1024]{1,0:T(8,128)(2,1)S(1)} %get-tuple-element.51.refs_0_, s32[4]{0:T(128)S(1)} %copy-done.12, bf16[512,1152]{1,0:T(8,128)(2,1)S(1)} %collective-permute-done.refs_1_.refs_2_, bf16[256,1152]{1,0:T(8,128)(2,1)S(1)} %collective-permute-done.2.refs_2_.refs_3_, ...), custom_call_target="tpu_custom_call" | custom-call | flops 2415919104 | bytes 9043968 | tf_op jit(solution)/shard_map/project/pallas_call | solution.py:47
  53.0 15.6 %collective-permute-done.8.refs_3_ = bf16[1216,512]{1,0:T(8,128)(2,1)S(1)} collective-permute-done((bf16[1216,512]{1,0:T(8,128)(2,1)S(1)}, bf16[1216,512]{1,0:T(8,128)(2,1)S(1)}, u32[]{:S(2)}, u32[]{:S(2)}) %collective-permute-start.8) | collective-permute-done | bytes 1245216 | tf_op jit(solution)/shard_map/ppermute | solution.py:798
  70.1 7.9 %collective-permute-done.10.refs_3_ = bf16[512,512]{1,0:T(8,128)(2,1)S(1)} collective-permute-done((bf16[512,512]{1,0:T(8,128)(2,1)S(1)}, bf16[512,512]{1,0:T(8,128)(2,1)S(1)}, u32[]{:S(2)}, u32[]{:S(2)}) %collective-permute-start.10) | collective-permute-done | bytes 524320 | tf_op jit(solution)/shard_map/ppermute | solution.py:813
  81.5 3.8 %attend.2 = (bf16[256,128]{1,0:T(8,128)(2,1)S(1)}, bf16[256,128]{1,0:T(8,128)(2,1)S(1)}, bf16[256,128]{1,0:T(8,128)(2,1)S(1)}, bf16[256,128]{1,0:T(8,128)(2,1)S(1)}) custom-call(bf16[512,512]{1,0:T(8,128)(2,1)S(1)} %onward.3.refs_0_, s32[4]{0:T(128)S(1)} %copy-done.12, f32[8]{0:T(128)S(1)} %copy-done.13, ...), custom_call_target="tpu_custom_call" | custom-call | flops 402653184 | bytes 262144 | tf_op jit(solution)/shard_map/attend/pallas_call | solution.py:47
  85.3 2.5 %collective-permute-done.13.refs_3_ = bf16[512,512]{1,0:T(8,128)(2,1)S(1)} collective-permute-done((bf16[512,512]{1,0:T(8,128)(2,1)S(1)}, bf16[512,512]{1,0:T(8,128)(2,1)S(1)}, u32[]{:S(2)}, u32[]{:S(2)}) %collective-permute-start.13) | collective-permute-done | bytes 524320 | tf_op jit(solution)/shard_map/ppermute | solution.py:813
  90.0 6.5 %attend.3 = (bf16[512,128]{1,0:T(8,128)(2,1)S(1)}, bf16[512,128]{1,0:T(8,128)(2,1)S(1)}, bf16[512,128]{1,0:T(8,128)(2,1)S(1)}, bf16[512,128]{1,0:T(8,128)(2,1)S(1)}) custom-call(bf16[512,384]{1,0:T(8,128)(2,1)S(1)} %get-tuple-element.61.refs_0_.refs_4_, s32[4]{0:T(128)S(1)} %copy-done.12, f32[8]{0:T(128)S(1)} %copy-done.13, ...), custom_call_target="tpu_custom_call" | custom-call | flops 402653184 | bytes 524288 | tf_op jit(solution)/shard_map/attend/pallas_call | solution.py:47
  96.5 3.5 %collective-permute-done.9.refs_0_.refs_7_ = bf16[1216,512]{1,0:T(8,128)(2,1)S(1)} collective-permute-done((bf16[1216,512]{1,0:T(8,128)(2,1)S(1)}, bf16[1216,512]{1,0:T(8,128)(2,1)S(1)}, u32[]{:S(2)}, u32[]{:S(2)}) %collective-permute-start.9) | collective-permute-done | bytes 1245216 | tf_op jit(solution)/shard_map/ppermute | solution.py:834
  100.7 2.8 %collective-permute-start.16 = (bf16[512,128]{1,0:T(8,128)(2,1)S(1)}, bf16[512,128]{1,0:T(8,128)(2,1)S(1)}, u32[]{:S(2)}, u32[]{:S(2)}) collective-permute-start(bf16[512,128]{1,0:T(8,128)(2,1)S(1)} %get-tuple-element.71), channel_id=1, source_target_pairs={{0,3},{1,2},{2,1},{3,0},{4,7},{5,6},{6,5},{7,4},{8,11},{9,10},{10,... | collective-permute-start | bytes 393224 | tf_op jit(solution)/shard_map/ppermute | solution.py:845
  104.9 2.6 %collective-permute-done.15.refs_1_ = bf16[512,128]{1,0:T(8,128)(2,1)S(1)} collective-permute-done((bf16[512,128]{1,0:T(8,128)(2,1)S(1)}, bf16[512,128]{1,0:T(8,128)(2,1)S(1)}, u32[]{:S(2)}, u32[]{:S(2)}) %collective-permute-start.15) | collective-permute-done | bytes 131104 | tf_op jit(solution)/shard_map/ppermute | solution.py:845
  107.5 3.1 %collective-permute-done.16.refs_2_ = bf16[512,128]{1,0:T(8,128)(2,1)S(1)} collective-permute-done((bf16[512,128]{1,0:T(8,128)(2,1)S(1)}, bf16[512,128]{1,0:T(8,128)(2,1)S(1)}, u32[]{:S(2)}, u32[]{:S(2)}) %collective-permute-start.16) | collective-permute-done | bytes 131104 | tf_op jit(solution)/shard_map/ppermute | solution.py:845
  112.3 4.8 %collective-permute-done.25.refs_4_ = bf16[512,128]{1,0:T(8,128)(2,1)S(1)} collective-permute-done((bf16[512,128]{1,0:T(8,128)(2,1)S(1)}, bf16[512,128]{1,0:T(8,128)(2,1)S(1)}, u32[]{:S(2)}, u32[]{:S(2)}) %collective-permute-start.25) | collective-permute-done | bytes 131104 | tf_op jit(solution)/shard_map/ppermute | solution.py:828
  117.1 2.4 %output.3 = (f32[4,64,1152]{2,1,0:T(8,128)S(1)}, bf16[4,64,1152]{2,1,0:T(8,128)(2,1)S(1)}) custom-call(s32[4]{0:T(128)S(1)} %copy-done.12, bf16[512,128]{1,0:T(8,128)(2,1)S(1)} %get-tuple-element.74.refs_1_, bf16[512,128]{1,0:T(8,128)(2,1)S(1)} %collective-permute-done.23.refs_2_, bf16[512,128]{1,0:T(8,128)(2,1)S(1)} %collective-permute-done.24.refs_3_, ...), custom_call_target="tpu_custom_call" | custom-call | flops 603979776 | bytes 8585216 | tf_op jit(solution)/shard_map/output/pallas_call | solution.py:47
  121.8 3.9 %collective-permute-start.27 = (bf16[4,64,1152]{2,1,0:T(8,128)(2,1)S(1)}, bf16[4,64,1152]{2,1,0:T(8,128)(2,1)S(1)}, u32[]{:S(2)}, u32[]{:S(2)}) collective-permute-start(bf16[4,64,1152]{2,1,0:T(8,128)(2,1)S(1)} %fold.1), channel_id=1, source_target_pairs={{0,2},{1,0},{2,3},{3,1},{4,6},{5,4},{6,7},{7,5},{8,10},{9,8},{10,1... | collective-permute-start | bytes 1769480 | tf_op jit(solution)/shard_map/ppermute | solution.py:843
  127.4 4.2 %collective-permute-done.19.refs_4_ = bf16[512,384]{1,0:T(8,128)(2,1)S(1)} collective-permute-done((bf16[512,384]{1,0:T(8,128)(2,1)S(1)}, bf16[512,384]{1,0:T(8,128)(2,1)S(1)}, u32[]{:S(2)}, u32[]{:S(2)}) %collective-permute-start.19) | collective-permute-done | bytes 393248 | tf_op jit(solution)/shard_map/ppermute | solution.py:828
  131.6 4.0 %output.2 = (f32[4,64,1152]{2,1,0:T(8,128)S(1)}, bf16[4,64,1152]{2,1,0:T(8,128)(2,1)S(1)}) custom-call(s32[4]{0:T(128)S(1)} %copy-done.12, bf16[512,384]{1,0:T(8,128)(2,1)S(1)} %beside.1.refs_1_, bf16[512,384]{1,0:T(8,128)(2,1)S(1)} %collective-permute-done.17.refs_2_, bf16[512,384]{1,0:T(8,128)(2,1)S(1)} %collective-permute-done.18.refs_3_, ...), custom_call_target="tpu_custom_call" | custom-call | flops 1811939328 | bytes 8585216 | tf_op jit(solution)/shard_map/output/pallas_call | solution.py:47
  135.7 2.7 %collective-permute-done.27.refs_2_ = bf16[4,64,1152]{2,1,0:T(8,128)(2,1)S(1)} collective-permute-done((bf16[4,64,1152]{2,1,0:T(8,128)(2,1)S(1)}, bf16[4,64,1152]{2,1,0:T(8,128)(2,1)S(1)}, u32[]{:S(2)}, u32[]{:S(2)}) %collective-permute-start.27) | collective-permute-done | bytes 589856 | tf_op jit(solution)/shard_map/ppermute | solution.py:843
  139.1 3.0 %collective-permute-start.30 = (bf16[64,1152]{1,0:T(8,128)(2,1)S(1)}, bf16[64,1152]{1,0:T(8,128)(2,1)S(1)}, u32[]{:S(2)}, u32[]{:S(2)}) collective-permute-start(bf16[64,1152]{1,0:T(8,128)(2,1)S(1)} %get-tuple-element.80), channel_id=1, source_target_pairs={{0,24},{4,28},{8,16},{12,20},{16,8},{20,12},{24,0},{28,4},{1,25},{... | collective-permute-start | bytes 442376 | tf_op jit(solution)/shard_map/ppermute | solution.py:849
  142.2 3.3 %collective-permute-done.28.refs_1_ = bf16[64,1152]{1,0:T(8,128)(2,1)S(1)} collective-permute-done((bf16[64,1152]{1,0:T(8,128)(2,1)S(1)}, bf16[64,1152]{1,0:T(8,128)(2,1)S(1)}, u32[]{:S(2)}, u32[]{:S(2)}) %collective-permute-start.28) | collective-permute-done | bytes 147488 | tf_op jit(solution)/shard_map/ppermute | solution.py:849
  149.5 2.0 %collective-permute-start.32 = (bf16[64,1152]{1,0:T(8,128)(2,1)S(1)}, bf16[64,1152]{1,0:T(8,128)(2,1)S(1)}, u32[]{:S(2)}, u32[]{:S(2)}) collective-permute-start(bf16[64,1152]{1,0:T(8,128)(2,1)S(1)} %get-tuple-element.83), channel_id=1, source_target_pairs={{0,2},{1,3},{2,0},{3,1},{4,6},{5,7},{6,4},{7,5},{8,10},{9,11},{10,... | collective-permute-start | bytes 442376 | tf_op jit(solution)/shard_map/ppermute | solution.py:851
  151.5 2.8 %collective-permute-start.33 = (bf16[64,1152]{1,0:T(8,128)(2,1)S(1)}, bf16[64,1152]{1,0:T(8,128)(2,1)S(1)}, u32[]{:S(2)}, u32[]{:S(2)}) collective-permute-start(bf16[64,1152]{1,0:T(8,128)(2,1)S(1)} %get-tuple-element.84), channel_id=1, source_target_pairs={{0,3},{1,0},{2,1},{3,2},{4,7},{5,4},{6,5},{7,6},{8,11},{9,8},{10,9... | collective-permute-start | bytes 442376 | tf_op jit(solution)/shard_map/ppermute | solution.py:851
  156.3 4.6 %collective-permute-done.32.refs_4_ = bf16[64,1152]{1,0:T(8,128)(2,1)S(1)} collective-permute-done((bf16[64,1152]{1,0:T(8,128)(2,1)S(1)}, bf16[64,1152]{1,0:T(8,128)(2,1)S(1)}, u32[]{:S(2)}, u32[]{:S(2)}) %collective-permute-start.32) | collective-permute-done | bytes 147488 | tf_op jit(solution)/shard_map/ppermute | solution.py:851
  (103 shorter events, 35.4 us)
Async XLA Ops:
  7.3 15.8 %collective-permute-start.1 = (bf16[576,2560]{1,0:T(8,128)(2,1)}, bf16[576,2560]{1,0:T(8,128)(2,1)}, u32[]{:S(2)}, u32[]{:S(2)}) collective-permute-start(bf16[576,2560]{1,0:T(8,128)(2,1)} %arrange.1.refs_0_), channel_id=1, source_target_pairs={{0,4},{4,0},{8,12},{12,8},{16,20},{20,16},{24,28},{28,24},{1,5},{5... | collective-permute-start | bytes 8847368 | tf_op jit(solution)/shard_map/ppermute | solution.py:789
  7.9 23.3 %collective-permute-start = (bf16[512,1152]{1,0:T(8,128)(2,1)}, bf16[512,1152]{1,0:T(8,128)(2,1)S(1)}, u32[]{:S(2)}, u32[]{:S(2)}) collective-permute-start(bf16[512,1152]{1,0:T(8,128)(2,1)} %get-tuple-element.45), channel_id=1, source_target_pairs={{0,8},{4,20},{8,0},{12,28},{16,24},{20,4},{24,16},{28,12},{1,9},{5... | collective-permute-start | bytes 3538952 | tf_op jit(solution)/shard_map/ppermute | solution.py:782
  10.4 8.4 %collective-permute-start.4 = (bf16[192,576]{1,0:T(8,128)(2,1)}, bf16[192,576]{1,0:T(8,128)(2,1)}, u32[]{:S(2)}, u32[]{:S(2)}) collective-permute-start(bf16[192,576]{1,0:T(8,128)(2,1)} %bitcast.3.refs_2_), channel_id=1, source_target_pairs={{0,1},{1,0},{2,3},{3,2},{4,5},{5,4},{6,7},{7,6},{8,9},{9,8},{10,11... | collective-permute-start | bytes 663560 | tf_op jit(solution)/shard_map/ppermute | solution.py:779
  12.0 27.6 %collective-permute-start.3 = (bf16[256,1152]{1,0:T(8,128)(2,1)}, bf16[256,1152]{1,0:T(8,128)(2,1)S(1)}, u32[]{:S(2)}, u32[]{:S(2)}) collective-permute-start(bf16[256,1152]{1,0:T(8,128)(2,1)} %get-tuple-element.50), channel_id=1, source_target_pairs={{0,16},{4,12},{8,24},{12,4},{16,0},{20,28},{24,8},{28,20},{1,17},{... | collective-permute-start | bytes 1769480 | tf_op jit(solution)/shard_map/ppermute | solution.py:783
  20.5 17.2 %collective-permute-start.5 = (bf16[256,576]{1,0:T(8,128)(2,1)S(1)}, bf16[256,576]{1,0:T(8,128)(2,1)S(1)}, u32[]{:S(2)}, u32[]{:S(2)}) collective-permute-start(bf16[256,576]{1,0:T(8,128)(2,1)S(1)} %pick.1.refs_3_), channel_id=1, source_target_pairs={{0,2},{1,3},{2,0},{3,1},{4,6},{5,7},{6,4},{7,5},{8,10},{9,11},{10,... | collective-permute-start | bytes 884744 | tf_op jit(solution)/shard_map/ppermute | solution.py:793
  31.3 10.0 %collective-permute-start.2 = (bf16[256,1152]{1,0:T(8,128)(2,1)S(1)}, bf16[256,1152]{1,0:T(8,128)(2,1)S(1)}, u32[]{:S(2)}, u32[]{:S(2)}) collective-permute-start(bf16[256,1152]{1,0:T(8,128)(2,1)S(1)} %lower.1), channel_id=1, source_target_pairs={{0,16},{4,12},{8,24},{12,4},{16,0},{20,28},{24,8},{28,20},{1,17},{... | collective-permute-start | bytes 1769480 | tf_op jit(solution)/shard_map/ppermute | solution.py:791
  37.9 30.7 %collective-permute-start.8 = (bf16[1216,512]{1,0:T(8,128)(2,1)S(1)}, bf16[1216,512]{1,0:T(8,128)(2,1)S(1)}, u32[]{:S(2)}, u32[]{:S(2)}) collective-permute-start(bf16[1216,512]{1,0:T(8,128)(2,1)S(1)} %get-tuple-element.54.refs_5_), channel_id=1, source_target_pairs={{0,1},{1,3},{2,0},{3,2},{4,5},{5,7},{6,4},{7,6},{8,9},{9,11},{10,8... | collective-permute-start | bytes 3735560 | tf_op jit(solution)/shard_map/ppermute | solution.py:798
  46.0 22.6 %collective-permute-start.7 = (bf16[512,1024]{1,0:T(8,128)(2,1)S(1)}, bf16[512,1024]{1,0:T(8,128)(2,1)S(1)}, u32[]{:S(2)}, u32[]{:S(2)}) collective-permute-start(bf16[512,1024]{1,0:T(8,128)(2,1)S(1)} %get-tuple-element.51.refs_0_), channel_id=1, source_target_pairs={{0,8},{4,20},{8,0},{12,28},{16,24},{20,4},{24,16},{28,12},{1,9},{5... | collective-permute-start | bytes 3145736 | tf_op jit(solution)/shard_map/ppermute | solution.py:808
  52.9 25.5 %collective-permute-start.11 = (bf16[512,1024]{1,0:T(8,128)(2,1)S(1)}, bf16[512,1024]{1,0:T(8,128)(2,1)S(1)}, u32[]{:S(2)}, u32[]{:S(2)}) collective-permute-start(bf16[512,1024]{1,0:T(8,128)(2,1)S(1)} %get-tuple-element.52.refs_0_), channel_id=1, source_target_pairs={{0,8},{4,20},{8,0},{12,28},{16,24},{20,4},{24,16},{28,12},{1,9},{5... | collective-permute-start | bytes 3145736 | tf_op jit(solution)/shard_map/ppermute | solution.py:808
  68.7 9.2 %collective-permute-start.10 = (bf16[512,512]{1,0:T(8,128)(2,1)S(1)}, bf16[512,512]{1,0:T(8,128)(2,1)S(1)}, u32[]{:S(2)}, u32[]{:S(2)}) collective-permute-start(bf16[512,512]{1,0:T(8,128)(2,1)S(1)} %get-tuple-element.56.refs_0_), channel_id=1, source_target_pairs={{0,16},{4,12},{8,24},{12,4},{16,0},{20,28},{24,8},{28,20},{1,17},{... | collective-permute-start | bytes 1572872 | tf_op jit(solution)/shard_map/ppermute | solution.py:813
  69.2 30.8 %collective-permute-start.9 = (bf16[1216,512]{1,0:T(8,128)(2,1)S(1)}, bf16[1216,512]{1,0:T(8,128)(2,1)S(1)}, u32[]{:S(2)}, u32[]{:S(2)}) collective-permute-start(bf16[1216,512]{1,0:T(8,128)(2,1)S(1)} %get-tuple-element.55.refs_6_), channel_id=1, source_target_pairs={{0,1},{1,3},{2,0},{3,2},{4,5},{5,7},{6,4},{7,6},{8,9},{9,11},{10,8... | collective-permute-start | bytes 3735560 | tf_op jit(solution)/shard_map/ppermute | solution.py:834
  78.5 9.2 %collective-permute-start.13 = (bf16[512,512]{1,0:T(8,128)(2,1)S(1)}, bf16[512,512]{1,0:T(8,128)(2,1)S(1)}, u32[]{:S(2)}, u32[]{:S(2)}) collective-permute-start(bf16[512,512]{1,0:T(8,128)(2,1)S(1)} %onward.3.refs_0_), channel_id=1, source_target_pairs={{0,16},{4,12},{8,24},{12,4},{16,0},{20,28},{24,8},{28,20},{1,17},{... | collective-permute-start | bytes 1572872 | tf_op jit(solution)/shard_map/ppermute | solution.py:813
  79.0 2.5 %collective-permute-start.12 = (bf16[512,384]{1,0:T(8,128)(2,1)S(1)}, bf16[512,384]{1,0:T(8,128)(2,1)S(1)}, u32[]{:S(2)}, u32[]{:S(2)}) collective-permute-start(bf16[512,384]{1,0:T(8,128)(2,1)S(1)} %get-tuple-element.59), channel_id=1, source_target_pairs={{0,4},{4,0},{8,12},{12,8},{16,20},{20,16},{24,28},{28,24},{1,5},{5... | collective-permute-start | bytes 1179656 | tf_op jit(solution)/shard_map/ppermute | solution.py:819
  88.2 1.8 %collective-permute-start.14 = (bf16[512,384]{1,0:T(8,128)(2,1)S(1)}, bf16[512,384]{1,0:T(8,128)(2,1)S(1)}, u32[]{:S(2)}, u32[]{:S(2)}) collective-permute-start(bf16[512,384]{1,0:T(8,128)(2,1)S(1)} %get-tuple-element.62), channel_id=1, source_target_pairs={{0,4},{4,0},{8,12},{12,8},{16,20},{20,16},{24,28},{28,24},{1,5},{5... | collective-permute-start | bytes 1179656 | tf_op jit(solution)/shard_map/ppermute | solution.py:819
  100.0 7.5 %collective-permute-start.15 = (bf16[512,128]{1,0:T(8,128)(2,1)S(1)}, bf16[512,128]{1,0:T(8,128)(2,1)S(1)}, u32[]{:S(2)}, u32[]{:S(2)}) collective-permute-start(bf16[512,128]{1,0:T(8,128)(2,1)S(1)} %get-tuple-element.70), channel_id=1, source_target_pairs={{0,1},{1,3},{2,0},{3,2},{4,5},{5,7},{6,4},{7,6},{8,9},{9,11},{10,8... | collective-permute-start | bytes 393224 | tf_op jit(solution)/shard_map/ppermute | solution.py:845
  100.7 9.9 %collective-permute-start.16 = (bf16[512,128]{1,0:T(8,128)(2,1)S(1)}, bf16[512,128]{1,0:T(8,128)(2,1)S(1)}, u32[]{:S(2)}, u32[]{:S(2)}) collective-permute-start(bf16[512,128]{1,0:T(8,128)(2,1)S(1)} %get-tuple-element.71), channel_id=1, source_target_pairs={{0,3},{1,2},{2,1},{3,0},{4,7},{5,6},{6,5},{7,4},{8,11},{9,10},{10,... | collective-permute-start | bytes 393224 | tf_op jit(solution)/shard_map/ppermute | solution.py:845
  103.5 7.2 %collective-permute-start.23 = (bf16[512,128]{1,0:T(8,128)(2,1)S(1)}, bf16[512,128]{1,0:T(8,128)(2,1)S(1)}, u32[]{:S(2)}, u32[]{:S(2)}) collective-permute-start(bf16[512,128]{1,0:T(8,128)(2,1)S(1)} %get-tuple-element.74.refs_1_), channel_id=1, source_target_pairs={{0,8},{4,20},{8,0},{12,28},{16,24},{20,4},{24,16},{28,12},{1,9},{5... | collective-permute-start | bytes 393224 | tf_op jit(solution)/shard_map/ppermute | solution.py:826
  103.9 6.9 %collective-permute-start.20 = (bf16[64,576]{1,0:T(8,128)(2,1)S(1)}, bf16[64,576]{1,0:T(8,128)(2,1)S(1)}, u32[]{:S(2)}, u32[]{:S(2)}) collective-permute-start(bf16[64,576]{1,0:T(8,128)(2,1)S(1)} %slice.10), channel_id=1, source_target_pairs={{0,1},{1,0},{2,3},{3,2},{4,5},{5,4},{6,7},{7,6},{8,9},{9,8},{10,11... | collective-permute-start | bytes 221192 | tf_op jit(solution)/shard_map/ppermute | solution.py:796
  104.5 7.8 %collective-permute-start.24 = (bf16[512,128]{1,0:T(8,128)(2,1)S(1)}, bf16[512,128]{1,0:T(8,128)(2,1)S(1)}, u32[]{:S(2)}, u32[]{:S(2)}) collective-permute-start(bf16[512,128]{1,0:T(8,128)(2,1)S(1)} %get-tuple-element.74.refs_1_), channel_id=1, source_target_pairs={{0,16},{4,12},{8,24},{12,4},{16,0},{20,28},{24,8},{28,20},{1,17},{... | collective-permute-start | bytes 393224 | tf_op jit(solution)/shard_map/ppermute | solution.py:827
  110.7 9.1 %collective-permute-start.17 = (bf16[512,384]{1,0:T(8,128)(2,1)S(1)}, bf16[512,384]{1,0:T(8,128)(2,1)S(1)}, u32[]{:S(2)}, u32[]{:S(2)}) collective-permute-start(bf16[512,384]{1,0:T(8,128)(2,1)S(1)} %beside.1.refs_1_), channel_id=1, source_target_pairs={{0,8},{4,20},{8,0},{12,28},{16,24},{20,4},{24,16},{28,12},{1,9},{5... | collective-permute-start | bytes 1179656 | tf_op jit(solution)/shard_map/ppermute | solution.py:826
  110.7 6.4 %collective-permute-start.25 = (bf16[512,128]{1,0:T(8,128)(2,1)S(1)}, bf16[512,128]{1,0:T(8,128)(2,1)S(1)}, u32[]{:S(2)}, u32[]{:S(2)}) collective-permute-start(bf16[512,128]{1,0:T(8,128)(2,1)S(1)} %collective-permute-done.23.refs_2_), channel_id=1, source_target_pairs={{0,16},{4,12},{8,24},{12,4},{16,0},{20,28},{24,8},{28,20},{1,17},{... | collective-permute-start | bytes 393224 | tf_op jit(solution)/shard_map/ppermute | solution.py:828
  119.5 2.2 %collective-permute-start.26 = (bf16[4,64,1152]{2,1,0:T(8,128)(2,1)S(1)}, bf16[4,64,1152]{2,1,0:T(8,128)(2,1)S(1)}, u32[]{:S(2)}, u32[]{:S(2)}) collective-permute-start(bf16[4,64,1152]{2,1,0:T(8,128)(2,1)S(1)} %get-tuple-element.76), channel_id=1, source_target_pairs={{0,4},{4,0},{8,12},{12,8},{16,20},{20,16},{24,28},{28,24},{1,5},{5... | collective-permute-start | bytes 1769480 | tf_op jit(solution)/shard_map/ppermute | solution.py:843
  119.6 7.8 %collective-permute-start.18 = (bf16[512,384]{1,0:T(8,128)(2,1)S(1)}, bf16[512,384]{1,0:T(8,128)(2,1)S(1)}, u32[]{:S(2)}, u32[]{:S(2)}) collective-permute-start(bf16[512,384]{1,0:T(8,128)(2,1)S(1)} %beside.1.refs_1_), channel_id=1, source_target_pairs={{0,16},{4,12},{8,24},{12,4},{16,0},{20,28},{24,8},{28,20},{1,17},{... | collective-permute-start | bytes 1179656 | tf_op jit(solution)/shard_map/ppermute | solution.py:827
  119.8 11.9 %collective-permute-start.19 = (bf16[512,384]{1,0:T(8,128)(2,1)S(1)}, bf16[512,384]{1,0:T(8,128)(2,1)S(1)}, u32[]{:S(2)}, u32[]{:S(2)}) collective-permute-start(bf16[512,384]{1,0:T(8,128)(2,1)S(1)} %collective-permute-done.17.refs_2_), channel_id=1, source_target_pairs={{0,16},{4,12},{8,24},{12,4},{16,0},{20,28},{24,8},{28,20},{1,17},{... | collective-permute-start | bytes 1179656 | tf_op jit(solution)/shard_map/ppermute | solution.py:828
  121.8 16.6 %collective-permute-start.27 = (bf16[4,64,1152]{2,1,0:T(8,128)(2,1)S(1)}, bf16[4,64,1152]{2,1,0:T(8,128)(2,1)S(1)}, u32[]{:S(2)}, u32[]{:S(2)}) collective-permute-start(bf16[4,64,1152]{2,1,0:T(8,128)(2,1)S(1)} %fold.1), channel_id=1, source_target_pairs={{0,2},{1,0},{2,3},{3,1},{4,6},{5,4},{6,7},{7,5},{8,10},{9,8},{10,1... | collective-permute-start | bytes 1769480 | tf_op jit(solution)/shard_map/ppermute | solution.py:843
  135.7 2.8 %collective-permute-start.22 = (bf16[4,64,1152]{2,1,0:T(8,128)(2,1)S(1)}, bf16[4,64,1152]{2,1,0:T(8,128)(2,1)S(1)}, u32[]{:S(2)}, u32[]{:S(2)}) collective-permute-start(bf16[4,64,1152]{2,1,0:T(8,128)(2,1)S(1)} %get-tuple-element.73), channel_id=1, source_target_pairs={{0,4},{4,0},{8,12},{12,8},{16,20},{20,16},{24,28},{28,24},{1,5},{5... | collective-permute-start | bytes 1769480 | tf_op jit(solution)/shard_map/ppermute | solution.py:848
  138.6 6.8 %collective-permute-start.28 = (bf16[64,1152]{1,0:T(8,128)(2,1)S(1)}, bf16[64,1152]{1,0:T(8,128)(2,1)S(1)}, u32[]{:S(2)}, u32[]{:S(2)}) collective-permute-start(bf16[64,1152]{1,0:T(8,128)(2,1)S(1)} %get-tuple-element.78), channel_id=1, source_target_pairs={{0,8},{4,12},{8,0},{12,4},{16,24},{20,28},{24,16},{28,20},{1,9},{5... | collective-permute-start | bytes 442376 | tf_op jit(solution)/shard_map/ppermute | solution.py:849
  139.1 8.2 %collective-permute-start.29 = (bf16[64,1152]{1,0:T(8,128)(2,1)S(1)}, bf16[64,1152]{1,0:T(8,128)(2,1)S(1)}, u32[]{:S(2)}, u32[]{:S(2)}) collective-permute-start(bf16[64,1152]{1,0:T(8,128)(2,1)S(1)} %get-tuple-element.79), channel_id=1, source_target_pairs={{0,16},{4,20},{8,24},{12,28},{16,0},{20,4},{24,8},{28,12},{1,17},{... | collective-permute-start | bytes 442376 | tf_op jit(solution)/shard_map/ppermute | solution.py:849
  139.1 8.2 %collective-permute-start.30 = (bf16[64,1152]{1,0:T(8,128)(2,1)S(1)}, bf16[64,1152]{1,0:T(8,128)(2,1)S(1)}, u32[]{:S(2)}, u32[]{:S(2)}) collective-permute-start(bf16[64,1152]{1,0:T(8,128)(2,1)S(1)} %get-tuple-element.80), channel_id=1, source_target_pairs={{0,24},{4,28},{8,16},{12,20},{16,8},{20,12},{24,0},{28,4},{1,25},{... | collective-permute-start | bytes 442376 | tf_op jit(solution)/shard_map/ppermute | solution.py:849
  147.6 8.6 %collective-permute-start.31 = (bf16[64,1152]{1,0:T(8,128)(2,1)S(1)}, bf16[64,1152]{1,0:T(8,128)(2,1)S(1)}, u32[]{:S(2)}, u32[]{:S(2)}) collective-permute-start(bf16[64,1152]{1,0:T(8,128)(2,1)S(1)} %get-tuple-element.82), channel_id=1, source_target_pairs={{0,1},{1,2},{2,3},{3,0},{4,5},{5,6},{6,7},{7,4},{8,9},{9,10},{10,1... | collective-permute-start | bytes 442376 | tf_op jit(solution)/shard_map/ppermute | solution.py:851
  149.5 11.4 %collective-permute-start.32 = (bf16[64,1152]{1,0:T(8,128)(2,1)S(1)}, bf16[64,1152]{1,0:T(8,128)(2,1)S(1)}, u32[]{:S(2)}, u32[]{:S(2)}) collective-permute-start(bf16[64,1152]{1,0:T(8,128)(2,1)S(1)} %get-tuple-element.83), channel_id=1, source_target_pairs={{0,2},{1,3},{2,0},{3,1},{4,6},{5,7},{6,4},{7,5},{8,10},{9,11},{10,... | collective-permute-start | bytes 442376 | tf_op jit(solution)/shard_map/ppermute | solution.py:851
  151.5 9.4 %collective-permute-start.33 = (bf16[64,1152]{1,0:T(8,128)(2,1)S(1)}, bf16[64,1152]{1,0:T(8,128)(2,1)S(1)}, u32[]{:S(2)}, u32[]{:S(2)}) collective-permute-start(bf16[64,1152]{1,0:T(8,128)(2,1)S(1)} %get-tuple-element.84), channel_id=1, source_target_pairs={{0,3},{1,0},{2,1},{3,2},{4,7},{5,4},{6,5},{7,6},{8,11},{9,8},{10,9... | collective-permute-start | bytes 442376 | tf_op jit(solution)/shard_map/ppermute | solution.py:851
  (17 other events, 105.3 us)
